TPU v7x, 32 devices: a whole 2x2x4 slice. The times are simulated.
32 devices in a mesh: dp: 8 (over z, core), fsdp: 4 (over y, x).
Axes of the slice: x: 2, y: 2, z: 4, core: 2. Of those that a mesh axis runs over, the one named last changes fastest.
Arguments:
- inputs: bfloat16 [12288, 2048], P(('dp', 'fsdp')), may hold values from -6 to 6
- cotangent: bfloat16 [12288, 2048], P(('dp', 'fsdp')), may hold values from -6 to 6
- segments: int32 [32, 384], P(('dp', 'fsdp')), may hold values from 0 to 2, as said below
- qkv_weight: float32 [2048, 2560], P(('dp', 'fsdp')), may hold values from -0.125 to 0.125
- out_weight: float32 [2048, 2048], P(('dp', 'fsdp')), may hold values from -0.625 to 0.625
- mlp_weight: float32 [2048, 11264], P(('dp', 'fsdp')), may hold values from -0.125 to 0.125
- down_weight: float32 [5632, 2048], P(('dp', 'fsdp')), may hold values from -0.078125 to 0.078125
- norm_gains: float32 [2, 2048], P(None, ('dp', 'fsdp')), may hold values from 0.25 to 3
- qkv_first: float32 [2048, 2560], P(('dp', 'fsdp')), may hold values from -0.00024414062 to 0.00024414062
- out_first: float32 [2048, 2048], P(('dp', 'fsdp')), may hold values from -0.00024414062 to 0.00024414062
- mlp_first: float32 [2048, 11264], P(('dp', 'fsdp')), may hold values from -0.00024414062 to 0.00024414062
- down_first: float32 [5632, 2048], P(('dp', 'fsdp')), may hold values from -0.00024414062 to 0.00024414062
- gains_first: float32 [2, 2048], P(None, ('dp', 'fsdp')), may hold values from -0.00024414062 to 0.00024414062
- qkv_second: float32 [2048, 2560], P(('dp', 'fsdp')), may hold values from 1.1942525e-09 to 4.7679283e-09
- out_second: float32 [2048, 2048], P(('dp', 'fsdp')), may hold values from 1.1942525e-09 to 4.7679283e-09
- mlp_second: float32 [2048, 11264], P(('dp', 'fsdp')), may hold values from 1.1942525e-09 to 4.7679283e-09
- down_second: float32 [5632, 2048], P(('dp', 'fsdp')), may hold values from 1.1942525e-09 to 4.7679283e-09
- gains_second: float32 [2, 2048], P(None, ('dp', 'fsdp')), may hold values from 1.1942525e-09 to 4.7679283e-09
Outputs:
- layer_out: bfloat16 [12288, 2048], P(('dp', 'fsdp'))
- input_grad: bfloat16 [12288, 2048], P(('dp', 'fsdp'))
- grad_norm: float32 [], replicated
- qkv_new: float32 [2048, 2560], P(('dp', 'fsdp'))
- out_new: float32 [2048, 2048], P(('dp', 'fsdp'))
- mlp_new: float32 [2048, 11264], P(('dp', 'fsdp'))
- down_new: float32 [5632, 2048], P(('dp', 'fsdp'))
- gains_new: float32 [2, 2048], P(None, ('dp', 'fsdp'))
- qkv_first_new: float32 [2048, 2560], P(('dp', 'fsdp'))
- out_first_new: float32 [2048, 2048], P(('dp', 'fsdp'))
- mlp_first_new: float32 [2048, 11264], P(('dp', 'fsdp'))
- down_first_new: float32 [5632, 2048], P(('dp', 'fsdp'))
- gains_first_new: float32 [2, 2048], P(None, ('dp', 'fsdp'))
- qkv_second_new: float32 [2048, 2560], P(('dp', 'fsdp'))
- out_second_new: float32 [2048, 2048], P(('dp', 'fsdp'))
- mlp_second_new: float32 [2048, 11264], P(('dp', 'fsdp'))
- down_second_new: float32 [5632, 2048], P(('dp', 'fsdp'))
- gains_second_new: float32 [2, 2048], P(None, ('dp', 'fsdp'))
Inputs may be any that keep to these rules, and one draw needn't show every extreme that they name: `segments`: along each row of 384 tokens the document numbers never fall; the first token of a row is in document 0 and the last in document 2, so a row holds two or three documents.
All inputs are finite; a program needn't handle non-finite values.
Results may differ from a plain program's by a relative error of at most 0.015.
The roundings to bfloat16 on the way count: a program that leaves them out, or rounds other values in their place, can miss the bound.
Values may be sent and summed in bfloat16 or wider, within the bound.
A program may use at most 384 MiB of HBM per device.

v0:
```python
import jax
import jax.numpy as jnp
from jax import lax
from jax.sharding import PartitionSpec as P

D = 2048
HEADS = 32
KVH = 4
HD = 64
FF = 5632
STEP = 10


norm_eps = 1e-05
rope_base = 10000.0
beta_one = 0.9
beta_two = 0.95
adam_eps = 1e-08
weight_decay = 0.1
matrix_rate = 0.04
gain_rate = 0.8
clip_norm = 1.0


def tables(segment_row):
    length = segment_row.shape[0]
    token_index = jnp.arange(length, dtype=jnp.int32)
    previous = jnp.concatenate([segment_row[:1] - 1, segment_row[:-1]])
    starts = lax.cummax(jnp.where(segment_row != previous, token_index, 0), axis=0)
    position = (token_index - starts).astype(jnp.float32)
    frequency = rope_base ** (-(jnp.arange(HD // 2, dtype=jnp.float32) * 2.0 / HD))
    angles = position[:, None] * frequency[None, :]
    angles = jnp.concatenate([angles, angles], axis=-1)
    allowed = (segment_row[:, None] == segment_row[None, :]) & (
        token_index[:, None] >= token_index[None, :]
    )
    return (jnp.cos(angles)[:, None, :], jnp.sin(angles)[:, None, :], allowed)


def rotate(heads_in, cosine, sine):
    half_width = heads_in.shape[-1] // 2
    turned = jnp.concatenate([-heads_in[..., half_width:], heads_in[..., :half_width]], axis=-1)
    return heads_in * cosine + turned * sine


def unrotate(gradient, cosine, sine):
    half_width = gradient.shape[-1] // 2
    scaled = gradient * sine
    return gradient * cosine + jnp.concatenate(
        [scaled[..., half_width:], -scaled[..., :half_width]], axis=-1
    )


def masked_scores(queries, key_rows, allowed, scale):
    scores = (
        jnp.einsum("tgh,sh->gts", queries, key_rows, preferred_element_type=jnp.float32) * scale
    )
    return jnp.where(allowed[None], scores, -1e30)


def attend_group(group, allowed, scale):
    queries, key_rows, values = group
    scores = masked_scores(queries, key_rows, allowed, scale)
    row_max = jnp.max(scores, axis=-1, keepdims=True)
    exp_scores = jnp.exp(scores - row_max)
    totals = jnp.sum(exp_scores, axis=-1, keepdims=True)
    attn_probs = (exp_scores / totals).astype(jnp.bfloat16)
    context = jnp.einsum("gts,sh->tgh", attn_probs, values, preferred_element_type=jnp.float32)
    return (context, row_max + jnp.log(totals))


def attend_grads(group, allowed, scale):
    queries, key_rows, values, log_totals, grad_context = group
    scores = masked_scores(queries, key_rows, allowed, scale)
    attn_probs = jnp.exp(scores - log_totals)
    grad_probs = jnp.einsum("tgh,sh->gts", grad_context, values, preferred_element_type=jnp.float32)
    grad_values = jnp.einsum(
        "gts,tgh->sh",
        attn_probs.astype(jnp.bfloat16),
        grad_context,
        preferred_element_type=jnp.float32,
    )
    grad_scores = attn_probs * (
        grad_probs - jnp.sum(attn_probs * grad_probs, axis=-1, keepdims=True)
    )
    grad_raw = (grad_scores * scale).astype(jnp.bfloat16)
    grad_queries = jnp.einsum("gts,sh->tgh", grad_raw, key_rows, preferred_element_type=jnp.float32)
    grad_keys = jnp.einsum("gts,tgh->sh", grad_raw, queries, preferred_element_type=jnp.float32)
    return (grad_queries, grad_keys, grad_values)


def adam_update(weight, gradient, first, second, rate, decay):
    first = beta_one * first + (1.0 - beta_one) * gradient
    second = beta_two * second + (1.0 - beta_two) * gradient * gradient
    first_hat = first / (1.0 - beta_one**STEP)
    second_hat = second / (1.0 - beta_two**STEP)
    weight = weight - rate * (first_hat / (jnp.sqrt(second_hat) + adam_eps) + decay * weight)
    return (weight, first, second)


def local(
    inputs,
    cotangent,
    segments,
    qkv_weight,
    out_weight,
    mlp_weight,
    down_weight,
    norm_gains,
    qkv_first,
    out_first,
    mlp_first,
    down_first,
    gains_first,
    qkv_second,
    out_second,
    mlp_second,
    down_second,
    gains_second,
):
    length = inputs.shape[0]
    groups = HEADS // KVH
    key_width = KVH * HD
    scale = HD ** (-0.5)
    cosine, sine, allowed = tables(segments[0])
    qkv_full, out_full, gains_full = (
        lax.all_gather(qkv_weight.astype(jnp.bfloat16), ("dp", "fsdp"), axis=0, tiled=True),
        lax.all_gather(out_weight.astype(jnp.bfloat16), ("dp", "fsdp"), axis=0, tiled=True),
        lax.all_gather(norm_gains.astype(jnp.bfloat16), ("dp", "fsdp"), axis=1, tiled=True),
    )
    mlp_full, down_full = (
        lax.all_gather(mlp_weight.astype(jnp.bfloat16), ("dp", "fsdp"), axis=0, tiled=True),
        lax.all_gather(down_weight.astype(jnp.bfloat16), ("dp", "fsdp"), axis=0, tiled=True),
    )
    tokens_f = inputs.astype(jnp.float32)
    gain_second = gains_full[1].astype(jnp.float32)
    inverse_one = lax.rsqrt(jnp.mean(tokens_f * tokens_f, axis=-1, keepdims=True) + norm_eps)
    normed_one = (tokens_f * inverse_one * gains_full[0].astype(jnp.float32)).astype(jnp.bfloat16)
    projected = jnp.dot(normed_one, qkv_full, preferred_element_type=jnp.float32)
    queries = rotate(projected[:, :D].reshape(length, HEADS, HD), cosine, sine).astype(jnp.bfloat16)
    key_heads = rotate(
        projected[:, D : D + key_width].reshape(length, KVH, HD), cosine, sine
    ).astype(jnp.bfloat16)
    values = projected[:, D + key_width :].reshape(length, KVH, HD).astype(jnp.bfloat16)
    query_groups = queries.reshape(length, KVH, groups, HD).transpose(1, 0, 2, 3)
    key_groups = key_heads.transpose(1, 0, 2)
    value_groups = values.transpose(1, 0, 2)
    contexts, log_totals = lax.map(
        lambda group: attend_group(group, allowed, scale), (query_groups, key_groups, value_groups)
    )
    attended = contexts.transpose(1, 0, 2, 3).reshape(length, D).astype(jnp.bfloat16)
    middle = tokens_f + jnp.dot(attended, out_full, preferred_element_type=jnp.float32)
    inverse_two = lax.rsqrt(jnp.mean(middle * middle, axis=-1, keepdims=True) + norm_eps)
    normed_two = (middle * inverse_two * gain_second).astype(jnp.bfloat16)
    hidden = jnp.dot(normed_two, mlp_full, preferred_element_type=jnp.float32)
    gate = hidden[:, :FF]
    up_part = hidden[:, FF:]
    sigmoid_gate = jax.nn.sigmoid(gate)
    silu_gate = gate * sigmoid_gate
    activated = (silu_gate * up_part).astype(jnp.bfloat16)
    layer_out = (middle + jnp.dot(activated, down_full, preferred_element_type=jnp.float32)).astype(
        jnp.bfloat16
    )
    mlp_back, down_back = (
        lax.all_gather(mlp_weight.astype(jnp.bfloat16), ("dp", "fsdp"), axis=0, tiled=True),
        lax.all_gather(down_weight.astype(jnp.bfloat16), ("dp", "fsdp"), axis=0, tiled=True),
    )
    grad_down = jnp.einsum("tf,td->fd", activated, cotangent, preferred_element_type=jnp.float32)
    grad_act = jnp.einsum("td,fd->tf", cotangent, down_back, preferred_element_type=jnp.float32)
    grad_gate = grad_act * up_part * sigmoid_gate * (1.0 + gate * (1.0 - sigmoid_gate))
    grad_up = grad_act * silu_gate
    grad_hidden = jnp.concatenate([grad_gate, grad_up], axis=1).astype(jnp.bfloat16)
    grad_mlp = jnp.einsum("td,tf->df", normed_two, grad_hidden, preferred_element_type=jnp.float32)
    grad_normed_two = jnp.einsum(
        "tf,df->td", grad_hidden, mlp_back, preferred_element_type=jnp.float32
    )
    mlp_sum, down_sum = (
        lax.psum_scatter(grad_mlp, ("dp", "fsdp"), scatter_dimension=0, tiled=True),
        lax.psum_scatter(grad_down, ("dp", "fsdp"), scatter_dimension=0, tiled=True),
    )
    gain_grad_two = jnp.sum(grad_normed_two * middle * inverse_two, axis=0)
    weighted_two = grad_normed_two * gain_second
    grad_middle = (
        cotangent.astype(jnp.float32)
        + inverse_two * weighted_two
        - middle * inverse_two**3 * jnp.mean(weighted_two * middle, axis=-1, keepdims=True)
    )
    qkv_back, out_back, gains_back = (
        lax.all_gather(qkv_weight.astype(jnp.bfloat16), ("dp", "fsdp"), axis=0, tiled=True),
        lax.all_gather(out_weight.astype(jnp.bfloat16), ("dp", "fsdp"), axis=0, tiled=True),
        lax.all_gather(norm_gains.astype(jnp.bfloat16), ("dp", "fsdp"), axis=1, tiled=True),
    )
    grad_branch = grad_middle.astype(jnp.bfloat16)
    grad_out = jnp.einsum("tc,td->cd", attended, grad_branch, preferred_element_type=jnp.float32)
    grad_context = jnp.einsum(
        "td,cd->tc", grad_branch, out_back, preferred_element_type=jnp.float32
    ).astype(jnp.bfloat16)
    grad_groups = grad_context.reshape(length, KVH, groups, HD).transpose(1, 0, 2, 3)
    grad_query, grad_key, grad_value = lax.map(
        lambda group: attend_grads(group, allowed, scale),
        (query_groups, key_groups, value_groups, log_totals, grad_groups),
    )
    grad_query = unrotate(
        grad_query.transpose(1, 0, 2, 3).reshape(length, HEADS, HD), cosine, sine
    ).reshape(length, D)
    grad_key = unrotate(grad_key.transpose(1, 0, 2), cosine, sine).reshape(length, key_width)
    grad_value = grad_value.transpose(1, 0, 2).reshape(length, key_width)
    grad_projected = jnp.concatenate([grad_query, grad_key, grad_value], axis=1).astype(
        jnp.bfloat16
    )
    grad_qkv = jnp.einsum(
        "td,tq->dq", normed_one, grad_projected, preferred_element_type=jnp.float32
    )
    grad_normed_one = jnp.einsum(
        "tq,dq->td", grad_projected, qkv_back, preferred_element_type=jnp.float32
    )
    gain_grad_one = jnp.sum(grad_normed_one * tokens_f * inverse_one, axis=0)
    weighted_one = grad_normed_one * gains_back[0].astype(jnp.float32)
    grad_inputs = (
        grad_middle
        + inverse_one * weighted_one
        - tokens_f * inverse_one**3 * jnp.mean(weighted_one * tokens_f, axis=-1, keepdims=True)
    )
    input_grad = grad_inputs.astype(jnp.bfloat16)
    gain_grads = jnp.stack([gain_grad_one, gain_grad_two])
    qkv_sum, out_sum, gains_sum = (
        lax.psum_scatter(grad_qkv, ("dp", "fsdp"), scatter_dimension=0, tiled=True),
        lax.psum_scatter(grad_out, ("dp", "fsdp"), scatter_dimension=0, tiled=True),
        lax.psum_scatter(gain_grads, ("dp", "fsdp"), scatter_dimension=1, tiled=True),
    )
    local_squares = (
        jnp.sum(qkv_sum * qkv_sum) + jnp.sum(out_sum * out_sum) + jnp.sum(mlp_sum * mlp_sum)
    )
    local_squares = local_squares + jnp.sum(down_sum * down_sum) + jnp.sum(gains_sum * gains_sum)
    total_squares = lax.psum(local_squares, ("dp", "fsdp"))
    grad_norm = jnp.sqrt(total_squares)
    clip_scale = clip_norm / jnp.maximum(grad_norm, clip_norm)
    qkv_new, qkv_first_new, qkv_second_new = adam_update(
        qkv_weight, qkv_sum * clip_scale, qkv_first, qkv_second, matrix_rate, weight_decay
    )
    out_new, out_first_new, out_second_new = adam_update(
        out_weight, out_sum * clip_scale, out_first, out_second, matrix_rate, weight_decay
    )
    mlp_new, mlp_first_new, mlp_second_new = adam_update(
        mlp_weight, mlp_sum * clip_scale, mlp_first, mlp_second, matrix_rate, weight_decay
    )
    down_new, down_first_new, down_second_new = adam_update(
        down_weight, down_sum * clip_scale, down_first, down_second, matrix_rate, weight_decay
    )
    gains_new, gains_first_new, gains_second_new = adam_update(
        norm_gains, gains_sum * clip_scale, gains_first, gains_second, gain_rate, 0.0
    )
    return (
        layer_out,
        input_grad,
        grad_norm,
        qkv_new,
        out_new,
        mlp_new,
        down_new,
        gains_new,
        qkv_first_new,
        out_first_new,
        mlp_first_new,
        down_first_new,
        gains_first_new,
        qkv_second_new,
        out_second_new,
        mlp_second_new,
        down_second_new,
        gains_second_new,
    )


def solution(mesh):
    placed = (
        P(("dp", "fsdp"), None),
        P(("dp", "fsdp"), None),
        P(("dp", "fsdp"), None),
        P(("dp", "fsdp"), None),
        P(("dp", "fsdp"), None),
        P(("dp", "fsdp"), None),
        P(("dp", "fsdp"), None),
        P(None, ("dp", "fsdp")),
        P(("dp", "fsdp"), None),
        P(("dp", "fsdp"), None),
        P(("dp", "fsdp"), None),
        P(("dp", "fsdp"), None),
        P(None, ("dp", "fsdp")),
        P(("dp", "fsdp"), None),
        P(("dp", "fsdp"), None),
        P(("dp", "fsdp"), None),
        P(("dp", "fsdp"), None),
        P(None, ("dp", "fsdp")),
    )
    return jax.shard_map(
        local,
        mesh=mesh,
        in_specs=placed,
        out_specs=(
            P(("dp", "fsdp"), None),
            P(("dp", "fsdp"), None),
            P(),
            P(("dp", "fsdp"), None),
            P(("dp", "fsdp"), None),
            P(("dp", "fsdp"), None),
            P(("dp", "fsdp"), None),
            P(None, ("dp", "fsdp")),
            P(("dp", "fsdp"), None),
            P(("dp", "fsdp"), None),
            P(("dp", "fsdp"), None),
            P(("dp", "fsdp"), None),
            P(None, ("dp", "fsdp")),
            P(("dp", "fsdp"), None),
            P(("dp", "fsdp"), None),
            P(("dp", "fsdp"), None),
            P(("dp", "fsdp"), None),
            P(None, ("dp", "fsdp")),
        ),
        check_vma=False,
    )
```

profile of v0, /device:TPU:0, one launch (start us, length us, event | category | flops | bytes accessed | tf_op | source)
XLA Modules:
  0.0 4723.9 jit_solution(7297673856560998222)
XLA Ops:
  15.9 69.8 %all-gather = bf16[32,64,2]{1,2,0:T(2,128)(2,1)S(1)} all-gather(bf16[1,64,2]{1,2,0:T(2,128)(2,1)S(1)} %convert_bitcast_fusion), channel_id=1, replica_groups=mesh['dp'=8,'fsdp'=4] {'dp','fsdp'}, dimensions={0}, use_global_device_ids=true | all-gather | bytes 8448 | tf_op jit(solution)/shard_map/all_gather | solution.py:129
  89.8 11.3 all-gather.6.cloned.1.call-done
  101.1 7.0 fusion.101
  118.4 23.7 while.30
  142.1 38.6 all-gather.8.cloned.1.call-done
  180.7 9.4 multiply_reduce_fusion.2
  190.1 248.0 %all-gather.10.cloned.1.call-done = bf16[2048,11264]{1,0:T(8,128)(2,1)} async-done(((bf16[64,11264]{1,0:T(8,128)(2,1)}), bf16[2048,11264]{1,0:T(8,128)(2,1)}) %all-gather.10.cloned.1.call-update) | async-done | bytes 46137360 | tf_op jit(solution)/shard_map/all_gather | solution.py:132
  438.1 29.5 fusion.116
  467.5 116.6 %all-gather.12.cloned.1.call-done = bf16[5632,2048]{1,0:T(8,128)(2,1)} async-done(((bf16[176,2048]{1,0:T(8,128)(2,1)}), bf16[5632,2048]{1,0:T(8,128)(2,1)}) %all-gather.12.cloned.1.call-update) | async-done | bytes 23068688 | tf_op jit(solution)/shard_map/all_gather | solution.py:133
  584.2 23.5 multiply_convert_fusion.1
  607.7 27.6 multiply_reduce_fusion
  635.3 3.7 multiply_subtract_fusion
  640.7 10.1 convolution_convert_fusion
  652.7 133.4 %while.31 = (s32[]{:T(128)}, f32[4,384,8,64]{1,3,2,0:T(8,128)}, f32[4,384,64]{1,2,0:T(8,128)}, bf16[4,384,64]{1,2,0:T(8,128)(2,1)}, bf16[4,384,64]{1,2,0:T(8,128...) while((s32[]{:T(128)}, f32[4,384,8,64]{1,3,2,0:T(8,128)}, ...), condition=%wide.region_11.12_spmd.clone.clone, body=%wide.region_9.11_spmd.clone.sunk.clone | while | flops 786094848 | bytes 55585392 | solution.py:199
  653.2 3.7 fusion.190
  656.9 3.8 fusion.191
  661.5 10.5 fusion.193
  672.0 10.2 fusion.194
  682.2 4.2 fusion.195
  686.3 3.7 fusion.190
  690.1 3.8 fusion.191
  694.7 10.5 fusion.193
  705.1 10.2 fusion.194
  715.3 4.2 fusion.195
  719.5 3.7 fusion.190
  723.2 3.8 fusion.191
  727.9 10.5 fusion.193
  738.3 10.2 fusion.194
  748.5 4.2 fusion.195
  752.7 3.7 fusion.190
  756.4 3.8 fusion.191
  761.1 10.5 fusion.193
  771.6 10.2 fusion.194
  781.8 4.2 fusion.195
  793.6 10.2 fusion.85
  805.4 10.1 fusion.95
  816.9 11.2 fusion.93
  829.5 20.6 fusion.124
  850.1 39.6 fusion.75
  890.3 16.1 add_convert_fusion
  906.4 32.0 reduce-scatter.16.cloned.1.call-done
  939.9 354.6 %reduce-scatter.10.cloned.1.call-done = f32[64,2048]{1,0:T(8,128)} async-done(((f32[2048,2048]{1,0:T(8,128)}), f32[64,2048]{1,0:T(8,128)}) %reduce-scatter.10.cloned.1.call-update) | async-done | bytes 524304 | tf_op jit(solution)/shard_map/reduce_scatter | solution.py:228
  1296.3 447.4 %reduce-scatter.8.cloned.1.call-done = f32[64,2560]{1,0:T(8,128)} async-done(((f32[2048,2560]{1,0:T(8,128)}), f32[64,2560]{1,0:T(8,128)}) %reduce-scatter.8.cloned.1.call-update) | async-done | bytes 655376 | tf_op jit(solution)/shard_map/reduce_scatter | solution.py:227
  1746.8 968.7 %reduce-scatter.14.cloned.1.call-done = f32[176,2048]{1,0:T(8,128)} async-done(((f32[5632,2048]{1,0:T(8,128)}), f32[176,2048]{1,0:T(8,128)}) %reduce-scatter.14.cloned.1.call-update) | async-done | bytes 1441808 | tf_op jit(solution)/shard_map/reduce_scatter | solution.py:179
  2717.8 1928.8 %reduce-scatter.12.cloned.1.call-done = f32[64,11264]{1,0:T(8,128)} async-done(((f32[2048,11264]{1,0:T(8,128)}), f32[64,11264]{1,0:T(8,128)}) %reduce-scatter.12.cloned.1.call-update) | async-done | bytes 2883600 | tf_op jit(solution)/shard_map/reduce_scatter | solution.py:178
  4651.7 5.0 fusion.82
  4656.7 41.8 psum.7
  4705.0 8.0 multiply_subtract_fusion.1
  (202 shorter events, 84.0 us)
Async XLA Ops:
  7.2 93.9 %all-gather.6.cloned.1.call-start = ((), (), s32[]{:S(2)}) async-start(), calls=%async_computation.5 | async-start | bytes 10813440 | tf_op jit(solution)/shard_map/all_gather | solution.py:127
  9.1 171.6 %all-gather.8.cloned.1.call-start = ((), (), s32[]{:S(2)}) async-start(), calls=%async_computation.6 | async-start | bytes 8650752 | tf_op jit(solution)/shard_map/all_gather | solution.py:128
  10.9 3.3 copy-start.14
  11.0 427.1 %all-gather.10.cloned.1.call-start = ((), (), s32[]{:S(2)}) async-start(), calls=%async_computation.7 | async-start | bytes 47579136 | tf_op jit(solution)/shard_map/all_gather | solution.py:132
  14.2 1.7 copy-start.41
  14.2 74.7 %copy-start = (bf16[384,2048]{1,0:T(8,128)(2,1)S(1)}, bf16[384,2048]{1,0:T(8,128)(2,1)}, u32[]{:S(2)}) copy-start(bf16[384,2048]{1,0:T(8,128)(2,1)} %param.22) | copy-start | bytes 4718596
  14.2 570.0 %all-gather.12.cloned.1.call-start = ((), (), s32[]{:S(2)}) async-start(), calls=%async_computation.8 | async-start | bytes 23789568 | tf_op jit(solution)/shard_map/all_gather | solution.py:133
  15.2 923.2 %reduce-scatter.16.cloned.1.call-start = ((), (), s32[]{:S(2)}) async-start(), calls=%async_computation.13 | async-start | bytes 1081344
  87.4 29.7 copy-start.19
  87.4 29.7 copy-start.21
  89.8 11.3 copy-start.36
  89.8 11.3 copy-start.32
  114.8 2.8 copy-start.2
  119.4 1.4 copy-start.4
  125.3 1.4 copy-start.4
  142.1 48.0 %copy-start.23 = (bf16[4,384,64]{1,2,0:T(8,128)(2,1)}, bf16[4,384,64]{1,2,0:T(8,128)(2,1)S(1)}, u32[]{:S(2)}) copy-start(bf16[4,384,64]{1,2,0:T(8,128)(2,1)S(1)} %get-tuple-element.458) | copy-start | bytes 589828
  438.1 146.1 %copy-start.12 = (bf16[384,2048]{1,0:T(8,128)(2,1)S(1)}, bf16[384,2048]{1,0:T(8,128)(2,1)}, u32[]{:S(2)}) copy-start(bf16[384,2048]{1,0:T(8,128)(2,1)} %param.23) | copy-start | bytes 4718596
  639.0 1.7 copy-start.3
  652.7 133.5 %copy-start.22 = (f32[384,64]{0,1:T(8,128)S(1)}, f32[384,64]{0,1:T(8,128)}, u32[]{:S(2)}) copy-start(f32[384,64]{0,1:T(8,128)} %copy-done.21) | copy-start | bytes 294916
  789.7 1.9 copy-start.7
  789.7 1.9 copy-start.20
  791.6 1.8 copy-start.1
  791.6 1.8 copy-start.33
  791.6 2.0 copy-start.35
  791.6 2.0 copy-start.37
  792.0 11.8 copy-start.10
  803.8 1.6 copy-start.6
  805.2 489.3 %reduce-scatter.10.cloned.1.call-start = ((), (), s32[]{:S(2)}) async-start(), calls=%async_computation.10 | async-start | bytes 17301504 | tf_op jit(solution)/shard_map/reduce_scatter | solution.py:228
  815.4 1.4 copy-start.11
  815.5 928.2 %reduce-scatter.8.cloned.1.call-start = ((), (), s32[]{:S(2)}) async-start(), calls=%async_computation.9 | async-start | bytes 21626880 | tf_op jit(solution)/shard_map/reduce_scatter | solution.py:227
  828.1 1887.4 %reduce-scatter.14.cloned.1.call-start = ((), (), s32[]{:S(2)}) async-start(), calls=%async_computation.12 | async-start | bytes 47579136 | tf_op jit(solution)/shard_map/reduce_scatter | solution.py:179
  850.1 3796.5 %reduce-scatter.12.cloned.1.call-start = ((), (), s32[]{:S(2)}) async-start(), calls=%async_computation.11 | async-start | bytes 95158272 | tf_op jit(solution)/shard_map/reduce_scatter | solution.py:178
  906.4 3745.3 %copy-start.34 = (f32[1,2048]{1,0:T(1,128)S(1)}, f32[1,2048]{1,0:T(1,128)}, u32[]{:S(2)}) copy-start(f32[1,2048]{1,0:T(1,128)} %copy-done.32) | copy-start | bytes 24580
  906.4 3745.3 %copy-start.38 = (f32[384]{0:T(512)S(1)}, f32[384]{0:T(512)}, u32[]{:S(2)}) copy-start(f32[384]{0:T(512)} %get-tuple-element.225) | copy-start | bytes 4612
  939.3 3712.4 %copy-start.40 = (f32[2,64]{1,0:T(2,128)}, f32[2,64]{1,0:T(2,128)S(1)}, u32[]{:S(2)}) copy-start(f32[2,64]{1,0:T(2,128)S(1)} %copy.73) | copy-start | bytes 1540
  4651.7 49.0 %copy-start.17 = (f32[64,2560]{1,0:T(8,128)S(1)}, f32[64,2560]{1,0:T(8,128)}, u32[]{:S(2)}) copy-start(f32[64,2560]{1,0:T(8,128)} %reduce-scatter.8.cloned.1.call-done) | copy-start | bytes 1966084
  4651.7 48.9 %copy-start.18 = (f32[64,2560]{1,0:T(8,128)S(1)}, f32[64,2560]{1,0:T(8,128)}, u32[]{:S(2)}) copy-start(f32[64,2560]{1,0:T(8,128)} %param.25) | copy-start | bytes 1966084
  4651.7 48.9 %copy-start.29 = (f32[64,2560]{1,0:T(8,128)S(1)}, f32[64,2560]{1,0:T(8,128)}, u32[]{:S(2)}) copy-start(f32[64,2560]{1,0:T(8,128)} %param.30) | copy-start | bytes 1966084
  4656.7 46.8 copy-start.24
  4656.7 46.8 copy-start.25
  4656.7 46.8 copy-start.30
  4699.3 4.3 copy-start.31
  4700.7 4.3 copy-start.8
  4700.7 4.3 copy-start.9
  4705.0 8.0 copy-start.15
  4705.0 8.0 copy-start.16
  4705.0 8.0 copy-start.27
  4705.0 8.0 copy-start.28
  (9 other events, 11.0 us)
Sparse Core Ops, SparseCore 0:
  11.5 89.5 all-gather.5
  104.5 76.1 all-gather.7
  184.1 253.8 all-gather.9
  441.4 142.7 all-gather.11
  805.3 133.0 reduce-scatter.15
  940.7 353.7 reduce-scatter.9
  1296.9 446.6 reduce-scatter.7
  1746.1 969.3 reduce-scatter.13
  2717.9 1928.5 reduce-scatter.11
where the time goes:
time: 4730 us; the launch traced here: 4720 us
  waiting for transfers between devices  4150 us (88%)
  matrix products  357 us (8%)
  blocking collectives  112 us (2%)
  other arithmetic  61.3 us (1%)
    reduce_scatter x1, waiting for transfers between devices, local(): lax.psum_scatter(grad_mlp, ('dp', 'fsdp'), scatter_dimension=0, tiled=True)  1930 us
    reduce_scatter x1, waiting for transfers between devices, local(): lax.psum_scatter(grad_down, ('dp', 'fsdp'), scatter_dimension=0, tiled=True)  969 us
    reduce_scatter x1, waiting for transfers between devices, local(): lax.psum_scatter(grad_qkv, ('dp', 'fsdp'), scatter_dimension=0, tiled=True)  447 us
    reduce_scatter x1, waiting for transfers between devices, local(): lax.psum_scatter(grad_out, ('dp', 'fsdp'), scatter_dimension=0, tiled=True)  355 us
    all_gather x1, waiting for transfers between devices, local(): lax.all_gather(mlp_weight.astype(jnp.bfloat16), ('dp', 'fsdp'), axis=0, t...  248 us
    all_gather x1, waiting for transfers between devices, local(): lax.all_gather(down_weight.astype(jnp.bfloat16), ('dp', 'fsdp'), axis=0,...  117 us
  transfers between devices with their start and end apart: 9, of which 9 were waited for; matrix products, arithmetic and copies ran while one was open for 4% of the time, Pallas kernels for 0%

commit v1 on v0

v1 whole, which is shorter than its diff:
```python
import functools

import jax
import jax.numpy as jnp
from jax import lax
from jax.experimental import pallas as pl
from jax.experimental.pallas import tpu as pltpu
from jax.sharding import PartitionSpec as P

D = 2048
HEADS = 32
KVH = 4
HD = 64
FF = 5632
STEP = 10
KW = KVH * HD
GROUP = HEADS // KVH


norm_eps = 1e-05
rope_base = 10000.0
beta_one = 0.9
beta_two = 0.95
adam_eps = 1e-08
weight_decay = 0.1
matrix_rate = 0.04
gain_rate = 0.8
clip_norm = 1.0

f32 = jnp.float32
bf16 = jnp.bfloat16


def tables(segment_row):
    length = segment_row.shape[0]
    token_index = jnp.arange(length, dtype=jnp.int32)
    previous = jnp.concatenate([segment_row[:1] - 1, segment_row[:-1]])
    starts = lax.cummax(jnp.where(segment_row != previous, token_index, 0), axis=0)
    position = (token_index - starts).astype(f32)
    frequency = rope_base ** (-(jnp.arange(HD // 2, dtype=f32) * 2.0 / HD))
    angles = position[:, None] * frequency[None, :]
    cosine, sine = jnp.cos(angles), jnp.sin(angles)
    cosine = jnp.concatenate([cosine] * 4, axis=-1)
    signed = jnp.concatenate([-sine, sine] * 2, axis=-1)
    return cosine, signed


def halves_swapped(pair):
    lane = lax.broadcasted_iota(jnp.int32, pair.shape, 1)
    return jnp.where(lane % HD < HD // 2, pltpu.roll(pair, 96, 1), pltpu.roll(pair, 32, 1))


def split_pair(pair):
    lane = lax.broadcasted_iota(jnp.int32, pair.shape, 1)
    zero = jnp.zeros_like(pair)
    return jnp.where(lane < HD, pair, zero), jnp.where(lane < HD, zero, pair)


def both_places(pair, odd):
    low, high = split_pair(pair)
    moved = pltpu.roll(pair.astype(f32), HD, 1).astype(pair.dtype)
    moved_low, moved_high = split_pair(moved)
    return (moved_low, high) if odd else (low, moved_high)


def dot_t(a, b):
    return lax.dot_general(a, b, (((1,), (1,)), ((), ())), preferred_element_type=f32)


def dot_n(a, b):
    return lax.dot_general(a, b, (((1,), (0,)), ((), ())), preferred_element_type=f32)


def dot_tn(a, b):
    return lax.dot_general(a, b, (((0,), (0,)), ((), ())), preferred_element_type=f32)


def mask_keys_rows(seg_col, seg_row, length):
    key_index = lax.broadcasted_iota(jnp.int32, (length, length), 0)
    query_index = lax.broadcasted_iota(jnp.int32, (length, length), 1)
    return (seg_col == seg_row) & (query_index >= key_index)


def attend_kernel(proj, cosine, sine, seg_col, seg_row, qkv, context, log_totals):
    length = proj.shape[0]
    cos, sin = cosine[...], sine[...]
    for c in range(0, D + KW, 128):
        pair = proj[:, c : c + 128]
        qkv[:, c : c + 128] = (pair * cos + halves_swapped(pair) * sin).astype(bf16)
    for c in range(D + KW, D + 2 * KW, 128):
        qkv[:, c : c + 128] = proj[:, c : c + 128].astype(bf16)
    allowed = mask_keys_rows(seg_col[...], seg_row[...], length)
    scale = HD ** (-0.5)
    for group in range(KVH):
        kc = D + (group // 2) * 128
        keys = both_places(qkv[:, kc : kc + 128], group % 2)
        values = both_places(qkv[:, kc + KW : kc + KW + 128], group % 2)

        def pair_step(pair_index, carry):
            pair = group * (GROUP // 2) + pair_index
            lanes = pl.ds(pl.multiple_of(pair * 128, 128), 128)
            queries = qkv[:, lanes]
            total = jnp.zeros((length, 128), f32)
            for side in range(2):
                scores = dot_t(keys[side], queries) * scale
                scores = jnp.where(allowed, scores, -1e30)
                top = jnp.max(scores, axis=0, keepdims=True)
                raised = jnp.exp(scores - top)
                totals = jnp.sum(raised, axis=0, keepdims=True)
                probs = (raised / totals).astype(bf16)
                total = total + dot_tn(probs, values[side])
                log_totals[pl.ds(2 * pair + side, 1), :] = top + jnp.log(totals)
            context[:, lanes] = total.astype(bf16)
            return carry

        lax.fori_loop(0, GROUP // 2, pair_step, 0)


def attend_grad_kernel(qkv, grad_context, log_totals, cosine, sine, seg_col, seg_row, grad_proj):
    length = qkv.shape[0]
    cos, sin = cosine[...], sine[...]
    allowed = mask_keys_rows(seg_col[...], seg_row[...], length)
    scale = HD ** (-0.5)

    def unrotate(pair):
        return pair * cos + halves_swapped(pair * sin)

    key_parts, value_parts = [], []
    for group in range(KVH):
        kc = D + (group // 2) * 128
        keys = both_places(qkv[:, kc : kc + 128], group % 2)
        values = both_places(qkv[:, kc + KW : kc + KW + 128], group % 2)

        def pair_step(pair_index, carry):
            grad_keys, grad_values = list(carry[:2]), list(carry[2:])
            pair = group * (GROUP // 2) + pair_index
            lanes = pl.ds(pl.multiple_of(pair * 128, 128), 128)
            queries = qkv[:, lanes]
            grads = grad_context[:, lanes]
            total = jnp.zeros((length, 128), f32)
            for side in range(2):
                scores = dot_t(keys[side], queries) * scale
                scores = jnp.where(allowed, scores, -1e30)
                probs = jnp.exp(scores - log_totals[pl.ds(2 * pair + side, 1), :])
                grad_probs = dot_t(values[side], grads)
                grad_values[side] = grad_values[side] + dot_n(probs.astype(bf16), grads)
                inner = jnp.sum(probs * grad_probs, axis=0, keepdims=True)
                raw = (probs * (grad_probs - inner) * scale).astype(bf16)
                total = total + dot_tn(raw, keys[side])
                grad_keys[side] = grad_keys[side] + dot_n(raw, queries)
            grad_proj[:, lanes] = unrotate(total).astype(bf16)
            return (*grad_keys, *grad_values)

        empty = jnp.zeros((length, 128), f32)
        out = lax.fori_loop(0, GROUP // 2, pair_step, (empty,) * 4)

        def joined(low_side, high_side):
            low, _ = split_pair(low_side)
            _, high = split_pair(high_side)
            both = low + high
            return both + pltpu.roll(both, HD, 1)

        key_parts.append(joined(out[0], out[1]))
        value_parts.append(joined(out[2], out[3]))
    lane = lax.broadcasted_iota(jnp.int32, (length, 128), 1)
    for c in range(KVH // 2):
        keys = jnp.where(lane < HD, key_parts[2 * c], key_parts[2 * c + 1])
        values = jnp.where(lane < HD, value_parts[2 * c], value_parts[2 * c + 1])
        grad_proj[:, D + c * 128 : D + (c + 1) * 128] = unrotate(keys).astype(bf16)
        grad_proj[:, D + KW + c * 128 : D + KW + (c + 1) * 128] = values.astype(bf16)


vmem_limit = 50 * 1024 * 1024


def attend(projected, cosine, sine, seg_col, seg_row):
    length = projected.shape[0]
    return pl.pallas_call(
        attend_kernel,
        out_shape=(
            jax.ShapeDtypeStruct((length, D + 2 * KW), bf16),
            jax.ShapeDtypeStruct((length, D), bf16),
            jax.ShapeDtypeStruct((HEADS, length), f32),
        ),
        compiler_params=pltpu.CompilerParams(vmem_limit_bytes=vmem_limit),
        name="attend",
    )(projected, cosine, sine, seg_col, seg_row)


def attend_grad(qkv, grad_context, log_totals, cosine, sine, seg_col, seg_row):
    length = qkv.shape[0]
    return pl.pallas_call(
        attend_grad_kernel,
        out_shape=jax.ShapeDtypeStruct((length, D + 2 * KW), bf16),
        compiler_params=pltpu.CompilerParams(vmem_limit_bytes=vmem_limit),
        name="attend_grad",
    )(qkv, grad_context, log_totals, cosine, sine, seg_col, seg_row)


def adam_update(weight, gradient, first, second, rate, decay):
    first = beta_one * first + (1.0 - beta_one) * gradient
    second = beta_two * second + (1.0 - beta_two) * gradient * gradient
    first_hat = first / (1.0 - beta_one**STEP)
    second_hat = second / (1.0 - beta_two**STEP)
    weight = weight - rate * (first_hat / (jnp.sqrt(second_hat) + adam_eps) + decay * weight)
    return (weight, first, second)


def matmul(a, b):
    return jnp.dot(a, b, preferred_element_type=f32)


def matmul_t(a, b):
    return lax.dot_general(a, b, (((1,), (1,)), ((), ())), preferred_element_type=f32)


def matmul_tn(a, b):
    return lax.dot_general(a, b, (((0,), (0,)), ((), ())), preferred_element_type=f32)


def swap_core(block, n_dp):
    return lax.ppermute(block, "dp", [(i, i ^ 1) for i in range(n_dp)])


def plane_swap(block, k, n_tp):
    return lax.ppermute(block, "fsdp", [(i, i ^ k) for i in range(n_tp)])


def core_sum(parts, n_dp):
    core = lax.axis_index("dp") % 2
    mine = lax.dynamic_index_in_dim(parts, core, 1, keepdims=False)
    other = lax.dynamic_index_in_dim(parts, 1 - core, 1, keepdims=False)
    return mine.astype(f32) + swap_core(other, n_dp).astype(f32)


def line_sum(parts, n_dp):
    lines = n_dp // 2
    place = lax.axis_index("dp") // 2
    result = lax.dynamic_index_in_dim(parts, place, 0, keepdims=False)
    for way in (1, -1):
        arrived = None
        for step in range(1, lines):
            target = jnp.clip(place + way * (lines - step), 0, lines - 1)
            load = lax.dynamic_index_in_dim(parts, target, 0, keepdims=False).astype(f32)
            if arrived is not None:
                load = load + arrived.astype(f32)
            senders = range(step) if way == 1 else range(lines - step, lines)
            pairs = [(2 * s + c, 2 * (s + way) + c) for s in senders for c in range(2)]
            arrived = lax.ppermute(load.astype(bf16), "dp", pairs)
        result = result.astype(f32) + arrived.astype(f32)
    return result


def plane_sum(parts, n_tp):
    here = lax.axis_index("fsdp")
    total = lax.dynamic_index_in_dim(parts, here, 0, keepdims=False).astype(f32)
    for k in range(1, n_tp):
        load = lax.dynamic_index_in_dim(parts, here ^ k, 0, keepdims=False).astype(bf16)
        total = total + plane_swap(load, k, n_tp).astype(f32)
    return total


def local(
    n_dp,
    n_tp,
    inputs,
    cotangent,
    segments,
    qkv_weight,
    out_weight,
    mlp_weight,
    down_weight,
    norm_gains,
    qkv_first,
    out_first,
    mlp_first,
    down_first,
    gains_first,
    qkv_second,
    out_second,
    mlp_second,
    down_second,
    gains_second,
):
    length = inputs.shape[0]
    lines = n_dp // 2
    rows = mlp_weight.shape[0]
    down_rows = down_weight.shape[0]
    ff = n_dp * down_rows
    both = ("dp", "fsdp")
    cosine, sine = tables(segments[0])
    seg_row = segments
    seg_col = segments.reshape(length, 1)

    gains_full = lax.all_gather(norm_gains.astype(bf16), both, axis=1, tiled=True).astype(f32)
    qkv_full = lax.all_gather(qkv_weight.astype(bf16), both, axis=0, tiled=True)
    out_full = lax.all_gather(out_weight.astype(bf16), both, axis=0, tiled=True)
    mlp_parts = mlp_weight.astype(bf16).reshape(rows, 2, n_dp, n_tp, down_rows)
    mlp_parts = mlp_parts.transpose(3, 0, 1, 2, 4).reshape(n_tp, rows, 2 * ff)
    mlp_mine = lax.all_to_all(mlp_parts, "fsdp", 0, 0, tiled=True).reshape(n_tp * rows, 2 * ff)
    mlp_cols = lax.all_gather(mlp_mine, "dp", axis=0, tiled=True)
    down_cols = lax.all_gather(down_weight.astype(bf16), "dp", axis=0, tiled=True)
    grads_in = [cotangent] + [plane_swap(cotangent, k, n_tp) for k in range(1, n_tp)]

    tokens_f = inputs.astype(f32)
    gain_one, gain_two = gains_full[0], gains_full[1]
    inverse_one = lax.rsqrt(jnp.mean(tokens_f * tokens_f, axis=-1, keepdims=True) + norm_eps)
    normed_one = (tokens_f * inverse_one * gain_one).astype(bf16)
    projected = matmul(normed_one, qkv_full)
    qkv, attended, log_totals = attend(projected, cosine, sine, seg_col, seg_row)
    middle = tokens_f + matmul(attended, out_full)
    inverse_two = lax.rsqrt(jnp.mean(middle * middle, axis=-1, keepdims=True) + norm_eps)
    normed_two = (middle * inverse_two * gain_two).astype(bf16)

    normed_all = jnp.concatenate(
        [normed_two] + [plane_swap(normed_two, k, n_tp) for k in range(1, n_tp)], axis=0
    )
    grads_all = jnp.concatenate(grads_in, axis=0)
    hidden = matmul(normed_all, mlp_cols)
    gate, up_part = hidden[:, :ff], hidden[:, ff:]
    sigmoid_gate = jax.nn.sigmoid(gate)
    silu_gate = gate * sigmoid_gate
    activated = (silu_gate * up_part).astype(bf16)
    grad_act = matmul_t(grads_all, down_cols)
    grad_gate = grad_act * up_part * sigmoid_gate * (1.0 + gate * (1.0 - sigmoid_gate))
    grad_up = grad_act * silu_gate
    grad_hidden = jnp.concatenate([grad_gate, grad_up], axis=1).astype(bf16)
    grad_normed = matmul_t(grad_hidden, mlp_cols).reshape(n_tp, length, D)
    grad_normed_two = grad_normed[0]
    for k in range(1, n_tp):
        grad_normed_two = grad_normed_two + plane_swap(grad_normed[k].astype(bf16), k, n_tp).astype(f32)
    grad_down = matmul_tn(activated, grads_all).astype(bf16).reshape(lines, 2, down_rows, D)
    grad_mlp = matmul_tn(normed_all, grad_hidden).astype(bf16)
    grad_mlp = grad_mlp.reshape(lines, 2, n_tp * rows, 2 * ff)
    layer_parts = matmul(activated, down_cols).reshape(n_tp, length, D)
    layer_out = middle + layer_parts[0]
    for k in range(1, n_tp):
        layer_out = layer_out + plane_swap(layer_parts[k].astype(bf16), k, n_tp).astype(f32)
    layer_out = layer_out.astype(bf16)

    down_sum = line_sum(core_sum(grad_down, n_dp), n_dp)
    mlp_sum = line_sum(core_sum(grad_mlp, n_dp), n_dp).astype(bf16).reshape(n_tp, rows, 2 * ff)
    mlp_sum = lax.all_to_all(mlp_sum, "fsdp", 0, 0, tiled=True)
    mlp_sum = mlp_sum.reshape(n_tp, rows, 2, n_dp, down_rows).transpose(1, 2, 3, 0, 4)
    mlp_sum = mlp_sum.reshape(rows, 2 * FF).astype(f32)

    gain_grad_two = jnp.sum(grad_normed_two * middle * inverse_two, axis=0)
    weighted_two = grad_normed_two * gain_two
    grad_middle = (
        cotangent.astype(f32)
        + inverse_two * weighted_two
        - middle * inverse_two**3 * jnp.mean(weighted_two * middle, axis=-1, keepdims=True)
    )
    grad_branch = grad_middle.astype(bf16)
    grad_context = matmul_t(grad_branch, out_full).astype(bf16)
    grad_projected = attend_grad(qkv, grad_context, log_totals, cosine, sine, seg_col, seg_row)

    def scatter(grads):
        parts = grads.astype(bf16).reshape(lines, 2, n_tp, rows, -1)
        parts = core_sum(parts, n_dp).transpose(1, 0, 2, 3)
        return line_sum(plane_sum(parts, n_tp), n_dp)

    out_sum = scatter(matmul_tn(attended, grad_branch))
    qkv_sum = scatter(matmul_tn(normed_one, grad_projected))
    grad_normed_one = matmul_t(grad_projected, qkv_full)
    gain_grad_one = jnp.sum(grad_normed_one * tokens_f * inverse_one, axis=0)
    weighted_one = grad_normed_one * gain_one
    grad_inputs = (
        grad_middle
        + inverse_one * weighted_one
        - tokens_f * inverse_one**3 * jnp.mean(weighted_one * tokens_f, axis=-1, keepdims=True)
    )
    input_grad = grad_inputs.astype(bf16)
    gain_grads = jnp.stack([gain_grad_one, gain_grad_two])
    gains_sum = lax.psum_scatter(gain_grads, both, scatter_dimension=1, tiled=True)

    local_squares = (
        jnp.sum(qkv_sum * qkv_sum) + jnp.sum(out_sum * out_sum) + jnp.sum(mlp_sum * mlp_sum)
    )
    local_squares = local_squares + jnp.sum(down_sum * down_sum) + jnp.sum(gains_sum * gains_sum)
    total_squares = lax.psum(local_squares, both)
    grad_norm = jnp.sqrt(total_squares)
    clip_scale = clip_norm / jnp.maximum(grad_norm, clip_norm)
    qkv_out = adam_update(
        qkv_weight, qkv_sum * clip_scale, qkv_first, qkv_second, matrix_rate, weight_decay
    )
    out_out = adam_update(
        out_weight, out_sum * clip_scale, out_first, out_second, matrix_rate, weight_decay
    )
    mlp_out = adam_update(
        mlp_weight, mlp_sum * clip_scale, mlp_first, mlp_second, matrix_rate, weight_decay
    )
    down_out = adam_update(
        down_weight, down_sum * clip_scale, down_first, down_second, matrix_rate, weight_decay
    )
    gains_out = adam_update(
        norm_gains, gains_sum * clip_scale, gains_first, gains_second, gain_rate, 0.0
    )
    news = [[new[i] for new in (qkv_out, out_out, mlp_out, down_out, gains_out)] for i in range(3)]
    return (layer_out, input_grad, grad_norm, *news[0], *news[1], *news[2])


def solution(mesh):
    split_rows = P(("dp", "fsdp"), None)
    split_columns = P(None, ("dp", "fsdp"))
    weights = (split_rows,) * 4 + (split_columns,)
    return jax.shard_map(
        functools.partial(local, mesh.shape["dp"], mesh.shape["fsdp"]),
        mesh=mesh,
        in_specs=(split_rows,) * 3 + weights * 3,
        out_specs=(split_rows, split_rows, P()) + weights * 3,
        check_vma=False,
    )
```

time: 4730 us -> 1100 us (0.23)
  waiting for transfers between devices: 4150 us -> 336 us
  matrix products: 357 us -> 183 us
  blocking collectives: 112 us -> 211 us
  starting transfers between devices: 0.37 us -> 89.3 us
  local copies, waits for them, and re-layouts: 26 us -> 99.6 us
  other arithmetic: 61.3 us -> 109 us
    reduce_scatter x4 -> x0, waiting for transfers between devices: 3700 us -> none  [the longest x1 1930 us: local(): lax.psum_scatter(grad_mlp, ('dp', 'fsdp'), scatter_dimension=0, tiled=True)]
    all_gather x4, waiting for transfers between devices: 415 us -> 90 us  [the longest x1 59 us: local(): mlp_cols = lax.all_gather(mlp_mine, 'dp', axis=0, tiled=True)]
    dot_general x40 -> x12, matrix products: 357 us -> 183 us  [the longest x4 66.3 us: matmul_t(): lax.dot_general(a, b, (((1,), (1,)), ((), ())), preferred_element_type=f32)]
    ppermute x0 -> x46, waiting for transfers between devices: none -> 150 us  [the longest x18 103 us: plane_swap(): return lax.ppermute(block, 'fsdp', [(i, i ^ k) for i in range(n_tp)])]
    ppermute x0 -> x46, starting transfers between devices: none -> 84.8 us  [the longest x24 61 us: line_sum(): arrived = lax.ppermute(load.astype(bf16), 'dp', pairs)]
    all_gather x1, blocking collectives: 69.8 us -> 144 us  [local(): lax.all_gather(norm_gains.astype(bf16), both, axis=1, tiled=True)]
    unnamed x10 -> x6, waiting for transfers between devices: 32.2 us -> 95.9 us
  transfers between devices with their start and end apart: 9 -> 52, of which waited for: 9 -> 14; matrix products, arithmetic and copies ran while one was open for 4% -> 25% of each run, Pallas kernels for 0% -> 4%
where the time goes in v1:
time: 1100 us; the launch traced here: 1090 us
  waiting for transfers between devices  336 us (31%)
  blocking collectives  211 us (19%)
  matrix products  183 us (17%)
  other arithmetic  109 us (10%)
  local copies, waits for them, and re-layouts  99.6 us (9%)
  starting transfers between devices  89.3 us (8%)
  Pallas kernels  43.8 us (4%)
  between operations  20.8 us (2%)
    all_gather x1, blocking collectives, local(): lax.all_gather(norm_gains.astype(bf16), both, axis=1, tiled=True)  144 us
    ppermute x18, waiting for transfers between devices, plane_swap(): return lax.ppermute(block, 'fsdp', [(i, i ^ k) for i in range(n_tp)])  103 us
    unnamed x6, waiting for transfers between devices  95.9 us
    dot_general x4, matrix products, matmul_t(): lax.dot_general(a, b, (((1,), (1,)), ((), ())), preferred_element_type=f32)  66.3 us
    dot_general x4, matrix products, matmul(): return jnp.dot(a, b, preferred_element_type=f32)  61.9 us
    ppermute x24, starting transfers between devices, line_sum(): arrived = lax.ppermute(load.astype(bf16), 'dp', pairs)  61 us
    all_gather x1, waiting for transfers between devices, local(): mlp_cols = lax.all_gather(mlp_mine, 'dp', axis=0, tiled=True)  59 us
    dot_general x4, matrix products, matmul_tn(): lax.dot_general(a, b, (((0,), (0,)), ((), ())), preferred_element_type=f32)  55 us
  transfers between devices with their start and end apart: 52, of which 14 were waited for; matrix products, arithmetic and copies ran while one was open for 25% of the time, Pallas kernels for 4%

profile of v1, /device:TPU:0, one launch (start us, length us, event | category | flops | bytes accessed | tf_op | source)
XLA Modules:
  0.0 1092.4 jit_solution(10013603067450250514)
XLA Ops:
  22.9 26.3 %all_to_all.10 = bf16[4,64,2816]{2,1,0:T(8,128)(2,1)} all-to-all(bf16[4,64,2816]{2,1,0:T(8,128)(2,1)S(1)} %reshape.208), channel_id=1, replica_groups=mesh['dp'=8,'fsdp'=4] {'fsdp'}, dimensions={0} | all-to-all | bytes 2883584 | tf_op jit(solution)/shard_map/all_to_all | solution.py:300
  57.1 144.1 %all-gather = bf16[32,64,2]{1,2,0:T(2,128)(2,1)S(1)} all-gather(bf16[1,64,2]{1,2,0:T(2,128)(2,1)S(1)} %convert_bitcast_fusion), channel_id=1, replica_groups=mesh['dp'=8,'fsdp'=4] {'dp','fsdp'}, dimensions={0}, use_global_device_ids=true | all-gather | bytes 8448 | tf_op jit(solution)/shard_map/all_gather | solution.py:295
  203.8 9.2 fusion.61.proj
  213.0 18.3 %attend.1 = (bf16[384,2560]{1,0:T(8,128)(2,1)}, bf16[384,2048]{1,0:T(8,128)(2,1)S(1)}, f32[32,384]{1,0:T(8,128)S(1)}) custom-call(f32[384,2560]{1,0:T(8,128)} %fusion.61.proj, f32[384,128]{1,0:T(8,128)S(1)} %get-tuple-element.103.cosine, f32[384,128]{1,0:T(8,128)S(1)} %get-tuple-element.104.sine, s32[384,1]{1,0:T(8,128)S(1)} %copy.80.seg_col, ...), custom_call_target="tpu_custom_call" | custom-call | tf_op jit(solution)/shard_map/attend/pallas_call | solution.py:178
  231.4 8.0 multiply_reduce_fusion.2
  255.5 59.0 %all-gather.10.cloned.1.call-done = bf16[2048,2816]{1,0:T(8,128)(2,1)} async-done(((bf16[256,2816]{1,0:T(8,128)(2,1)}), bf16[2048,2816]{1,0:T(8,128)(2,1)}) %all-gather.10.cloned.1.call-update) | async-done | bytes 11534352 | tf_op jit(solution)/shard_map/all_gather | solution.py:301
  314.6 29.9 %fusion.40 = f32[1536,2816]{1,0:T(8,128)} fusion(bf16[2048,2816]{1,0:T(8,128)(2,1)} %all-gather.10.cloned.1.call-done, bf16[384,2048]{1,0:T(8,128)(2,1)} %collective-permute-done.2, bf16[384,2048]{1,0:T(8,128)(2,1)} %collective-permute-done.1, bf16[384,2048]{1,0:T(8,128)(2,1)} %collective-permute-done, bf16[384,2048]{1,0:T(8,128)(2,1)} %multiply_convert_fusion.3), kind=kOutput, calls=%fused_computation.106 | convolution fusion | flops 17741905920 | bytes 35127296 | tf_op jit(solution)/shard_map/dot_general | solution.py:210
  344.4 30.9 %all-gather.12.cloned.1.call-done = bf16[1408,2048]{1,0:T(8,128)(2,1)} async-done(((bf16[176,2048]{1,0:T(8,128)(2,1)}), bf16[1408,2048]{1,0:T(8,128)(2,1)}) %all-gather.12.cloned.1.call-update) | async-done | bytes 5767184 | tf_op jit(solution)/shard_map/all_gather | solution.py:302
  375.4 23.0 %multiply_convert_fusion.1 = (bf16[1536,1408]{1,0:T(8,128)(2,1)}, bf16[1536,1408]{1,0:T(8,128)(2,1)}, bf16[1536,1408]{1,0:T(8,128)(2,1)}) fusion(f32[1536,2816]{1,0:T(8,128)} %fusion.40, bf16[1536,2048]{1,0:T(8,128)(2,1)} %constant_dynamic-update-slice_fusion, bf16[1408,2048]{1,0:T(8,128)(2,1)} %all-gather.12.cloned.1.call-done), kind=kOutput, calls=%fused_computation.6 | convolution fusion | flops 8890810368 | bytes 42336256 | tf_op jit(solution)/shard_map/dot_general | solution.py:214
  398.4 14.4 %convolution_convert_fusion.2 = bf16[1408,2048]{1,0:T(8,128)(2,1)} fusion(bf16[1536,1408]{1,0:T(8,128)(2,1)} %get-tuple-element.52, bf16[1536,2048]{1,0:T(8,128)(2,1)} %constant_dynamic-update-slice_fusion), kind=kOutput, calls=%fused_computation.11 | convolution fusion | flops 8861253632 | bytes 16384000 | tf_op jit(solution)/shard_map/dot_general | solution.py:218
  412.8 25.8 %fusion.86 = (bf16[1536,2048]{1,0:T(8,128)(2,1)}, f32[1536,2048]{1,0:T(8,128)}) fusion(bf16[2048,2816]{1,0:T(8,128)(2,1)} %all-gather.10.cloned.1.call-done, bf16[1536,1408]{1,0:T(8,128)(2,1)} %get-tuple-element.51, bf16[1536,1408]{1,0:T(8,128)(2,1)} %get-tuple-element.50), kind=kOutput, calls=%fused_computation.194 | convolution fusion | flops 17737187328 | bytes 39059456 | tf_op jit(solution)/shard_map/dot_general | solution.py:214
  438.6 4.9 fusion.83
  447.0 14.9 %fusion.87 = (bf16[1536,2048]{1,0:T(8,128)(2,1)S(1)}, f32[1536,2048]{1,0:T(8,128)}) fusion(bf16[1536,1408]{1,0:T(8,128)(2,1)S(1)} %copy-done.45, bf16[1408,2048]{1,0:T(8,128)(2,1)} %all-gather.12.cloned.1.call-done), kind=kOutput, calls=%fused_computation.195 | convolution fusion | flops 8861515776 | bytes 28966912 | tf_op jit(solution)/shard_map/dot_general | solution.py:210
  466.9 24.7 %convolution_convert_fusion = bf16[2048,2816]{1,0:T(8,128)(2,1)} fusion(bf16[1536,1408]{1,0:T(8,128)(2,1)} %get-tuple-element.51, bf16[1536,1408]{1,0:T(8,128)(2,1)} %get-tuple-element.50, bf16[384,2048]{1,0:T(8,128)(2,1)} %collective-permute-done.2, bf16[384,2048]{1,0:T(8,128)(2,1)} %collective-permute-done.1, bf16[384,2048]{1,0:T(8,128)(2,1)} %collective-permute-done, ...), kind=kOutput, calls=%fused_computation.1 | convolution fusion | flops 17764974592 | bytes 26476544 | tf_op jit(solution)/shard_map/dot_general | solution.py:218
  491.6 23.0 %collective-permute-done.10 = bf16[384,2048]{1,0:T(8,128)(2,1)S(1)} collective-permute-done((bf16[384,2048]{1,0:T(8,128)(2,1)}, bf16[384,2048]{1,0:T(8,128)(2,1)S(1)}, u32[]{:S(2)}, u32[]{:S(2)}) %collective-permute-start.10) | collective-permute-done | bytes 1572896 | tf_op jit(solution)/shard_map/ppermute | solution.py:226
  518.8 5.6 dynamic-slice_bitcast_fusion
  529.9 20.0 %collective-permute-done.3 = bf16[384,2048]{1,0:T(8,128)(2,1)} collective-permute-done((bf16[384,2048]{1,0:T(8,128)(2,1)}, bf16[384,2048]{1,0:T(8,128)(2,1)}, u32[]{:S(2)}, u32[]{:S(2)}) %collective-permute-start.3) | collective-permute-done | bytes 1572896 | tf_op jit(solution)/shard_map/ppermute | solution.py:226
  550.0 33.5 %collective-permute-done.5 = bf16[384,2048]{1,0:T(8,128)(2,1)S(1)} collective-permute-done((bf16[384,2048]{1,0:T(8,128)(2,1)S(1)}, bf16[384,2048]{1,0:T(8,128)(2,1)S(1)}, u32[]{:S(2)}, u32[]{:S(2)}) %collective-permute-start.5) | collective-permute-done | bytes 1572896 | tf_op jit(solution)/shard_map/ppermute | solution.py:226
  583.5 5.3 multiply_subtract_fusion
  588.8 7.3 convolution_convert_fusion.3
  596.1 6.7 constant_dynamic-slice_fusion.1
  605.1 6.8 convolution_convert_fusion.4.grad_context
  611.9 25.5 %attend_grad.1 = bf16[384,2560]{1,0:T(8,128)(2,1)} custom-call(bf16[384,2560]{1,0:T(8,128)(2,1)} %get-tuple-element.22.qkv, bf16[384,2048]{1,0:T(8,128)(2,1)S(1)} %convolution_convert_fusion.4.grad_context, f32[32,384]{1,0:T(8,128)S(1)} %get-tuple-element.23.log_totals, f32[384,128]{1,0:T(8,128)S(1)} %get-tuple-element.103.cosine, ...), custom_call_target="tpu_custom_call" | custom-call | tf_op jit(solution)/shard_map/attend_grad/pallas_call | solution.py:192
  647.6 8.6 convolution_convert_fusion.1
  656.1 9.2 constant_dynamic-slice_fusion.3
  665.3 5.3 copy.107
  677.3 10.7 fusion.10
  708.1 9.8 convert_add_fusion
  718.0 4.6 fusion.30
  723.4 6.3 collective-permute-start.33
  729.7 95.8 %reduce-scatter.4.cloned.1.call-done = f32[64,2]{1,0:T(8,128)} async-done(((f32[2048,2]{1,0:T(8,128)}), f32[64,2]{1,0:T(8,128)}) %reduce-scatter.4.cloned.1.call-update) | async-done | bytes 528
  842.0 9.9 convert_add_fusion.1
  860.1 10.5 collective-permute-done.34
  870.6 4.4 collective-permute-start.27
  882.7 4.9 collective-permute-done.13
  888.2 21.7 %collective-permute-done.14 = bf16[4,64,2560]{2,1,0:T(8,128)(2,1)S(1)} collective-permute-done((bf16[4,64,2560]{2,1,0:T(8,128)(2,1)S(1)}, bf16[4,64,2560]{2,1,0:T(8,128)(2,1)S(1)}, u32[]{:S(2)}, u32[]{:S(2)}) %collective-permute-start.14) | collective-permute-done | bytes 1310752 | tf_op jit(solution)/shard_map/ppermute | solution.py:226
  923.4 5.0 collective-permute-start.17
  931.5 22.9 %collective-permute-done.17 = bf16[64,2560]{1,0:T(8,128)(2,1)S(1)} collective-permute-done((bf16[64,2560]{1,0:T(8,128)(2,1)S(1)}, bf16[64,2560]{1,0:T(8,128)(2,1)S(1)}, u32[]{:S(2)}, u32[]{:S(2)}) %collective-permute-start.17) | collective-permute-done | bytes 327712 | tf_op jit(solution)/shard_map/ppermute | solution.py:249
  954.4 5.1 collective-permute-start.28
  964.6 4.3 all-to-all-start.1
  968.9 11.5 %collective-permute-start.18 = (bf16[64,2560]{1,0:T(8,128)(2,1)S(1)}, bf16[64,2560]{1,0:T(8,128)(2,1)S(1)}, u32[]{:S(2)}, u32[]{:S(2)}) collective-permute-start(bf16[64,2560]{1,0:T(8,128)(2,1)S(1)} %get-tuple-element.79), channel_id=1, source_target_pairs={{0,8},{4,12},{8,16},{12,20},{16,24},{20,28},{1,9},{5,13},{9,17},{1... | collective-permute-start | bytes 983048 | tf_op jit(solution)/shard_map/ppermute | solution.py:249
  989.3 5.4 collective-permute-done.21
  1002.3 5.4 fusion.7
  1007.7 40.1 %psum.7 = f32[]{:T(128)} all-reduce(f32[]{:T(128)S(6)} %add.432), channel_id=1, replica_groups=mesh['dp'=8,'fsdp'=4] {'dp','fsdp'}, use_global_device_ids=true, to_apply=%region_14.15 | all-reduce | flops 1 | bytes 8 | tf_op jit(solution)/shard_map/psum | solution.py:381
  1050.1 4.8 mul.462
  1054.9 8.2 copy.90
  1063.1 5.7 mul.464
  1069.4 5.7 multiply_subtract_fusion.2
  (269 shorter events, 178.6 us)
Async XLA Ops:
  7.2 196.6 %all-gather.6.cloned.1.call-start = ((), (), s32[]{:S(2)}) async-start(), calls=%async_computation.3 | async-start | bytes 10813440 | tf_op jit(solution)/shard_map/all_gather | solution.py:296
  9.1 222.3 %all-gather.8.cloned.1.call-start = ((), (), s32[]{:S(2)}) async-start(), calls=%async_computation.4 | async-start | bytes 8650752 | tf_op jit(solution)/shard_map/all_gather | solution.py:297
  11.0 303.6 %all-gather.10.cloned.1.call-start = ((), (), s32[]{:S(2)}) async-start(), calls=%async_computation.5 | async-start | bytes 12976128 | tf_op jit(solution)/shard_map/all_gather | solution.py:301
  49.2 326.2 %all-gather.12.cloned.1.call-start = ((), (), s32[]{:S(2)}) async-start(), calls=%async_computation.6 | async-start | bytes 6488064 | tf_op jit(solution)/shard_map/all_gather | solution.py:302
  51.7 773.8 %reduce-scatter.4.cloned.1.call-start = ((), (), s32[]{:S(2)}) async-start(), calls=%async_computation.7 | async-start | bytes 1081344
  51.8 191.1 %collective-permute-start.6 = (bf16[384,2048]{1,0:T(8,128)(2,1)}, bf16[384,2048]{1,0:T(8,128)(2,1)}, u32[]{:S(2)}, u32[]{:S(2)}) collective-permute-start(bf16[384,2048]{1,0:T(8,128)(2,1)} %param.19), channel_id=1, source_target_pairs={{0,1},{1,0},{2,3},{3,2},{4,5},{5,4},{6,7},{7,6},{8,9},{9,8},{10,11... | collective-permute-start | bytes 4718600 | tf_op jit(solution)/shard_map/ppermute | solution.py:226
  53.3 196.7 %collective-permute-start.7 = (bf16[384,2048]{1,0:T(8,128)(2,1)}, bf16[384,2048]{1,0:T(8,128)(2,1)}, u32[]{:S(2)}, u32[]{:S(2)}) collective-permute-start(bf16[384,2048]{1,0:T(8,128)(2,1)} %param.19), channel_id=1, source_target_pairs={{0,2},{1,3},{2,0},{3,1},{4,6},{5,7},{6,4},{7,5},{8,10},{9,11},{10,... | collective-permute-start | bytes 4718600 | tf_op jit(solution)/shard_map/ppermute | solution.py:226
  53.4 199.4 %collective-permute-start.8 = (bf16[384,2048]{1,0:T(8,128)(2,1)}, bf16[384,2048]{1,0:T(8,128)(2,1)}, u32[]{:S(2)}, u32[]{:S(2)}) collective-permute-start(bf16[384,2048]{1,0:T(8,128)(2,1)} %param.19), channel_id=1, source_target_pairs={{0,3},{1,2},{2,1},{3,0},{4,7},{5,6},{6,5},{7,4},{8,11},{9,10},{10,... | collective-permute-start | bytes 4718600 | tf_op jit(solution)/shard_map/ppermute | solution.py:226
  242.5 72.1 %collective-permute-start = (bf16[384,2048]{1,0:T(8,128)(2,1)}, bf16[384,2048]{1,0:T(8,128)(2,1)}, u32[]{:S(2)}, u32[]{:S(2)}) collective-permute-start(bf16[384,2048]{1,0:T(8,128)(2,1)} %multiply_convert_fusion.3), channel_id=1, source_target_pairs={{0,1},{1,0},{2,3},{3,2},{4,5},{5,4},{6,7},{7,6},{8,9},{9,8},{10,11... | collective-permute-start | bytes 4718600 | tf_op jit(solution)/shard_map/ppermute | solution.py:226
  242.9 71.7 %collective-permute-start.1 = (bf16[384,2048]{1,0:T(8,128)(2,1)}, bf16[384,2048]{1,0:T(8,128)(2,1)}, u32[]{:S(2)}, u32[]{:S(2)}) collective-permute-start(bf16[384,2048]{1,0:T(8,128)(2,1)} %multiply_convert_fusion.3), channel_id=1, source_target_pairs={{0,2},{1,3},{2,0},{3,1},{4,6},{5,7},{6,4},{7,5},{8,10},{9,11},{10,... | collective-permute-start | bytes 4718600 | tf_op jit(solution)/shard_map/ppermute | solution.py:226
  242.9 71.7 %collective-permute-start.2 = (bf16[384,2048]{1,0:T(8,128)(2,1)}, bf16[384,2048]{1,0:T(8,128)(2,1)}, u32[]{:S(2)}, u32[]{:S(2)}) collective-permute-start(bf16[384,2048]{1,0:T(8,128)(2,1)} %multiply_convert_fusion.3), channel_id=1, source_target_pairs={{0,3},{1,2},{2,1},{3,0},{4,7},{5,6},{6,5},{7,4},{8,11},{9,10},{10,... | collective-permute-start | bytes 4718600 | tf_op jit(solution)/shard_map/ppermute | solution.py:226
  443.5 71.1 %collective-permute-start.10 = (bf16[384,2048]{1,0:T(8,128)(2,1)}, bf16[384,2048]{1,0:T(8,128)(2,1)S(1)}, u32[]{:S(2)}, u32[]{:S(2)}) collective-permute-start(bf16[384,2048]{1,0:T(8,128)(2,1)} %get-tuple-element.69), channel_id=1, source_target_pairs={{0,2},{1,3},{2,0},{3,1},{4,6},{5,7},{6,4},{7,5},{8,10},{9,11},{10,... | collective-permute-start | bytes 4718600 | tf_op jit(solution)/shard_map/ppermute | solution.py:226
  445.0 79.5 %collective-permute-start.11 = (bf16[384,2048]{1,0:T(8,128)(2,1)}, bf16[384,2048]{1,0:T(8,128)(2,1)S(1)}, u32[]{:S(2)}, u32[]{:S(2)}) collective-permute-start(bf16[384,2048]{1,0:T(8,128)(2,1)} %get-tuple-element.68), channel_id=1, source_target_pairs={{0,3},{1,2},{2,1},{3,0},{4,7},{5,6},{6,5},{7,4},{8,11},{9,10},{10,... | collective-permute-start | bytes 4718600 | tf_op jit(solution)/shard_map/ppermute | solution.py:226
  446.4 78.0 %collective-permute-start.9 = (bf16[384,2048]{1,0:T(8,128)(2,1)}, bf16[384,2048]{1,0:T(8,128)(2,1)S(1)}, u32[]{:S(2)}, u32[]{:S(2)}) collective-permute-start(bf16[384,2048]{1,0:T(8,128)(2,1)} %get-tuple-element.67), channel_id=1, source_target_pairs={{0,1},{1,0},{2,3},{3,2},{4,5},{5,4},{6,7},{7,6},{8,9},{9,8},{10,11... | collective-permute-start | bytes 4718600 | tf_op jit(solution)/shard_map/ppermute | solution.py:226
  464.0 86.0 %collective-permute-start.3 = (bf16[384,2048]{1,0:T(8,128)(2,1)}, bf16[384,2048]{1,0:T(8,128)(2,1)}, u32[]{:S(2)}, u32[]{:S(2)}) collective-permute-start(bf16[384,2048]{1,0:T(8,128)(2,1)} %get-tuple-element.70), channel_id=1, source_target_pairs={{0,1},{1,0},{2,3},{3,2},{4,5},{5,4},{6,7},{7,6},{8,9},{9,8},{10,11... | collective-permute-start | bytes 4718600 | tf_op jit(solution)/shard_map/ppermute | solution.py:226
  465.4 84.5 %collective-permute-start.4 = (bf16[384,2048]{1,0:T(8,128)(2,1)}, bf16[384,2048]{1,0:T(8,128)(2,1)}, u32[]{:S(2)}, u32[]{:S(2)}) collective-permute-start(bf16[384,2048]{1,0:T(8,128)(2,1)} %get-tuple-element.72), channel_id=1, source_target_pairs={{0,2},{1,3},{2,0},{3,1},{4,6},{5,7},{6,4},{7,5},{8,10},{9,11},{10,... | collective-permute-start | bytes 4718600 | tf_op jit(solution)/shard_map/ppermute | solution.py:226
  514.6 68.9 %collective-permute-start.5 = (bf16[384,2048]{1,0:T(8,128)(2,1)S(1)}, bf16[384,2048]{1,0:T(8,128)(2,1)S(1)}, u32[]{:S(2)}, u32[]{:S(2)}) collective-permute-start(bf16[384,2048]{1,0:T(8,128)(2,1)S(1)} %get-tuple-element.71), channel_id=1, source_target_pairs={{0,3},{1,2},{2,1},{3,0},{4,7},{5,6},{6,5},{7,4},{8,11},{9,10},{10,... | collective-permute-start | bytes 4718600 | tf_op jit(solution)/shard_map/ppermute | solution.py:226
  524.5 112.9 %collective-permute-start.39 = (bf16[4,176,2048]{2,1,0:T(8,128)(2,1)}, bf16[4,176,2048]{2,1,0:T(8,128)(2,1)}, u32[]{:S(2)}, u32[]{:S(2)}) collective-permute-start(bf16[4,176,2048]{2,1,0:T(8,128)(2,1)} %dynamic-slice_bitcast_fusion.1), channel_id=1, source_target_pairs={{0,4},{4,0},{8,12},{12,8},{16,20},{20,16},{24,28},{28,24},{1,5},{5... | collective-permute-start | bytes 8650760 | tf_op jit(solution)/shard_map/ppermute | solution.py:222
  524.5 182.2 %collective-permute-start.32 = (bf16[4,256,2816]{2,1,0:T(8,128)(2,1)}, bf16[4,256,2816]{2,1,0:T(8,128)(2,1)}, u32[]{:S(2)}, u32[]{:S(2)}) collective-permute-start(bf16[4,256,2816]{2,1,0:T(8,128)(2,1)} %dynamic-slice_bitcast_fusion), channel_id=1, source_target_pairs={{0,4},{4,0},{8,12},{12,8},{16,20},{20,16},{24,28},{28,24},{1,5},{5... | collective-permute-start | bytes 17301512 | tf_op jit(solution)/shard_map/ppermute | solution.py:222
  605.0 91.9 %collective-permute-start.22 = (bf16[4,4,64,2048]{3,2,0,1:T(8,128)(2,1)}, bf16[4,4,64,2048]{3,2,0,1:T(8,128)(2,1)}, u32[]{:S(2)}, u32[]{:S(2)}) collective-permute-start(bf16[4,4,64,2048]{3,2,0,1:T(8,128)(2,1)} %bitcast.208), channel_id=1, source_target_pairs={{0,4},{4,0},{8,12},{12,8},{16,20},{20,16},{24,28},{28,24},{1,5},{5... | collective-permute-start | bytes 12582920 | tf_op jit(solution)/shard_map/ppermute | solution.py:222
  645.2 27.3 %collective-permute-start.40 = (bf16[176,2048]{1,0:T(8,128)(2,1)}, bf16[176,2048]{1,0:T(8,128)(2,1)}, u32[]{:S(2)}, u32[]{:S(2)}) collective-permute-start(bf16[176,2048]{1,0:T(8,128)(2,1)} %get-tuple-element.75), channel_id=1, source_target_pairs={{0,8},{4,12},{1,9},{5,13},{2,10},{6,14},{3,11},{7,15}} | collective-permute-start | bytes 2162696 | tf_op jit(solution)/shard_map/ppermute | solution.py:249
  670.6 171.4 %collective-permute-start.12 = (bf16[4,4,64,2560]{3,2,0,1:T(8,128)(2,1)}, bf16[4,4,64,2560]{3,2,0,1:T(8,128)(2,1)}, u32[]{:S(2)}, u32[]{:S(2)}) collective-permute-start(bf16[4,4,64,2560]{3,2,0,1:T(8,128)(2,1)} %bitcast.207), channel_id=1, source_target_pairs={{0,4},{4,0},{8,12},{12,8},{16,20},{20,16},{24,28},{28,24},{1,5},{5... | collective-permute-start | bytes 15728648 | tf_op jit(solution)/shard_map/ppermute | solution.py:222
  671.0 18.5 %collective-permute-start.43 = (bf16[176,2048]{1,0:T(8,128)(2,1)}, bf16[176,2048]{1,0:T(8,128)(2,1)}, u32[]{:S(2)}, u32[]{:S(2)}) collective-permute-start(bf16[176,2048]{1,0:T(8,128)(2,1)} %get-tuple-element.76), channel_id=1, source_target_pairs={{24,16},{28,20},{25,17},{29,21},{26,18},{30,22},{27,19},{31,23}} | collective-permute-start | bytes 2162696 | tf_op jit(solution)/shard_map/ppermute | solution.py:249
  675.2 17.6 %collective-permute-start.41 = (bf16[176,2048]{1,0:T(8,128)(2,1)}, bf16[176,2048]{1,0:T(8,128)(2,1)}, u32[]{:S(2)}, u32[]{:S(2)}) collective-permute-start(bf16[176,2048]{1,0:T(8,128)(2,1)} %fusion.34), channel_id=1, source_target_pairs={{0,8},{4,12},{8,16},{12,20},{1,9},{5,13},{9,17},{13,21},{2,10},{6,... | collective-permute-start | bytes 2162696 | tf_op jit(solution)/shard_map/ppermute | solution.py:249
  696.2 26.3 %collective-permute-start.44 = (bf16[176,2048]{1,0:T(8,128)(2,1)S(1)}, bf16[176,2048]{1,0:T(8,128)(2,1)S(1)}, u32[]{:S(2)}, u32[]{:S(2)}) collective-permute-start(bf16[176,2048]{1,0:T(8,128)(2,1)S(1)} %get-tuple-element.74), channel_id=1, source_target_pairs={{16,8},{20,12},{24,16},{28,20},{17,9},{21,13},{25,17},{29,21},{18,... | collective-permute-start | bytes 2162696 | tf_op jit(solution)/shard_map/ppermute | solution.py:249
  704.6 125.0 %collective-permute-start.23 = (bf16[4,64,2048]{2,1,0:T(8,128)(2,1)S(1)}, bf16[4,64,2048]{2,1,0:T(8,128)(2,1)}, u32[]{:S(2)}, u32[]{:S(2)}) collective-permute-start(bf16[4,64,2048]{2,1,0:T(8,128)(2,1)S(1)} %get-tuple-element.62), channel_id=1, source_target_pairs={{0,1},{1,0},{2,3},{3,2},{4,5},{5,4},{6,7},{7,6},{8,9},{9,8},{10,11... | collective-permute-start | bytes 3145736 | tf_op jit(solution)/shard_map/ppermute | solution.py:226
  706.1 125.3 %collective-permute-start.24 = (bf16[4,64,2048]{2,1,0:T(8,128)(2,1)S(1)}, bf16[4,64,2048]{2,1,0:T(8,128)(2,1)}, u32[]{:S(2)}, u32[]{:S(2)}) collective-permute-start(bf16[4,64,2048]{2,1,0:T(8,128)(2,1)S(1)} %get-tuple-element.64), channel_id=1, source_target_pairs={{0,2},{1,3},{2,0},{3,1},{4,6},{5,7},{6,4},{7,5},{8,10},{9,11},{10,... | collective-permute-start | bytes 3145736 | tf_op jit(solution)/shard_map/ppermute | solution.py:226
  706.7 124.8 %collective-permute-start.25 = (bf16[4,64,2048]{2,1,0:T(8,128)(2,1)S(1)}, bf16[4,64,2048]{2,1,0:T(8,128)(2,1)}, u32[]{:S(2)}, u32[]{:S(2)}) collective-permute-start(bf16[4,64,2048]{2,1,0:T(8,128)(2,1)S(1)} %get-tuple-element.63), channel_id=1, source_target_pairs={{0,3},{1,2},{2,1},{3,0},{4,7},{5,6},{6,5},{7,4},{8,11},{9,10},{10,... | collective-permute-start | bytes 3145736 | tf_op jit(solution)/shard_map/ppermute | solution.py:226
  723.4 112.6 %collective-permute-start.33 = (bf16[256,2816]{1,0:T(8,128)(2,1)}, bf16[256,2816]{1,0:T(8,128)(2,1)}, u32[]{:S(2)}, u32[]{:S(2)}) collective-permute-start(bf16[256,2816]{1,0:T(8,128)(2,1)} %get-tuple-element.55), channel_id=1, source_target_pairs={{0,8},{4,12},{1,9},{5,13},{2,10},{6,14},{3,11},{7,15}} | collective-permute-start | bytes 4325384 | tf_op jit(solution)/shard_map/ppermute | solution.py:249
  829.6 29.8 %collective-permute-start.36 = (bf16[256,2816]{1,0:T(8,128)(2,1)}, bf16[256,2816]{1,0:T(8,128)(2,1)}, u32[]{:S(2)}, u32[]{:S(2)}) collective-permute-start(bf16[256,2816]{1,0:T(8,128)(2,1)} %get-tuple-element.56), channel_id=1, source_target_pairs={{24,16},{28,20},{25,17},{29,21},{26,18},{30,22},{27,19},{31,23}} | collective-permute-start | bytes 4325384 | tf_op jit(solution)/shard_map/ppermute | solution.py:249
  834.7 21.3 %collective-permute-start.26 = (bf16[64,2048]{1,0:T(8,128)(2,1)S(1)}, bf16[64,2048]{1,0:T(8,128)(2,1)S(1)}, u32[]{:S(2)}, u32[]{:S(2)}) collective-permute-start(bf16[64,2048]{1,0:T(8,128)(2,1)S(1)} %get-tuple-element.85), channel_id=1, source_target_pairs={{0,8},{4,12},{1,9},{5,13},{2,10},{6,14},{3,11},{7,15}} | collective-permute-start | bytes 786440 | tf_op jit(solution)/shard_map/ppermute | solution.py:249
  839.6 30.9 %collective-permute-start.34 = (bf16[256,2816]{1,0:T(8,128)(2,1)}, bf16[256,2816]{1,0:T(8,128)(2,1)}, u32[]{:S(2)}, u32[]{:S(2)}) collective-permute-start(bf16[256,2816]{1,0:T(8,128)(2,1)} %fusion.21), channel_id=1, source_target_pairs={{0,8},{4,12},{8,16},{12,20},{1,9},{5,13},{9,17},{13,21},{2,10},{6,... | collective-permute-start | bytes 4325384 | tf_op jit(solution)/shard_map/ppermute | solution.py:249
  855.8 31.8 %collective-permute-start.13 = (bf16[4,64,2560]{2,1,0:T(8,128)(2,1)S(1)}, bf16[4,64,2560]{2,1,0:T(8,128)(2,1)S(1)}, u32[]{:S(2)}, u32[]{:S(2)}) collective-permute-start(bf16[4,64,2560]{2,1,0:T(8,128)(2,1)S(1)} %get-tuple-element.57), channel_id=1, source_target_pairs={{0,1},{1,0},{2,3},{3,2},{4,5},{5,4},{6,7},{7,6},{8,9},{9,8},{10,11... | collective-permute-start | bytes 3932168 | tf_op jit(solution)/shard_map/ppermute | solution.py:226
  855.9 54.1 %collective-permute-start.14 = (bf16[4,64,2560]{2,1,0:T(8,128)(2,1)S(1)}, bf16[4,64,2560]{2,1,0:T(8,128)(2,1)S(1)}, u32[]{:S(2)}, u32[]{:S(2)}) collective-permute-start(bf16[4,64,2560]{2,1,0:T(8,128)(2,1)S(1)} %get-tuple-element.59), channel_id=1, source_target_pairs={{0,2},{1,3},{2,0},{3,1},{4,6},{5,7},{6,4},{7,5},{8,10},{9,11},{10,... | collective-permute-start | bytes 3932168 | tf_op jit(solution)/shard_map/ppermute | solution.py:226
  856.0 54.0 %collective-permute-start.15 = (bf16[4,64,2560]{2,1,0:T(8,128)(2,1)S(1)}, bf16[4,64,2560]{2,1,0:T(8,128)(2,1)S(1)}, u32[]{:S(2)}, u32[]{:S(2)}) collective-permute-start(bf16[4,64,2560]{2,1,0:T(8,128)(2,1)S(1)} %get-tuple-element.58), channel_id=1, source_target_pairs={{0,3},{1,2},{2,1},{3,0},{4,7},{5,6},{6,5},{7,4},{8,11},{9,10},{10,... | collective-permute-start | bytes 3932168 | tf_op jit(solution)/shard_map/ppermute | solution.py:226
  859.4 18.0 %collective-permute-start.29 = (bf16[64,2048]{1,0:T(8,128)(2,1)S(1)}, bf16[64,2048]{1,0:T(8,128)(2,1)S(1)}, u32[]{:S(2)}, u32[]{:S(2)}) collective-permute-start(bf16[64,2048]{1,0:T(8,128)(2,1)S(1)} %get-tuple-element.86), channel_id=1, source_target_pairs={{24,16},{28,20},{25,17},{29,21},{26,18},{30,22},{27,19},{31,23}} | collective-permute-start | bytes 786440 | tf_op jit(solution)/shard_map/ppermute | solution.py:249
  877.4 104.0 %collective-permute-start.42 = (bf16[176,2048]{1,0:T(8,128)(2,1)}, bf16[176,2048]{1,0:T(8,128)(2,1)}, u32[]{:S(2)}, u32[]{:S(2)}) collective-permute-start(bf16[176,2048]{1,0:T(8,128)(2,1)} %get-tuple-element.73), channel_id=1, source_target_pairs={{0,8},{4,12},{8,16},{12,20},{16,24},{20,28},{1,9},{5,13},{9,17},{1... | collective-permute-start | bytes 2162696 | tf_op jit(solution)/shard_map/ppermute | solution.py:249
  881.1 33.5 %collective-permute-start.37 = (bf16[256,2816]{1,0:T(8,128)(2,1)S(1)}, bf16[256,2816]{1,0:T(8,128)(2,1)S(1)}, u32[]{:S(2)}, u32[]{:S(2)}) collective-permute-start(bf16[256,2816]{1,0:T(8,128)(2,1)S(1)} %get-tuple-element.54), channel_id=1, source_target_pairs={{16,8},{20,12},{24,16},{28,20},{17,9},{21,13},{25,17},{29,21},{18,... | collective-permute-start | bytes 4325384 | tf_op jit(solution)/shard_map/ppermute | solution.py:249
  887.6 35.8 %collective-permute-start.30 = (bf16[64,2048]{1,0:T(8,128)(2,1)S(1)}, bf16[64,2048]{1,0:T(8,128)(2,1)S(1)}, u32[]{:S(2)}, u32[]{:S(2)}) collective-permute-start(bf16[64,2048]{1,0:T(8,128)(2,1)S(1)} %get-tuple-element.84), channel_id=1, source_target_pairs={{16,8},{20,12},{24,16},{28,20},{17,9},{21,13},{25,17},{29,21},{18,... | collective-permute-start | bytes 786440 | tf_op jit(solution)/shard_map/ppermute | solution.py:249
  913.9 16.3 %collective-permute-start.19 = (bf16[64,2560]{1,0:T(8,128)(2,1)S(1)}, bf16[64,2560]{1,0:T(8,128)(2,1)S(1)}, u32[]{:S(2)}, u32[]{:S(2)}) collective-permute-start(bf16[64,2560]{1,0:T(8,128)(2,1)S(1)} %get-tuple-element.82), channel_id=1, source_target_pairs={{24,16},{28,20},{25,17},{29,21},{26,18},{30,22},{27,19},{31,23}} | collective-permute-start | bytes 983048 | tf_op jit(solution)/shard_map/ppermute | solution.py:249
  914.6 45.7 %collective-permute-start.35 = (bf16[256,2816]{1,0:T(8,128)(2,1)S(1)}, bf16[256,2816]{1,0:T(8,128)(2,1)S(1)}, u32[]{:S(2)}, u32[]{:S(2)}) collective-permute-start(bf16[256,2816]{1,0:T(8,128)(2,1)S(1)} %get-tuple-element.53), channel_id=1, source_target_pairs={{0,8},{4,12},{8,16},{12,20},{16,24},{20,28},{1,9},{5,13},{9,17},{1... | collective-permute-start | bytes 4325384 | tf_op jit(solution)/shard_map/ppermute | solution.py:249
  922.0 39.6 %collective-permute-start.38 = (bf16[256,2816]{1,0:T(8,128)(2,1)S(1)}, bf16[256,2816]{1,0:T(8,128)(2,1)S(1)}, u32[]{:S(2)}, u32[]{:S(2)}) collective-permute-start(bf16[256,2816]{1,0:T(8,128)(2,1)S(1)} %fusion.20), channel_id=1, source_target_pairs={{8,0},{12,4},{16,8},{20,12},{24,16},{28,20},{9,1},{13,5},{17,9},{2... | collective-permute-start | bytes 4325384 | tf_op jit(solution)/shard_map/ppermute | solution.py:249
  923.4 31.0 %collective-permute-start.17 = (bf16[64,2560]{1,0:T(8,128)(2,1)S(1)}, bf16[64,2560]{1,0:T(8,128)(2,1)S(1)}, u32[]{:S(2)}, u32[]{:S(2)}) collective-permute-start(bf16[64,2560]{1,0:T(8,128)(2,1)S(1)} %fusion.51), channel_id=1, source_target_pairs={{0,8},{4,12},{8,16},{12,20},{1,9},{5,13},{9,17},{13,21},{2,10},{6,... | collective-permute-start | bytes 983048 | tf_op jit(solution)/shard_map/ppermute | solution.py:249
  930.2 52.5 %collective-permute-start.45 = (bf16[176,2048]{1,0:T(8,128)(2,1)}, bf16[176,2048]{1,0:T(8,128)(2,1)}, u32[]{:S(2)}, u32[]{:S(2)}) collective-permute-start(bf16[176,2048]{1,0:T(8,128)(2,1)} %fusion.33), channel_id=1, source_target_pairs={{8,0},{12,4},{16,8},{20,12},{24,16},{28,20},{9,1},{13,5},{17,9},{2... | collective-permute-start | bytes 2162696 | tf_op jit(solution)/shard_map/ppermute | solution.py:249
  954.4 32.2 %collective-permute-start.28 = (bf16[64,2048]{1,0:T(8,128)(2,1)}, bf16[64,2048]{1,0:T(8,128)(2,1)}, u32[]{:S(2)}, u32[]{:S(2)}) collective-permute-start(bf16[64,2048]{1,0:T(8,128)(2,1)} %get-tuple-element.83), channel_id=1, source_target_pairs={{0,8},{4,12},{8,16},{12,20},{16,24},{20,28},{1,9},{5,13},{9,17},{1... | collective-permute-start | bytes 786440 | tf_op jit(solution)/shard_map/ppermute | solution.py:249
  960.3 26.3 %collective-permute-start.31 = (bf16[64,2048]{1,0:T(8,128)(2,1)}, bf16[64,2048]{1,0:T(8,128)(2,1)}, u32[]{:S(2)}, u32[]{:S(2)}) collective-permute-start(bf16[64,2048]{1,0:T(8,128)(2,1)} %fusion.56), channel_id=1, source_target_pairs={{8,0},{12,4},{16,8},{20,12},{24,16},{28,20},{9,1},{13,5},{17,9},{2... | collective-permute-start | bytes 786440 | tf_op jit(solution)/shard_map/ppermute | solution.py:249
  964.6 33.1 %all-to-all-start.1 = ((bf16[4,64,2816]{2,1,0:T(8,128)(2,1)}), bf16[4,64,2816]{2,1,0:T(8,128)(2,1)}, u32[]{:S(2)}, u32[]{:S(2)}) async-start(bf16[4,64,2816]{2,1,0:T(8,128)(2,1)} %bitcast.219), calls=%async_computation.1 | async-start | bytes 2883584 | tf_op jit(solution)/shard_map/all_to_all | solution.py:343
  968.9 20.4 %collective-permute-start.18 = (bf16[64,2560]{1,0:T(8,128)(2,1)S(1)}, bf16[64,2560]{1,0:T(8,128)(2,1)S(1)}, u32[]{:S(2)}, u32[]{:S(2)}) collective-permute-start(bf16[64,2560]{1,0:T(8,128)(2,1)S(1)} %get-tuple-element.79), channel_id=1, source_target_pairs={{0,8},{4,12},{8,16},{12,20},{16,24},{20,28},{1,9},{5,13},{9,17},{1... | collective-permute-start | bytes 983048 | tf_op jit(solution)/shard_map/ppermute | solution.py:249
  (55 other events, 920.5 us)
Sparse Core Ops, SparseCore 0:
  11.5 114.2 all-gather.5
  129.2 76.9 all-gather.7
  207.9 106.6 all-gather.9
  316.6 58.7 all-gather.11
  689.5 135.9 reduce-scatter.3

commit v2 on v1

--- a/solution.py
+++ b/solution.py
@@ -183,6 +183,7 @@
             jax.ShapeDtypeStruct((HEADS, length), f32),
         ),
         compiler_params=pltpu.CompilerParams(vmem_limit_bytes=vmem_limit),
+        cost_estimate=cost(18),
         name="attend",
     )(projected, cosine, sine, seg_col, seg_row)
 
@@ -193,8 +194,398 @@
         attend_grad_kernel,
         out_shape=jax.ShapeDtypeStruct((length, D + 2 * KW), bf16),
         compiler_params=pltpu.CompilerParams(vmem_limit_bytes=vmem_limit),
+        cost_estimate=cost(26),
         name="attend_grad",
     )(qkv, grad_context, log_totals, cosine, sine, seg_col, seg_row)
+
+
+MESH = pl.DeviceIdType.MESH
+
+
+def cost(microseconds):
+    return pl.CostEstimate(flops=0, bytes_accessed=int(microseconds * 3.69e6), transcendentals=0)
+
+
+def place():
+    dp = lax.axis_index("dp")
+    return dp // 2, dp % 2, lax.axis_index("fsdp")
+
+
+def device(line, core, plane):
+    return {"dp": line * 2 + core, "fsdp": plane}
+
+
+def flipped(index, bit):
+    return index + bit - 2 * bit * ((index // bit) % 2)
+
+
+def greet(partners, ends):
+    barrier = pltpu.get_barrier_semaphore()
+    count = len(partners)
+    for partner in partners:
+        pl.semaphore_signal(barrier, inc=1, device_id=partner, device_id_type=MESH)
+    for there, partner in ends:
+        count = count + there
+
+        @pl.when(there == 1)
+        def _():
+            pl.semaphore_signal(barrier, inc=1, device_id=partner, device_id_type=MESH)
+
+    pl.semaphore_wait(barrier, count)
+
+
+def gather_kernel(lines, own, weight, down, full, parts, down_full, cut, line_send, line_recv, x_send, x_recv, y_send, y_recv,
+                  dx_send, dx_recv, dy_send, dy_recv, core_send, core_recv, cut_send, cut_recv, down_send, down_recv, down_core_send,
+                  down_core_recv, here_sem):
+    z, c, f = place()
+    half = own.shape[0] // 2
+    fx, fy = flipped(f, 1), flipped(f, 2)
+    fd = flipped(fx, 2)
+    x_dev, y_dev, core_dev = device(z, c, fx), device(z, c, fy), device(z, 1 - c, f)
+    has_left = jnp.minimum(z, 1)
+    has_right = jnp.minimum(lines - 1 - z, 1)
+    left_dev = device(jnp.maximum(z - 1, 0), c, f)
+    right_dev = device(jnp.minimum(z + 1, lines - 1), c, f)
+    far_dev = device(z, c, fd)
+    greet([x_dev, y_dev, far_dev, core_dev], [(has_left, left_dev), (has_right, right_dev)])
+
+    def cut_copy(k):
+        to = flipped(f, k) if k < 3 else fd
+        return pltpu.make_async_remote_copy(
+            cut.at[to], parts.at[f], cut_send.at[k], cut_recv.at[k], device_id=device(z, c, to), device_id_type=MESH
+        )
+
+    def copy(line, plane, send, recv, dev, src=None, rows=None):
+        dst = full.at[line, c, plane]
+        src = dst if src is None else src
+        if rows is not None:
+            dst, src = dst.at[rows], src.at[rows]
+        return pltpu.make_async_remote_copy(
+            src, dst, send, recv, device_id=dev, device_id_type=MESH
+        )
+
+    def to_right(line, src=None):
+        return copy(line, f, line_send.at[0, line], line_recv.at[line], right_dev, src)
+
+    def to_left(line, src=None):
+        return copy(line, f, line_send.at[1, line], line_recv.at[line], left_dev, src)
+
+    def to_x(line, src=None):
+        return copy(line, f, x_send.at[line], x_recv.at[line], x_dev, src)
+
+    def to_y(line, src=None):
+        return copy(line, f, y_send.at[line], y_recv.at[line], y_dev, src)
+
+    def diag_y(line):
+        return copy(line, fx, dy_send.at[line], dy_recv.at[line], y_dev, None, pl.ds(0, half))
+
+    def diag_x(line):
+        return copy(line, fy, dx_send.at[line], dx_recv.at[line], x_dev, None, pl.ds(half, half))
+
+    def to_core(line, plane, src=None):
+        return copy(line, plane, core_send.at[line, plane], core_recv.at[line, plane], core_dev, src)
+
+    def down_copy(line, way, src=None):
+        dst = down_full.at[line, c]
+        return pltpu.make_async_remote_copy(
+            dst if src is None else src, dst, down_send.at[way, line], down_recv.at[line],
+            device_id=(right_dev, left_dev)[way], device_id_type=MESH,
+        )
+
+    def down_core(line, src=None):
+        dst = down_full.at[line, c]
+        return pltpu.make_async_remote_copy(
+            dst if src is None else src, dst, down_core_send.at[line], down_core_recv.at[line],
+            device_id=core_dev, device_id_type=MESH,
+        )
+
+    here = pltpu.make_async_copy(own, full.at[z, c, f], here_sem.at[0])
+    here.start()
+    here_down = pltpu.make_async_copy(down, down_full.at[z, c], here_sem.at[2])
+    here_down.start()
+
+    @pl.when(has_right == 1)
+    def _():
+        to_right(z, own).start()
+
+    @pl.when(has_left == 1)
+    def _():
+        to_left(z, own).start()
+
+    to_x(z, own).start()
+    to_y(z, own).start()
+    to_core(z, f, own).start()
+
+    cut_columns(weight, cut, 2 * lines, 4)
+    here_cut = pltpu.make_async_copy(cut.at[f], parts.at[f], here_sem.at[1])
+    here_cut.start()
+    for k in range(1, 4):
+        cut_copy(k).start()
+
+    down_core(z, down).start()
+    for t in range(1, lines):
+
+        @pl.when(z >= t)
+        def _():
+            line = z - t
+            to_right(line).wait_recv()
+
+            @pl.when(has_right == 1)
+            def _():
+                to_right(line).start()
+
+            to_x(line).start()
+            to_y(line).start()
+            to_core(line, f).start()
+
+        @pl.when(z + t <= lines - 1)
+        def _():
+            line = z + t
+            to_left(line).wait_recv()
+
+            @pl.when(has_left == 1)
+            def _():
+                to_left(line).start()
+
+            to_x(line).start()
+            to_y(line).start()
+            to_core(line, f).start()
+
+    @pl.when(has_right == 1)
+    def _():
+        down_copy(z, 0, down).start()
+
+    @pl.when(has_left == 1)
+    def _():
+        down_copy(z, 1, down).start()
+
+    here.wait()
+    order = []
+    for t in range(lines):
+        line = z
+        for b in range(lines.bit_length() - 1):
+            if t >> b & 1:
+                line = flipped(line, 1 << b)
+        order.append(line)
+    for t, line in enumerate(order):
+        to_x(line).wait_recv()
+        diag_y(line).start()
+        to_core(line, fx).start()
+        to_y(line).wait_recv()
+        diag_x(line).start()
+        to_core(line, fy).start()
+        if t == 0:
+            continue
+
+        @pl.when(z >= t)
+        def _():
+            down_copy(z - t, 0).wait_recv()
+
+            @pl.when(has_right == 1)
+            def _():
+                down_copy(z - t, 0).start()
+
+            down_core(z - t).start()
+
+        @pl.when(z + t <= lines - 1)
+        def _():
+            down_copy(z + t, 1).wait_recv()
+
+            @pl.when(has_left == 1)
+            def _():
+                down_copy(z + t, 1).start()
+
+            down_core(z + t).start()
+
+    for line in order:
+        diag_y(line).wait_recv()
+        diag_x(line).wait_recv()
+        to_core(line, fd).start()
+    here_cut.wait()
+    here_down.wait()
+    for k in range(1, 4):
+        cut_copy(k).wait()
+    for line in range(lines):
+        for plane in range(4):
+            to_core(line, plane).wait()
+        to_x(line).wait_send()
+        to_y(line).wait_send()
+        diag_x(line).wait_send()
+        diag_y(line).wait_send()
+
+        down_core(line).wait()
+
+        @pl.when((line <= z) & (has_right == 1))
+        def _():
+            to_right(line).wait_send()
+            down_copy(line, 0).wait_send()
+
+        @pl.when((line >= z) & (has_left == 1))
+        def _():
+            to_left(line).wait_send()
+            down_copy(line, 1).wait_send()
+
+
+def gather_all(shard, weight, down, n_dp, n_tp):
+    rows, columns = shard.shape
+    width = weight.shape[1] // n_tp
+    lines = n_dp // 2
+    if n_tp != 4 or rows % 32:
+        full = lax.all_gather(shard, ("dp", "fsdp"), axis=0, tiled=True)
+        down_full = lax.all_gather(down, "dp", axis=0, tiled=True)
+        return full, columns_out(weight, n_dp, n_tp), down_full
+    dma = pltpu.SemaphoreType.DMA
+    hbm = pl.BlockSpec(memory_space=pl.ANY)
+    full, parts, down_full = pl.pallas_call(
+        functools.partial(gather_kernel, lines),
+        out_shape=(
+            jax.ShapeDtypeStruct((lines, 2, n_tp, rows, columns), bf16),
+            jax.ShapeDtypeStruct((n_tp, rows, width), bf16),
+            jax.ShapeDtypeStruct((lines, 2, *down.shape), bf16),
+        ),
+        in_specs=[hbm, pl.BlockSpec(memory_space=pltpu.VMEM), hbm],
+        out_specs=(hbm, hbm, hbm),
+        scratch_shapes=[pltpu.VMEM((n_tp, rows, width), bf16), dma((2, lines))]
+        + [dma((lines,))] * 9
+        + [dma((lines, n_tp))] * 2
+        + [dma((n_tp,)), dma((n_tp,)), dma((2, lines)), dma((lines,)), dma((lines,)), dma((lines,)), dma((3,))],
+        compiler_params=pltpu.CompilerParams(
+            collective_id=0, has_side_effects=True, vmem_limit_bytes=vmem_limit
+        ),
+        cost_estimate=cost(100),
+        name="gather_all",
+    )(shard, weight, down)
+    full = full.reshape(n_dp * n_tp * rows, columns)
+    return full, parts, down_full.reshape(n_dp * down.shape[0], down.shape[1])
+
+
+def cut_columns(weight, cut, n_dp, n_tp):
+    unit = weight.shape[1] // (2 * n_dp * n_tp)
+    half = n_dp * unit
+    for to in range(n_tp):
+        for side in range(2):
+            starts = [side * n_tp * half + (j * n_tp + to) * unit for j in range(n_dp)]
+            pieces = [weight[:, start : start + unit] for start in starts]
+            cut[to, :, side * half : (side + 1) * half] = jnp.concatenate(pieces, axis=1).astype(bf16)
+
+
+def columns_out_kernel(n_dp, n_tp, weight, parts, cut, send, recv, here_sem):
+    z, c, f = place()
+    greet([device(z, c, (f + k) % n_tp) for k in range(1, n_tp)], [])
+
+    def away(k):
+        to = (f + k) % n_tp
+        return pltpu.make_async_remote_copy(
+            cut.at[to], parts.at[f], send.at[k], recv.at[k], device_id=device(z, c, to), device_id_type=MESH
+        )
+
+    cut_columns(weight, cut, n_dp, n_tp)
+    for k in range(1, n_tp):
+        away(k).start()
+    here = pltpu.make_async_copy(cut.at[f], parts.at[f], here_sem)
+    here.start()
+    here.wait()
+    for k in range(1, n_tp):
+        away(k).wait()
+
+
+def columns_out(weight, n_dp, n_tp):
+    rows, width = weight.shape
+    dma = pltpu.SemaphoreType.DMA
+    return pl.pallas_call(
+        functools.partial(columns_out_kernel, n_dp, n_tp),
+        out_shape=jax.ShapeDtypeStruct((n_tp, rows, width // n_tp), bf16),
+        out_specs=pl.BlockSpec(memory_space=pl.ANY),
+        scratch_shapes=[
+            pltpu.VMEM((n_tp, rows, width // n_tp), bf16), dma((n_tp,)), dma((n_tp,)), dma(()),
+        ],
+        compiler_params=pltpu.CompilerParams(
+            collective_id=1, has_side_effects=True, vmem_limit_bytes=vmem_limit
+        ),
+        cost_estimate=cost(20),
+        name="columns_out",
+    )(weight)
+
+
+def columns_back_kernel(n_dp, n_tp, parts, whole, got, send, recv, here_sem):
+    z, c, f = place()
+    greet([device(z, c, (f + k) % n_tp) for k in range(1, n_tp)], [])
+    unit = whole.shape[1] // (2 * n_dp * n_tp)
+    half = n_dp * unit
+
+    def away(k):
+        to = (f + k) % n_tp
+        return pltpu.make_async_remote_copy(
+            parts.at[to], got.at[f], send.at[k], recv.at[k], device_id=device(z, c, to), device_id_type=MESH
+        )
+
+    for k in range(1, n_tp):
+        away(k).start()
+    here = pltpu.make_async_copy(parts.at[f], got.at[f], here_sem)
+    here.start()
+    here.wait()
+    for k in range(1, n_tp):
+        away(k).wait()
+    for side in range(2):
+        pieces = [
+            got[frm, :, side * half + j * unit : side * half + (j + 1) * unit].astype(f32)
+            for j in range(n_dp)
+            for frm in range(n_tp)
+        ]
+        whole[:, side * n_tp * half : (side + 1) * n_tp * half] = jnp.concatenate(pieces, axis=1)
+
+
+def columns_back(parts, n_dp, n_tp):
+    _, rows, width = parts.shape
+    dma = pltpu.SemaphoreType.DMA
+    return pl.pallas_call(
+        functools.partial(columns_back_kernel, n_dp, n_tp),
+        out_shape=jax.ShapeDtypeStruct((rows, width * n_tp), f32),
+        in_specs=[pl.BlockSpec(memory_space=pl.ANY)],
+        scratch_shapes=[pltpu.VMEM(parts.shape, bf16), dma((n_tp,)), dma((n_tp,)), dma(())],
+        compiler_params=pltpu.CompilerParams(
+            collective_id=2, has_side_effects=True, vmem_limit_bytes=vmem_limit
+        ),
+        cost_estimate=cost(20),
+        name="columns_back",
+    )(parts)
+
+
+def total_kernel(n_dp, n_tp, value, total, held, got, send, recv):
+    dp, f = lax.axis_index("dp"), lax.axis_index("fsdp")
+    partners = []
+    for axis, size in (("dp", n_dp), ("fsdp", n_tp)):
+        for bit in range(size.bit_length() - 1):
+            index = {"dp": dp, "fsdp": f}
+            index[axis] = flipped(index[axis], 1 << bit)
+            partners.append(index)
+    greet(partners, [])
+    held[0] = value[...]
+    for step, partner in enumerate(partners):
+        swap = pltpu.make_async_remote_copy(
+            held.at[step], got.at[step], send.at[step], recv.at[step], device_id=partner, device_id_type=MESH
+        )
+        swap.start()
+        swap.wait()
+        held[step + 1] = held[step] + got[step]
+    total[...] = held[len(partners)]
+
+
+def total_over_devices(value, n_dp, n_tp):
+    steps = (n_dp * n_tp).bit_length() - 1
+    dma = pltpu.SemaphoreType.DMA
+    tile = (8, 128)
+    spread = pl.pallas_call(
+        functools.partial(total_kernel, n_dp, n_tp),
+        out_shape=jax.ShapeDtypeStruct(tile, f32),
+        scratch_shapes=[
+            pltpu.VMEM((steps + 1, *tile), f32), pltpu.VMEM((steps, *tile), f32), dma((steps,)), dma((steps,)),
+        ],
+        compiler_params=pltpu.CompilerParams(collective_id=3, has_side_effects=True),
+        cost_estimate=cost(13),
+        name="total",
+    )(jnp.broadcast_to(value, tile))
+    return spread[0, 0]
 
 
 def adam_update(weight, gradient, first, second, rate, decay):
@@ -224,6 +615,15 @@
 
 def plane_swap(block, k, n_tp):
     return lax.ppermute(block, "fsdp", [(i, i ^ k) for i in range(n_tp)])
+
+
+def plane_gather(block, n_tp):
+    if n_tp != 4:
+        return jnp.concatenate([block] + [plane_swap(block, k, n_tp) for k in range(1, n_tp)], axis=0)
+    half = block.shape[0] // 2
+    over_x, over_y = plane_swap(block, 1, n_tp), plane_swap(block, 2, n_tp)
+    far = [plane_swap(over_y[:half], 1, n_tp), plane_swap(over_x[half:], 2, n_tp)]
+    return jnp.concatenate([block, over_x, over_y] + far, axis=0)
 
 
 def core_sum(parts, n_dp):
@@ -258,6 +658,201 @@
         load = lax.dynamic_index_in_dim(parts, here ^ k, 0, keepdims=False).astype(bf16)
         total = total + plane_swap(load, k, n_tp).astype(f32)
     return total
+
+
+def by_rows(rows, body):
+    def step(i, carry):
+        body(pl.ds(pl.multiple_of(i * 16, 16), 16))
+        return carry
+
+    lax.fori_loop(0, rows // 16, step, 0)
+
+
+def scatter_kernel(lines, n_arrays, *refs):
+    groups = [refs[i * n_arrays : (i + 1) * n_arrays] for i in range(8)]
+    arrays, outs, sums, others, firsts, seconds, alongs, leaving = groups
+    load_sem, core_send, core_recv, one_send, one_recv, two_send, two_recv, line_send, line_recv = refs[8 * n_arrays :]
+    z, c, f = place()
+    planes, rows = sums[0].shape[1:3]
+    half = rows // 2
+    fx, fy = flipped(f, 1), flipped(f, 2)
+    fd = flipped(fx, 2)
+    x_dev, y_dev, core_dev = device(z, c, fx), device(z, c, fy), device(z, 1 - c, f)
+    has_left = jnp.minimum(z, 1)
+    has_right = jnp.minimum(lines - 1 - z, 1)
+    left_dev = device(jnp.maximum(z - 1, 0), c, f)
+    right_dev = device(jnp.minimum(z + 1, lines - 1), c, f)
+    greet([x_dev, y_dev, core_dev], [(has_left, left_dev), (has_right, right_dev)])
+    halves = (pl.ds(0, half), pl.ds(half, half))
+    near, next_near, step_dev = (fx, fy), (fy, fx), (x_dev, y_dev)
+
+    def remote(src, dst, send, recv, dev):
+        return pltpu.make_async_remote_copy(src, dst, send, recv, device_id=dev, device_id_type=MESH)
+
+    def to_core(a, d):
+        return remote(arrays[a].at[d, 1 - c], others[a].at[d], core_send.at[a, d], core_recv.at[a, d], core_dev)
+
+    def load(a, d):
+        return pltpu.make_async_copy(arrays[a].at[d, c], sums[a].at[d], load_sem.at[a, d])
+
+    def one(a, d, way, i):
+        block = (near[way], fd)[i]
+        return remote(
+            sums[a].at[d, block, halves[way]], firsts[a].at[way, d, i],
+            one_send.at[a, d, way, i], one_recv.at[a, d, way, i], step_dev[way],
+        )
+
+    def two(a, d, way):
+        return remote(
+            sums[a].at[d, next_near[way], halves[way]], seconds[a].at[way, d],
+            two_send.at[a, d, way], two_recv.at[a, d, way], step_dev[1 - way],
+        )
+
+    def to_right(a, d):
+        return remote(leaving[a].at[d], alongs[a].at[d], line_send.at[a, d], line_recv.at[a, d], right_dev)
+
+    def to_left(a, d, slot):
+        return remote(leaving[a].at[d], alongs[a].at[slot], line_send.at[a, d], line_recv.at[a, slot], left_dev)
+
+    def add_along(a, slot):
+        def step(r):
+            outs[a][r] += alongs[a][slot, r].astype(f32)
+
+        by_rows(rows, step)
+
+    order = []
+    for t in reversed(range(lines)):
+        line = z
+        for b in range(lines.bit_length() - 1):
+            if t >> b & 1:
+                line = flipped(line, 1 << b)
+        order.append(line)
+    chunks = [(a, d) for d in order for a in range(n_arrays)]
+    for a, d in chunks:
+        to_core(a, d).start()
+        load(a, d).start()
+    for a, d in chunks:
+        load(a, d).wait()
+        to_core(a, d).wait_recv()
+
+        def core_add(r):
+            for plane in range(planes):
+                sums[a][d, plane, r] = (sums[a][d, plane, r].astype(f32) + others[a][d, plane, r].astype(f32)).astype(bf16)
+
+        by_rows(rows, core_add)
+        for i in (1, 0):
+            for way in range(2):
+                one(a, d, way, i).start()
+    for a, d in chunks:
+        for way in range(2):
+            one(a, d, way, 1).wait_recv()
+
+            def first_add(r):
+                there = pl.ds(pl.multiple_of(r.start + way * half, 16), r.size)
+                mine = sums[a][d, next_near[way], there].astype(f32)
+                sums[a][d, next_near[way], there] = (mine + firsts[a][way, d, 1, r].astype(f32)).astype(bf16)
+
+            by_rows(half, first_add)
+            two(a, d, way).start()
+    for a, d in chunks:
+        for way in range(2):
+            one(a, d, way, 0).wait_recv()
+            two(a, d, way).wait_recv()
+
+            def second_add(r):
+                there = pl.ds(pl.multiple_of(r.start + way * half, 16), r.size)
+                outs[a][there] = (
+                    sums[a][d, f, there].astype(f32)
+                    + firsts[a][way, d, 0, r].astype(f32)
+                    + seconds[a][way, d, r].astype(f32)
+                )
+
+            by_rows(half, second_add)
+
+        @pl.when((d > z) & (has_left == 1))
+        def _():
+            to_right(a, d).wait_recv()
+            add_along(a, d)
+
+        @pl.when((d < z) & (has_right == 1))
+        def _():
+            to_left(a, d, d).wait_recv()
+            add_along(a, d)
+
+        @pl.when(d != z)
+        def _():
+            def leave(r):
+                leaving[a][d, r] = outs[a][r].astype(bf16)
+
+            by_rows(rows, leave)
+
+        @pl.when(d > z)
+        def _():
+            to_right(a, d).start()
+
+        @pl.when((d < z) & (d + 1 < z))
+        def _():
+            to_left(a, d, d).start()
+
+        @pl.when(d + 1 == z)
+        def _():
+            to_left(a, d, lines).start()
+
+    for a in range(n_arrays):
+
+        @pl.when(has_left == 1)
+        def _():
+            to_right(a, z).wait_recv()
+            add_along(a, z)
+
+        @pl.when(has_right == 1)
+        def _():
+            to_left(a, z, lines).wait_recv()
+            add_along(a, lines)
+
+    for a, d in chunks:
+        to_core(a, d).wait_send()
+        for way in range(2):
+            one(a, d, way, 0).wait_send()
+            one(a, d, way, 1).wait_send()
+            two(a, d, way).wait_send()
+
+        @pl.when(d != z)
+        def _():
+            to_right(a, d).wait_send()
+
+
+def scatter_all(arrays, n_dp, n_tp):
+    lines = n_dp // 2
+    rows = arrays[0].shape[0] // (n_dp * n_tp)
+    if n_tp != 4 or rows % 32:
+        results = []
+        for array in arrays:
+            parts = core_sum(array.reshape(lines, 2, n_tp, rows, -1), n_dp)
+            results.append(line_sum(plane_sum(parts.transpose(1, 0, 2, 3), n_tp), n_dp))
+        return results
+    dma = pltpu.SemaphoreType.DMA
+    widths = [array.shape[1] for array in arrays]
+    n = len(widths)
+    shapes = [
+        (lines, n_tp, rows), (lines, n_tp, rows), (2, lines, 2, rows // 2), (2, lines, rows // 2),
+        (lines + 1, rows), (lines, rows),
+    ]
+    return pl.pallas_call(
+        functools.partial(scatter_kernel, lines, n),
+        out_shape=[jax.ShapeDtypeStruct((rows, width), f32) for width in widths],
+        in_specs=[pl.BlockSpec(memory_space=pl.ANY)] * n,
+        scratch_shapes=[pltpu.VMEM((*shape, width), bf16) for shape in shapes for width in widths]
+        + [dma((n, lines))] * 3
+        + [dma((n, lines, 2, 2))] * 2
+        + [dma((n, lines, 2))] * 2
+        + [dma((n, lines)), dma((n, lines + 1))],
+        compiler_params=pltpu.CompilerParams(
+            collective_id=4, has_side_effects=True, vmem_limit_bytes=vmem_limit
+        ),
+        cost_estimate=cost(110),
+        name="scatter_all",
+    )(*[array.reshape(lines, 2, n_tp, rows, -1) for array in arrays])
 
 
 def local(
@@ -287,20 +882,20 @@
     rows = mlp_weight.shape[0]
     down_rows = down_weight.shape[0]
     ff = n_dp * down_rows
-    both = ("dp", "fsdp")
     cosine, sine = tables(segments[0])
     seg_row = segments
     seg_col = segments.reshape(length, 1)
 
-    gains_full = lax.all_gather(norm_gains.astype(bf16), both, axis=1, tiled=True).astype(f32)
-    qkv_full = lax.all_gather(qkv_weight.astype(bf16), both, axis=0, tiled=True)
-    out_full = lax.all_gather(out_weight.astype(bf16), both, axis=0, tiled=True)
-    mlp_parts = mlp_weight.astype(bf16).reshape(rows, 2, n_dp, n_tp, down_rows)
-    mlp_parts = mlp_parts.transpose(3, 0, 1, 2, 4).reshape(n_tp, rows, 2 * ff)
-    mlp_mine = lax.all_to_all(mlp_parts, "fsdp", 0, 0, tiled=True).reshape(n_tp * rows, 2 * ff)
-    mlp_cols = lax.all_gather(mlp_mine, "dp", axis=0, tiled=True)
-    down_cols = lax.all_gather(down_weight.astype(bf16), "dp", axis=0, tiled=True)
-    grads_in = [cotangent] + [plane_swap(cotangent, k, n_tp) for k in range(1, n_tp)]
+    shard = jnp.concatenate(
+        [qkv_weight, out_weight, jnp.pad(norm_gains.T, ((0, 0), (0, 126)))], axis=1
+    ).astype(bf16)
+    attn_full, mlp_parts, down_cols = gather_all(shard, mlp_weight, down_weight.astype(bf16), n_dp, n_tp)
+    qkv_full = attn_full[:, : D + 2 * KW]
+    out_full = attn_full[:, D + 2 * KW : 2 * D + 2 * KW]
+    gains_full = attn_full[:, 2 * D + 2 * KW :].astype(f32).T
+    mlp_cols = lax.all_gather(mlp_parts.reshape(n_tp * rows, 2 * ff), "dp", axis=0, tiled=True)
+    grads_late, _ = lax.optimization_barrier((cotangent, attn_full))
+    grads_all = plane_gather(grads_late, n_tp)
 
     tokens_f = inputs.astype(f32)
     gain_one, gain_two = gains_full[0], gains_full[1]
@@ -312,10 +907,7 @@
     inverse_two = lax.rsqrt(jnp.mean(middle * middle, axis=-1, keepdims=True) + norm_eps)
     normed_two = (middle * inverse_two * gain_two).astype(bf16)
 
-    normed_all = jnp.concatenate(
-        [normed_two] + [plane_swap(normed_two, k, n_tp) for k in range(1, n_tp)], axis=0
-    )
-    grads_all = jnp.concatenate(grads_in, axis=0)
+    normed_all = plane_gather(normed_two, n_tp)
     hidden = matmul(normed_all, mlp_cols)
     gate, up_part = hidden[:, :ff], hidden[:, ff:]
     sigmoid_gate = jax.nn.sigmoid(gate)
@@ -329,20 +921,18 @@
     grad_normed_two = grad_normed[0]
     for k in range(1, n_tp):
         grad_normed_two = grad_normed_two + plane_swap(grad_normed[k].astype(bf16), k, n_tp).astype(f32)
-    grad_down = matmul_tn(activated, grads_all).astype(bf16).reshape(lines, 2, down_rows, D)
+    grad_down = matmul_tn(activated, grads_all).astype(bf16)
     grad_mlp = matmul_tn(normed_all, grad_hidden).astype(bf16)
-    grad_mlp = grad_mlp.reshape(lines, 2, n_tp * rows, 2 * ff)
-    layer_parts = matmul(activated, down_cols).reshape(n_tp, length, D)
+    layer_parts = matmul(activated, down_cols).astype(bf16).reshape(n_tp, length, D)
+    layer_parts, _ = lax.optimization_barrier((layer_parts, grad_normed_two))
     layer_out = middle + layer_parts[0]
     for k in range(1, n_tp):
-        layer_out = layer_out + plane_swap(layer_parts[k].astype(bf16), k, n_tp).astype(f32)
+        layer_out = layer_out + plane_swap(layer_parts[k], k, n_tp).astype(f32)
     layer_out = layer_out.astype(bf16)
 
-    down_sum = line_sum(core_sum(grad_down, n_dp), n_dp)
-    mlp_sum = line_sum(core_sum(grad_mlp, n_dp), n_dp).astype(bf16).reshape(n_tp, rows, 2 * ff)
-    mlp_sum = lax.all_to_all(mlp_sum, "fsdp", 0, 0, tiled=True)
-    mlp_sum = mlp_sum.reshape(n_tp, rows, 2, n_dp, down_rows).transpose(1, 2, 3, 0, 4)
-    mlp_sum = mlp_sum.reshape(rows, 2 * FF).astype(f32)
+    down_sum = lax.psum_scatter(grad_down, "dp", scatter_dimension=0, tiled=True).astype(f32)
+    mlp_sum = lax.psum_scatter(grad_mlp, "dp", scatter_dimension=0, tiled=True)
+    mlp_sum = columns_back(mlp_sum.reshape(n_tp, rows, 2 * ff), n_dp, n_tp)
 
     gain_grad_two = jnp.sum(grad_normed_two * middle * inverse_two, axis=0)
     weighted_two = grad_normed_two * gain_two
@@ -355,13 +945,8 @@
     grad_context = matmul_t(grad_branch, out_full).astype(bf16)
     grad_projected = attend_grad(qkv, grad_context, log_totals, cosine, sine, seg_col, seg_row)
 
-    def scatter(grads):
-        parts = grads.astype(bf16).reshape(lines, 2, n_tp, rows, -1)
-        parts = core_sum(parts, n_dp).transpose(1, 0, 2, 3)
-        return line_sum(plane_sum(parts, n_tp), n_dp)
-
-    out_sum = scatter(matmul_tn(attended, grad_branch))
-    qkv_sum = scatter(matmul_tn(normed_one, grad_projected))
+    grad_out = matmul_tn(attended, grad_branch).astype(bf16)
+    grad_qkv = matmul_tn(normed_one, grad_projected)
     grad_normed_one = matmul_t(grad_projected, qkv_full)
     gain_grad_one = jnp.sum(grad_normed_one * tokens_f * inverse_one, axis=0)
     weighted_one = grad_normed_one * gain_one
@@ -371,14 +956,17 @@
         - tokens_f * inverse_one**3 * jnp.mean(weighted_one * tokens_f, axis=-1, keepdims=True)
     )
     input_grad = grad_inputs.astype(bf16)
-    gain_grads = jnp.stack([gain_grad_one, gain_grad_two])
-    gains_sum = lax.psum_scatter(gain_grads, both, scatter_dimension=1, tiled=True)
+    gain_grads = jnp.pad(jnp.stack([gain_grad_one, gain_grad_two], axis=1), ((0, 0), (0, 126)))
+    grad_qkv = jnp.concatenate([grad_qkv.astype(bf16), gain_grads.astype(bf16)], axis=1)
+    out_sum, qkv_sum = scatter_all([grad_out, grad_qkv], n_dp, n_tp)
+    gains_sum = qkv_sum[:, D + 2 * KW : D + 2 * KW + 2].T
+    qkv_sum = qkv_sum[:, : D + 2 * KW]
 
     local_squares = (
         jnp.sum(qkv_sum * qkv_sum) + jnp.sum(out_sum * out_sum) + jnp.sum(mlp_sum * mlp_sum)
     )
     local_squares = local_squares + jnp.sum(down_sum * down_sum) + jnp.sum(gains_sum * gains_sum)
-    total_squares = lax.psum(local_squares, both)
+    total_squares = total_over_devices(local_squares, n_dp, n_tp)
     grad_norm = jnp.sqrt(total_squares)
     clip_scale = clip_norm / jnp.maximum(grad_norm, clip_norm)
     qkv_out = adam_update(

time: 1100 us -> 813 us (0.74)
  Pallas kernels: 43.8 us -> 304 us
  blocking collectives: 211 us -> 0 us
  waiting for transfers between devices: 336 us -> 212 us
  local copies, waits for them, and re-layouts: 99.6 us -> 23.2 us
  starting transfers between devices: 89.3 us -> 15.3 us
  other arithmetic: 109 us -> 51.3 us
    pallas_call x0 -> x4, Pallas kernels: none -> 260 us  [the longest x1 122 us: scatter_all(): pl.pallas_call(functools.partial(scatter_kernel, lines, n), out_shape=[ja...]
    all_gather x1 -> x0, blocking collectives: 144 us -> none  [local(): lax.all_gather(norm_gains.astype(bf16), both, axis=1, tiled=True)]
    ppermute x18 -> x14, waiting for transfers between devices: 103 us -> 212 us  [plane_swap(): return lax.ppermute(block, 'fsdp', [(i, i ^ k) for i in range(n_tp)])]
    unnamed x6 -> x3, waiting for transfers between devices: 95.9 us -> 0.05 us
    all_gather x4 -> x1, waiting for transfers between devices: 90 us -> 0.01 us  [local(): lax.all_gather(mlp_parts.reshape(n_tp * rows, 2 * ff), 'dp', axis=0, tile...]
    ppermute x28 -> x0, starting transfers between devices: 61.9 us -> none  [the longest x24 61 us: line_sum(): arrived = lax.ppermute(load.astype(bf16), 'dp', pairs)]
    ppermute x28 -> x0, waiting for transfers between devices: 47.1 us -> none  [the longest x24 47.1 us: line_sum(): arrived = lax.ppermute(load.astype(bf16), 'dp', pairs)]
    psum x1 -> x0, blocking collectives: 40.1 us -> none  [local(): total_squares = lax.psum(local_squares, both)]
  transfers between devices with their start and end apart: 52 -> 17, of which waited for: 14 -> 9; matrix products, arithmetic and copies ran while one was open for 25% -> 20% of each run, Pallas kernels for 4% -> 21%
where the time goes in v2:
time: 813 us; the launch traced here: 806 us
  Pallas kernels  304 us (37%)
  waiting for transfers between devices  212 us (26%)
  matrix products  179 us (22%)
  other arithmetic  51.3 us (6%)
  local copies, waits for them, and re-layouts  23.2 us (3%)
  between operations  20.2 us (2%)
  starting transfers between devices  15.3 us (2%)
    ppermute x14, waiting for transfers between devices, plane_swap(): return lax.ppermute(block, 'fsdp', [(i, i ^ k) for i in range(n_tp)])  212 us
    pallas_call x1, Pallas kernels, scatter_all(): pl.pallas_call(functools.partial(scatter_kernel, lines, n), out_shape=[ja...  122 us
    pallas_call x1, Pallas kernels, gather_all(): pl.pallas_call(functools.partial(gather_kernel, lines), out_shape=(jax.Sh...  103 us
    dot_general x4, matrix products, matmul_t(): lax.dot_general(a, b, (((1,), (1,)), ((), ())), preferred_element_type=f32)  68.1 us
    dot_general x4, matrix products, matmul(): return jnp.dot(a, b, preferred_element_type=f32)  57.2 us
    dot_general x4, matrix products, matmul_tn(): lax.dot_general(a, b, (((0,), (0,)), ((), ())), preferred_element_type=f32)  54.2 us
    pallas_call x1, Pallas kernels, attend_grad(): pl.pallas_call(attend_grad_kernel, out_shape=jax.ShapeDtypeStruct((length...  25.8 us
    pallas_call x1, Pallas kernels, columns_back(): pl.pallas_call(functools.partial(columns_back_kernel, n_dp, n_tp), out_sh...  21.7 us
  transfers between devices with their start and end apart: 17, of which 9 were waited for; matrix products, arithmetic and copies ran while one was open for 20% of the time, Pallas kernels for 21%

profile of v2, /device:TPU:0, one launch (start us, length us, event | category | flops | bytes accessed | tf_op | source)
XLA Modules:
  0.0 805.6 jit_solution(6380516527248734264)
XLA Ops:
  10.2 1.5 convert_element_type.91.down
  11.8 103.3 %gather_all.1 = (bf16[4,2,4,64,4736]{4,3,2,1,0:T(8,128)(2,1)}, bf16[4,64,2816]{2,1,0:T(8,128)(2,1)}, bf16[4,2,176,2048]{3,2,1,0:T(8,128)(2,1)}) custom-call(bf16[64,4736]{1,0:T(8,128)(2,1)S(1)} %fusion.41.own, f32[64,11264]{1,0:T(8,128)} %weight.1, bf16[176,2048]{1,0:T(8,128)(2,1)S(1)} %convert_element_type.91.down), custom_call_target="tpu_custom_call" | custom-call | bytes 369000000 | tf_op jit(solution)/shard_map/gather_all/pallas_call | solution.py:439
  120.9 11.3 %fusion.4.proj = f32[384,2560]{1,0:T(8,128)} fusion(bf16[2048,4736]{1,0:T(8,128)(2,1)} %bitcast.74, bf16[384,2048]{1,0:T(8,128)(2,1)S(1)} %copy-done.13, f32[2048]{0:T(1024)S(1)} %bitcast.69, f32[384]{0:T(512)S(1)} %get-tuple-element.152), kind=kOutput, calls=%fused_computation.7 | convolution fusion | flops 4029677568 | bytes 16000512 | tf_op jit(solution)/shard_map/dot_general | solution.py:601
  132.3 18.0 %attend.1 = (bf16[384,2560]{1,0:T(8,128)(2,1)}, bf16[384,2048]{1,0:T(8,128)(2,1)S(1)}, f32[32,384]{1,0:T(8,128)S(1)}) custom-call(f32[384,2560]{1,0:T(8,128)} %fusion.4.proj, f32[384,128]{1,0:T(8,128)S(1)} %get-tuple-element.160.cosine, f32[384,128]{1,0:T(8,128)S(1)} %get-tuple-element.161.sine, s32[384,1]{1,0:T(8,128)S(1)} %copy.96.seg_col, ...), custom_call_target="tpu_custom_call" | custom-call | bytes 66420000 | tf_op jit(solution)/shard_map/attend/pallas_call | solution.py:178
  150.3 6.6 multiply_reduce_fusion.2
  158.7 1.5 collective-permute-start.1
  160.3 1.8 collective-permute-start.5
  164.0 31.9 %collective-permute-done.1 = bf16[384,2048]{1,0:T(8,128)(2,1)S(1)} collective-permute-done((bf16[384,2048]{1,0:T(8,128)(2,1)S(1)}, bf16[384,2048]{1,0:T(8,128)(2,1)S(1)}, u32[]{:S(2)}, u32[]{:S(2)}) %collective-permute-start.1) | collective-permute-done | bytes 1572896 | tf_op jit(solution)/shard_map/ppermute | solution.py:617
  196.0 1.5 collective-permute-start.2
  198.1 31.5 %collective-permute-done.5 = bf16[384,2048]{1,0:T(8,128)(2,1)S(1)} collective-permute-done((bf16[384,2048]{1,0:T(8,128)(2,1)S(1)}, bf16[384,2048]{1,0:T(8,128)(2,1)S(1)}, u32[]{:S(2)}, u32[]{:S(2)}) %collective-permute-start.5) | collective-permute-done | bytes 1572896 | tf_op jit(solution)/shard_map/ppermute | solution.py:617
  229.7 1.5 collective-permute-start.6
  234.6 13.3 %collective-permute-done.2 = bf16[192,2048]{1,0:T(8,128)(2,1)S(1)} collective-permute-done((bf16[192,2048]{1,0:T(8,128)(2,1)S(1)}, bf16[192,2048]{1,0:T(8,128)(2,1)S(1)}, u32[]{:S(2)}, u32[]{:S(2)}) %collective-permute-start.2) | collective-permute-done | bytes 786464 | tf_op jit(solution)/shard_map/ppermute | solution.py:617
  248.1 15.8 %collective-permute-done.6 = bf16[192,2048]{1,0:T(8,128)(2,1)S(1)} collective-permute-done((bf16[192,2048]{1,0:T(8,128)(2,1)S(1)}, bf16[192,2048]{1,0:T(8,128)(2,1)S(1)}, u32[]{:S(2)}, u32[]{:S(2)}) %collective-permute-start.6) | collective-permute-done | bytes 786464 | tf_op jit(solution)/shard_map/ppermute | solution.py:617
  265.8 25.7 %fusion.63 = f32[1536,2816]{1,0:T(8,128)} fusion(bf16[1536,2048]{1,0:T(8,128)(2,1)} %copy-done.27, bf16[2048,2816]{1,0:T(8,128)(2,1)} %all-gather.2.cloned.1.call-done), kind=kOutput, calls=%fused_computation.129 | convolution fusion | flops 17716740096 | bytes 35127296 | tf_op jit(solution)/shard_map/dot_general | solution.py:601
  291.6 23.2 %multiply_convert_fusion.1 = (bf16[1536,1408]{1,0:T(8,128)(2,1)}, bf16[1536,1408]{1,0:T(8,128)(2,1)}, bf16[1536,1408]{1,0:T(8,128)(2,1)}) fusion(f32[1536,2816]{1,0:T(8,128)} %fusion.63, bf16[1536,2048]{1,0:T(8,128)(2,1)} %constant_dynamic-update-slice_fusion.5, bf16[1408,2048]{1,0:T(8,128)(2,1)} %bitcast.78), kind=kOutput, calls=%fused_computation.11 | convolution fusion | flops 8890810368 | bytes 42336256 | tf_op jit(solution)/shard_map/dot_general | solution.py:605
  314.8 14.2 %convolution_convert_fusion.2 = bf16[1408,2048]{1,0:T(8,128)(2,1)} fusion(bf16[1536,1408]{1,0:T(8,128)(2,1)} %get-tuple-element.135, bf16[1536,2048]{1,0:T(8,128)(2,1)} %constant_dynamic-update-slice_fusion.5), kind=kOutput, calls=%fused_computation.15 | convolution fusion | flops 8861253632 | bytes 16384000 | tf_op jit(solution)/shard_map/dot_general | solution.py:609
  329.1 24.9 %convolution_convert_fusion = bf16[2048,2816]{1,0:T(8,128)(2,1)} fusion(bf16[1536,2048]{1,0:T(8,128)(2,1)} %copy-done.27, bf16[1536,1408]{1,0:T(8,128)(2,1)} %get-tuple-element.134, bf16[1536,1408]{1,0:T(8,128)(2,1)} %get-tuple-element.133), kind=kOutput, calls=%fused_computation.2 | convolution fusion | flops 17739808768 | bytes 26476544 | tf_op jit(solution)/shard_map/dot_general | solution.py:609
  354.0 26.0 %fusion.62 = (bf16[1536,2048]{1,0:T(8,128)(2,1)}, f32[1536,2048]{1,0:T(8,128)}) fusion(bf16[2048,2816]{1,0:T(8,128)(2,1)} %all-gather.2.cloned.1.call-done, bf16[1536,1408]{1,0:T(8,128)(2,1)} %get-tuple-element.134, bf16[1536,1408]{1,0:T(8,128)(2,1)} %get-tuple-element.133), kind=kOutput, calls=%fused_computation.128 | convolution fusion | flops 17737187328 | bytes 39059456 | tf_op jit(solution)/shard_map/dot_general | solution.py:605
  380.0 2.8 fusion.60
  382.8 1.4 collective-permute-start.10
  384.9 1.5 collective-permute-start.9
  386.4 13.5 %convolution_convert_fusion.4 = bf16[1536,2048]{1,0:T(8,128)(2,1)S(1)} fusion(bf16[1536,1408]{1,0:T(8,128)(2,1)} %get-tuple-element.135, bf16[1408,2048]{1,0:T(8,128)(2,1)} %bitcast.79), kind=kOutput, calls=%fused_computation.17 | convolution fusion | flops 8861515776 | bytes 16384000 | tf_op jit(solution)/shard_map/dot_general | solution.py:601
  399.9 21.2 %collective-permute-done.10 = bf16[384,2048]{1,0:T(8,128)(2,1)S(1)} collective-permute-done((bf16[384,2048]{1,0:T(8,128)(2,1)S(1)}, bf16[384,2048]{1,0:T(8,128)(2,1)S(1)}, u32[]{:S(2)}, u32[]{:S(2)}) %collective-permute-start.10) | collective-permute-done | bytes 1572896 | tf_op jit(solution)/shard_map/ppermute | solution.py:617
  421.2 31.0 %collective-permute-done.8 = bf16[384,2048]{1,0:T(8,128)(2,1)S(1)} collective-permute-done((bf16[384,2048]{1,0:T(8,128)(2,1)S(1)}, bf16[384,2048]{1,0:T(8,128)(2,1)S(1)}, u32[]{:S(2)}, u32[]{:S(2)}) %collective-permute-start.8) | collective-permute-done | bytes 1572896 | tf_op jit(solution)/shard_map/ppermute | solution.py:617
  453.0 4.5 multiply_reduce_fusion
  457.6 2.4 slice_bitcast_fusion.2
  460.6 1.4 collective-permute-start.12
  462.0 1.5 collective-permute-start.13
  463.8 33.7 %collective-permute-done.11 = bf16[384,2048]{1,0:T(8,128)(2,1)} collective-permute-done((bf16[384,2048]{1,0:T(8,128)(2,1)}, bf16[384,2048]{1,0:T(8,128)(2,1)}, u32[]{:S(2)}, u32[]{:S(2)}) %collective-permute-start.11) | collective-permute-done | bytes 1572896 | tf_op jit(solution)/shard_map/ppermute | solution.py:617
  497.5 33.0 %collective-permute-done.12 = bf16[384,2048]{1,0:T(8,128)(2,1)} collective-permute-done((bf16[384,2048]{1,0:T(8,128)(2,1)}, bf16[384,2048]{1,0:T(8,128)(2,1)}, u32[]{:S(2)}, u32[]{:S(2)}) %collective-permute-start.12) | collective-permute-done | bytes 1572896 | tf_op jit(solution)/shard_map/ppermute | solution.py:617
  530.6 6.3 multiply_subtract_fusion
  536.9 8.0 fusion.30.grad_context
  545.0 25.8 %attend_grad.1 = bf16[384,2560]{1,0:T(8,128)(2,1)} custom-call(bf16[384,2560]{1,0:T(8,128)(2,1)} %get-tuple-element.34.qkv, bf16[384,2048]{1,0:T(8,128)(2,1)S(1)} %fusion.30.grad_context, f32[32,384]{1,0:T(8,128)S(1)} %get-tuple-element.35.log_totals, f32[384,128]{1,0:T(8,128)S(1)} %copy-done.1, f32[384,128]{1,0:T(8,128)S(1)} %copy-done.3, ...), custom_call_target="tpu_custom_call" | custom-call | bytes 95940000 | tf_op jit(solution)/shard_map/attend_grad/pallas_call | solution.py:193
  570.8 10.9 %fusion.20 = (bf16[2048]{0:T(1024)(128)(2,1)S(1)}, f32[384]{0:T(512)S(1)}, f32[384,2048]{1,0:T(8,128)}) fusion(bf16[384,2048]{1,0:T(8,128)(2,1)S(1)} %copy-done.14, f32[384]{0:T(512)S(1)} %copy-done.37, f32[2048]{0:T(1024)S(1)} %bitcast.70, bf16[384,2560]{1,0:T(8,128)(2,1)} %attend_grad.1, bf16[2048,4736]{1,0:T(8,128)(2,1)} %bitcast.77), kind=kOutput, calls=%fused_computation.38 | convolution fusion | flops 4032034304 | bytes 17185792 | tf_op jit(solution)/shard_map/dot_general | solution.py:605
  582.8 8.8 %convolution_convert_fusion.3 = bf16[2048,2048]{1,0:T(8,128)(2,1)} fusion(bf16[384,2048]{1,0:T(8,128)(2,1)S(1)} %copy-done.7, f32[384,2048]{1,0:T(8,128)} %copy-done.10), kind=kOutput, calls=%fused_computation.16 | convolution fusion | flops 3226206208 | bytes 13107200 | tf_op jit(solution)/shard_map/dot_general | solution.py:609
  591.6 6.3 convolution_convert_fusion.1
  597.9 4.7 fusion.1
  602.6 121.5 %scatter_all.1 = (f32[64,2048]{1,0:T(8,128)S(1)}, f32[64,2688]{1,0:T(8,128)S(1)}) custom-call(bf16[4,2,4,64,2048]{4,3,2,1,0:T(8,128)(2,1)} %bitcast.62, bf16[4,2,4,64,2688]{4,3,2,1,0:T(8,128)(2,1)} %bitcast.61), custom_call_target="tpu_custom_call" | custom-call | bytes 405900000 | tf_op jit(solution)/shard_map/scatter_all/pallas_call | solution.py:841
  727.5 4.9 fusion.17
  732.4 2.1 fusion.35
  734.5 1.4 copy-done.4
  735.9 21.7 %columns_back.1 = f32[64,11264]{1,0:T(8,128)} custom-call(bf16[4,64,2816]{2,1,0:T(8,128)(2,1)S(1)} %bitcast.59), custom_call_target="tpu_custom_call" | custom-call | bytes 73800000 | tf_op jit(solution)/shard_map/columns_back/pallas_call | solution.py:541
  757.6 3.2 multiply_reduce_fusion.3
  763.3 13.2 %total.1 = f32[8,128]{1,0:T(8,128)} custom-call(f32[8,128]{1,0:T(8,128)} %broadcast_in_dim.7.value), custom_call_target="tpu_custom_call" | custom-call | bytes 47970000 | tf_op jit(solution)/shard_map/total/pallas_call | solution.py:578
  780.6 9.4 %multiply_subtract_fusion.1 = (f32[64,11264]{1,0:T(8,128)}, f32[64,11264]{1,0:T(8,128)}, f32[64,11264]{1,0:T(8,128)}) fusion(f32[64,11264]{1,0:T(8,128)} %weight.1, f32[64,11264]{1,0:T(8,128)} %columns_back.1, f32[]{:T(128)S(6)} %div.106, f32[64,11264]{1,0:T(8,128)} %param.28, f32[64,11264]{1,0:T(8,128)} %param.33), kind=kLoop, calls=%fused_computation.53 | loop fusion | flops 11534336 | bytes 20185092 | tf_op jit(solution)/shard_map/sub | solution.py:596
  790.1 1.4 multiply_subtract_fusion.4
  792.1 1.6 multiply_subtract_fusion.3
  794.9 2.8 multiply_subtract_fusion.2
  (166 shorter events, 29.8 us)
Async XLA Ops:
  7.2 258.7 %all-gather.2.cloned.1.call-start = ((), (), s32[]{:S(2)}) async-start(), calls=%async_computation.2 | async-start | bytes 12976128 | tf_op jit(solution)/shard_map/all_gather | solution.py:896
  11.8 104.8 %copy-start.5 = (s32[1,384]{1,0:T(1,128)S(1)}, s32[1,384]{1,0:T(1,128)}, u32[]{:S(2)}) copy-start(s32[1,384]{1,0:T(1,128)} %seg_row.3) | copy-start | bytes 4612
  115.0 4.7 copy-start.13
  115.1 617.4 %reduce-scatter.5.cloned.1.call-start = ((), (), s32[]{:S(2)}) async-start(), calls=%async_computation.4 | async-start | bytes 6488064 | tf_op jit(solution)/shard_map/reduce_scatter | solution.py:933
  119.8 12.5 %copy-start = (f32[384,128]{1,0:T(8,128)}, f32[384,128]{1,0:T(8,128)S(1)}, u32[]{:S(2)}) copy-start(f32[384,128]{1,0:T(8,128)S(1)} %get-tuple-element.160.cosine) | copy-start | bytes 589828
  119.8 12.5 %copy-start.2 = (f32[384,128]{1,0:T(8,128)}, f32[384,128]{1,0:T(8,128)S(1)}, u32[]{:S(2)}) copy-start(f32[384,128]{1,0:T(8,128)S(1)} %get-tuple-element.161.sine) | copy-start | bytes 589828
  120.8 11.5 %copy-start.36 = (f32[384]{0:T(512)}, f32[384]{0:T(512)S(1)}, u32[]{:S(2)}) copy-start(f32[384]{0:T(512)S(1)} %get-tuple-element.152) | copy-start | bytes 4612
  120.9 11.3 %copy-start.32 = (f32[1,2048]{1,0:T(1,128)}, f32[1,2048]{1,0:T(1,128)S(1)}, u32[]{:S(2)}) copy-start(f32[1,2048]{1,0:T(1,128)S(1)} %get-tuple-element.145) | copy-start | bytes 24580
  120.9 36.7 %copy-start.28 = (f32[1,2048]{1,0:T(1,128)}, f32[1,2048]{1,0:T(1,128)S(1)}, u32[]{:S(2)}) copy-start(f32[1,2048]{1,0:T(1,128)S(1)} %get-tuple-element.144) | copy-start | bytes 24580
  150.3 6.6 copy-start.6
  158.7 37.2 %collective-permute-start.1 = (bf16[384,2048]{1,0:T(8,128)(2,1)S(1)}, bf16[384,2048]{1,0:T(8,128)(2,1)S(1)}, u32[]{:S(2)}, u32[]{:S(2)}) collective-permute-start(bf16[384,2048]{1,0:T(8,128)(2,1)S(1)} %get-tuple-element.132), channel_id=1, source_target_pairs={{0,2},{1,3},{2,0},{3,1},{4,6},{5,7},{6,4},{7,5},{8,10},{9,11},{10,... | collective-permute-start | bytes 4718600 | tf_op jit(solution)/shard_map/ppermute | solution.py:617
  160.2 37.3 %collective-permute-start = (bf16[384,2048]{1,0:T(8,128)(2,1)S(1)}, bf16[384,2048]{1,0:T(8,128)(2,1)S(1)}, u32[]{:S(2)}, u32[]{:S(2)}) collective-permute-start(bf16[384,2048]{1,0:T(8,128)(2,1)S(1)} %get-tuple-element.132), channel_id=1, source_target_pairs={{0,1},{1,0},{2,3},{3,2},{4,5},{5,4},{6,7},{7,6},{8,9},{9,8},{10,11... | collective-permute-start | bytes 4718600 | tf_op jit(solution)/shard_map/ppermute | solution.py:617
  160.3 69.3 %collective-permute-start.5 = (bf16[384,2048]{1,0:T(8,128)(2,1)S(1)}, bf16[384,2048]{1,0:T(8,128)(2,1)S(1)}, u32[]{:S(2)}, u32[]{:S(2)}) collective-permute-start(bf16[384,2048]{1,0:T(8,128)(2,1)S(1)} %copy-done.12), channel_id=1, source_target_pairs={{0,2},{1,3},{2,0},{3,1},{4,6},{5,7},{6,4},{7,5},{8,10},{9,11},{10,... | collective-permute-start | bytes 4718600 | tf_op jit(solution)/shard_map/ppermute | solution.py:617
  162.1 69.0 %collective-permute-start.4 = (bf16[384,2048]{1,0:T(8,128)(2,1)S(1)}, bf16[384,2048]{1,0:T(8,128)(2,1)S(1)}, u32[]{:S(2)}, u32[]{:S(2)}) collective-permute-start(bf16[384,2048]{1,0:T(8,128)(2,1)S(1)} %copy-done.12), channel_id=1, source_target_pairs={{0,1},{1,0},{2,3},{3,2},{4,5},{5,4},{6,7},{7,6},{8,9},{9,8},{10,11... | collective-permute-start | bytes 4718600 | tf_op jit(solution)/shard_map/ppermute | solution.py:617
  196.0 52.0 %collective-permute-start.2 = (bf16[192,2048]{1,0:T(8,128)(2,1)S(1)}, bf16[192,2048]{1,0:T(8,128)(2,1)S(1)}, u32[]{:S(2)}, u32[]{:S(2)}) collective-permute-start(bf16[192,2048]{1,0:T(8,128)(2,1)S(1)} %slice.122), channel_id=1, source_target_pairs={{0,1},{1,0},{2,3},{3,2},{4,5},{5,4},{6,7},{7,6},{8,9},{9,8},{10,11... | collective-permute-start | bytes 2359304 | tf_op jit(solution)/shard_map/ppermute | solution.py:617
  197.5 50.5 %collective-permute-start.3 = (bf16[192,2048]{1,0:T(8,128)(2,1)S(1)}, bf16[192,2048]{1,0:T(8,128)(2,1)S(1)}, u32[]{:S(2)}, u32[]{:S(2)}) collective-permute-start(bf16[192,2048]{1,0:T(8,128)(2,1)S(1)} %slice.123), channel_id=1, source_target_pairs={{0,2},{1,3},{2,0},{3,1},{4,6},{5,7},{6,4},{7,5},{8,10},{9,11},{10,... | collective-permute-start | bytes 2359304 | tf_op jit(solution)/shard_map/ppermute | solution.py:617
  229.7 34.3 %collective-permute-start.6 = (bf16[192,2048]{1,0:T(8,128)(2,1)S(1)}, bf16[192,2048]{1,0:T(8,128)(2,1)S(1)}, u32[]{:S(2)}, u32[]{:S(2)}) collective-permute-start(bf16[192,2048]{1,0:T(8,128)(2,1)S(1)} %slice.126), channel_id=1, source_target_pairs={{0,1},{1,0},{2,3},{3,2},{4,5},{5,4},{6,7},{7,6},{8,9},{9,8},{10,11... | collective-permute-start | bytes 2359304 | tf_op jit(solution)/shard_map/ppermute | solution.py:617
  231.2 33.7 %collective-permute-start.7 = (bf16[192,2048]{1,0:T(8,128)(2,1)S(1)}, bf16[192,2048]{1,0:T(8,128)(2,1)S(1)}, u32[]{:S(2)}, u32[]{:S(2)}) collective-permute-start(bf16[192,2048]{1,0:T(8,128)(2,1)S(1)} %slice.127), channel_id=1, source_target_pairs={{0,2},{1,3},{2,0},{3,1},{4,6},{5,7},{6,4},{7,5},{8,10},{9,11},{10,... | collective-permute-start | bytes 2359304 | tf_op jit(solution)/shard_map/ppermute | solution.py:617
  248.1 16.8 %copy-start.27 = (bf16[1536,2048]{1,0:T(8,128)(2,1)}, bf16[1536,2048]{1,0:T(8,128)(2,1)S(1)}, u32[]{:S(2)}) copy-start(bf16[1536,2048]{1,0:T(8,128)(2,1)S(1)} %constant_dynamic-update-slice_fusion) | copy-start | bytes 18874372
  329.1 405.5 %reduce-scatter.3.cloned.1.call-start = ((), (), s32[]{:S(2)}) async-start(), calls=%async_computation.3 | async-start | bytes 12976128 | tf_op jit(solution)/shard_map/reduce_scatter | solution.py:934
  382.8 38.3 %collective-permute-start.10 = (bf16[384,2048]{1,0:T(8,128)(2,1)S(1)}, bf16[384,2048]{1,0:T(8,128)(2,1)S(1)}, u32[]{:S(2)}, u32[]{:S(2)}) collective-permute-start(bf16[384,2048]{1,0:T(8,128)(2,1)S(1)} %get-tuple-element.140), channel_id=1, source_target_pairs={{0,3},{1,2},{2,1},{3,0},{4,7},{5,6},{6,5},{7,4},{8,11},{9,10},{10,... | collective-permute-start | bytes 4718600 | tf_op jit(solution)/shard_map/ppermute | solution.py:617
  384.3 67.9 %collective-permute-start.8 = (bf16[384,2048]{1,0:T(8,128)(2,1)S(1)}, bf16[384,2048]{1,0:T(8,128)(2,1)S(1)}, u32[]{:S(2)}, u32[]{:S(2)}) collective-permute-start(bf16[384,2048]{1,0:T(8,128)(2,1)S(1)} %get-tuple-element.139), channel_id=1, source_target_pairs={{0,1},{1,0},{2,3},{3,2},{4,5},{5,4},{6,7},{7,6},{8,9},{9,8},{10,11... | collective-permute-start | bytes 4718600 | tf_op jit(solution)/shard_map/ppermute | solution.py:617
  384.9 68.1 %copy-start.9 = (f32[384,2048]{1,0:T(8,128)S(1)}, f32[384,2048]{1,0:T(8,128)}, u32[]{:S(2)}) copy-start(f32[384,2048]{1,0:T(8,128)} %copy-done.8) | copy-start | bytes 9437188
  384.9 68.1 %copy-start.29 = (f32[1,2048]{1,0:T(1,128)S(1)}, f32[1,2048]{1,0:T(1,128)}, u32[]{:S(2)}) copy-start(f32[1,2048]{1,0:T(1,128)} %copy-done.28) | copy-start | bytes 24580
  384.9 68.1 %copy-start.31 = (f32[384]{0:T(512)S(1)}, f32[384]{0:T(512)}, u32[]{:S(2)}) copy-start(f32[384]{0:T(512)} %copy-done.30) | copy-start | bytes 4612
  384.9 68.1 %collective-permute-start.9 = (bf16[384,2048]{1,0:T(8,128)(2,1)S(1)}, bf16[384,2048]{1,0:T(8,128)(2,1)S(1)}, u32[]{:S(2)}, u32[]{:S(2)}) collective-permute-start(bf16[384,2048]{1,0:T(8,128)(2,1)S(1)} %get-tuple-element.141), channel_id=1, source_target_pairs={{0,2},{1,3},{2,0},{3,1},{4,6},{5,7},{6,4},{7,5},{8,10},{9,11},{10,... | collective-permute-start | bytes 4718600 | tf_op jit(solution)/shard_map/ppermute | solution.py:617
  399.9 57.7 %copy-start.11 = (bf16[1536,2048]{1,0:T(8,128)(2,1)}, bf16[1536,2048]{1,0:T(8,128)(2,1)S(1)}, u32[]{:S(2)}) copy-start(bf16[1536,2048]{1,0:T(8,128)(2,1)S(1)} %convolution_convert_fusion.4) | copy-start | bytes 18874372
  457.6 5.9 copy-start.38
  457.6 6.0 copy-start.39
  457.6 6.1 copy-start.40
  457.6 73.0 %copy-start.34 = (f32[384]{0:T(512)S(1)}, f32[384]{0:T(512)}, u32[]{:S(2)}) copy-start(f32[384]{0:T(512)} %get-tuple-element.153) | copy-start | bytes 4612
  460.0 37.6 %collective-permute-start.11 = (bf16[384,2048]{1,0:T(8,128)(2,1)}, bf16[384,2048]{1,0:T(8,128)(2,1)}, u32[]{:S(2)}, u32[]{:S(2)}) collective-permute-start(bf16[384,2048]{1,0:T(8,128)(2,1)} %get-tuple-element.136), channel_id=1, source_target_pairs={{0,1},{1,0},{2,3},{3,2},{4,5},{5,4},{6,7},{7,6},{8,9},{9,8},{10,11... | collective-permute-start | bytes 4718600 | tf_op jit(solution)/shard_map/ppermute | solution.py:617
  460.6 70.0 %collective-permute-start.12 = (bf16[384,2048]{1,0:T(8,128)(2,1)}, bf16[384,2048]{1,0:T(8,128)(2,1)}, u32[]{:S(2)}, u32[]{:S(2)}) collective-permute-start(bf16[384,2048]{1,0:T(8,128)(2,1)} %get-tuple-element.138), channel_id=1, source_target_pairs={{0,2},{1,3},{2,0},{3,1},{4,6},{5,7},{6,4},{7,5},{8,10},{9,11},{10,... | collective-permute-start | bytes 4718600 | tf_op jit(solution)/shard_map/ppermute | solution.py:617
  462.0 68.6 %collective-permute-start.13 = (bf16[384,2048]{1,0:T(8,128)(2,1)}, bf16[384,2048]{1,0:T(8,128)(2,1)}, u32[]{:S(2)}, u32[]{:S(2)}) collective-permute-start(bf16[384,2048]{1,0:T(8,128)(2,1)} %get-tuple-element.137), channel_id=1, source_target_pairs={{0,3},{1,2},{2,1},{3,0},{4,7},{5,6},{6,5},{7,4},{8,11},{9,10},{10,... | collective-permute-start | bytes 4718600 | tf_op jit(solution)/shard_map/ppermute | solution.py:617
  536.9 8.0 copy-start.10
  536.9 8.1 %copy-start.1 = (f32[384,128]{1,0:T(8,128)S(1)}, f32[384,128]{1,0:T(8,128)}, u32[]{:S(2)}) copy-start(f32[384,128]{1,0:T(8,128)} %copy-done) | copy-start | bytes 589828
  536.9 8.1 %copy-start.3 = (f32[384,128]{1,0:T(8,128)S(1)}, f32[384,128]{1,0:T(8,128)}, u32[]{:S(2)}) copy-start(f32[384,128]{1,0:T(8,128)} %copy-done.2) | copy-start | bytes 589828
  544.9 25.9 %copy-start.14 = (bf16[384,2048]{1,0:T(8,128)(2,1)S(1)}, bf16[384,2048]{1,0:T(8,128)(2,1)}, u32[]{:S(2)}) copy-start(bf16[384,2048]{1,0:T(8,128)(2,1)} %param.18) | copy-start | bytes 4718596
  544.9 25.9 %copy-start.33 = (f32[1,2048]{1,0:T(1,128)S(1)}, f32[1,2048]{1,0:T(1,128)}, u32[]{:S(2)}) copy-start(f32[1,2048]{1,0:T(1,128)} %copy-done.32) | copy-start | bytes 24580
  544.9 25.9 %copy-start.37 = (f32[384]{0:T(512)S(1)}, f32[384]{0:T(512)}, u32[]{:S(2)}) copy-start(f32[384]{0:T(512)} %copy-done.36) | copy-start | bytes 4612
  570.8 12.0 %copy-start.7 = (bf16[384,2048]{1,0:T(8,128)(2,1)S(1)}, bf16[384,2048]{1,0:T(8,128)(2,1)}, u32[]{:S(2)}) copy-start(bf16[384,2048]{1,0:T(8,128)(2,1)} %copy-done.6) | copy-start | bytes 4718596
  582.8 8.8 %copy-start.20 = (bf16[384,2560]{1,0:T(8,128)(2,1)S(1)}, bf16[384,2560]{1,0:T(8,128)(2,1)}, u32[]{:S(2)}) copy-start(bf16[384,2560]{1,0:T(8,128)(2,1)} %attend_grad.1) | copy-start | bytes 5898244
  591.6 6.3 copy-start.18
  602.6 125.0 %copy-start.35 = (f32[384]{0:T(512)S(1)}, f32[384]{0:T(512)}, u32[]{:S(2)}) copy-start(f32[384]{0:T(512)} %get-tuple-element.151) | copy-start | bytes 4612
  780.6 9.4 %copy-start.19 = (f32[64,2048]{1,0:T(8,128)S(1)}, f32[64,2048]{1,0:T(8,128)}, u32[]{:S(2)}) copy-start(f32[64,2048]{1,0:T(8,128)} %param.22) | copy-start | bytes 1572868
  780.6 9.4 %copy-start.25 = (f32[64,2048]{1,0:T(8,128)S(1)}, f32[64,2048]{1,0:T(8,128)}, u32[]{:S(2)}) copy-start(f32[64,2048]{1,0:T(8,128)} %param.27) | copy-start | bytes 1572868
  780.6 9.4 %copy-start.26 = (f32[64,2048]{1,0:T(8,128)S(1)}, f32[64,2048]{1,0:T(8,128)}, u32[]{:S(2)}) copy-start(f32[64,2048]{1,0:T(8,128)} %param.32) | copy-start | bytes 1572868
  790.1 3.6 copy-start.22
  (10 other events, 19.1 us)
Sparse Core Ops, SparseCore 0:
  115.2 108.3 all-gather.1
  329.2 65.1 reduce-scatter.4
  396.7 117.6 reduce-scatter.2

commit v3 on v2

--- a/solution.py
+++ b/solution.py
@@ -171,6 +171,7 @@
 
 
 vmem_limit = 50 * 1024 * 1024
+feed_vmem_limit = 62 * 1024 * 1024
 
 
 def attend(projected, cosine, sine, seg_col, seg_row):
@@ -855,6 +856,363 @@
     )(*[array.reshape(lines, 2, n_tp, rows, -1) for array in arrays])
 
 
+def rope_tile(tile, cos, sin):
+    pairs = [tile[:, i : i + 128] for i in range(0, tile.shape[1], 128)]
+    return jnp.concatenate([pair * cos + halves_swapped(pair) * sin for pair in pairs], axis=1)
+
+
+def attend_heads(qkv, context, log_totals, allowed):
+    length = qkv.shape[0]
+    scale = HD ** (-0.5)
+    for group in range(KVH):
+        kc = D + (group // 2) * 128
+        keys = both_places(qkv[:, kc : kc + 128], group % 2)
+        values = both_places(qkv[:, kc + KW : kc + KW + 128], group % 2)
+
+        def pair_step(pair_index, carry):
+            pair = group * (GROUP // 2) + pair_index
+            lanes = pl.ds(pl.multiple_of(pair * 128, 128), 128)
+            queries = qkv[:, lanes]
+            total = jnp.zeros((length, 128), f32)
+            for side in range(2):
+                scores = dot_t(keys[side], queries) * scale
+                scores = jnp.where(allowed, scores, -1e30)
+                top = jnp.max(scores, axis=0, keepdims=True)
+                raised = jnp.exp(scores - top)
+                totals = jnp.sum(raised, axis=0, keepdims=True)
+                probs = (raised / totals).astype(bf16)
+                total = total + dot_tn(probs, values[side])
+                log_totals[pl.ds(2 * pair + side, 1), :] = top + jnp.log(totals)
+            context[:, lanes] = total.astype(bf16)
+            return carry
+
+        lax.fori_loop(0, GROUP // 2, pair_step, 0)
+
+
+def tile_at(i, width, start=0):
+    return pl.ds(pl.multiple_of(start + i * width, 128), width)
+
+
+class Exchange:
+    def __init__(self, own, whole, sems, i, x_dev, y_dev):
+        send, recv, here = sems
+        half = own.shape[0] // 2
+
+        def remote(src, dst, k, dev):
+            return pltpu.make_async_remote_copy(
+                src, dst, send.at[i, k], recv.at[i, k], device_id=dev, device_id_type=MESH
+            )
+
+        low, high = pl.ds(0, half), pl.ds(half, half)
+        self.near = [remote(own, whole.at[1], 0, x_dev), remote(own, whole.at[2], 1, y_dev)]
+        self.far = [
+            remote(whole.at[2, low], whole.at[3, low], 2, x_dev),
+            remote(whole.at[1, high], whole.at[3, high], 3, y_dev),
+        ]
+        self.here = pltpu.make_async_copy(own, whole.at[0], here.at[i])
+
+    def start(self):
+        for copy in self.near:
+            copy.start()
+        self.here.start()
+
+    def pass_on(self):
+        for copy in self.near:
+            copy.wait_recv()
+        for copy in self.far:
+            copy.start()
+
+    def finish(self):
+        for copy in self.far:
+            copy.wait()
+        for copy in self.near:
+            copy.wait_send()
+        self.here.wait()
+
+
+def forward_kernel(x, grads, gains, cosine, sine, seg_col, seg_row, weights, qkv, context, log_totals, middle,
+                   normed_one, normed_all, grads_all, q_weight, o_weight, normed_two, load_sem, *sems):
+    z, c, f = place()
+    x_dev, y_dev = device(z, c, flipped(f, 1)), device(z, c, flipped(f, 2))
+    greet([x_dev, y_dev], [])
+    length = x.shape[0]
+    width = D + 2 * KW
+    of_grads = Exchange(grads, grads_all, sems, 0, x_dev, y_dev)
+    of_normed = Exchange(normed_two, normed_all, sems, 1, x_dev, y_dev)
+    of_grads.start()
+    load_q = pltpu.make_async_copy(weights.at[:, pl.ds(0, width)], q_weight, load_sem.at[0])
+    load_o = pltpu.make_async_copy(weights.at[:, pl.ds(width, D)], o_weight, load_sem.at[1])
+    load_q.start()
+    load_o.start()
+
+    def norm_one(r):
+        rows = x[r].astype(f32)
+        inverse = lax.rsqrt(jnp.mean(rows * rows, axis=-1, keepdims=True) + norm_eps)
+        normed_one[r] = (rows * inverse * gains[0:1, :]).astype(bf16)
+
+    by_rows(length, norm_one)
+    load_q.wait()
+    cos, sin = cosine[...], sine[...]
+
+    def project(i, carry):
+        lanes = tile_at(i, 256)
+        qkv[:, lanes] = rope_tile(dot_n(normed_one[...], q_weight[:, lanes]), cos, sin).astype(bf16)
+        return carry
+
+    lax.fori_loop(0, (D + KW) // 256, project, 0)
+    qkv[:, D + KW :] = dot_n(normed_one[...], q_weight[:, D + KW :]).astype(bf16)
+    allowed = mask_keys_rows(seg_col[...], seg_row[...], length)
+    attend_heads(qkv, context, log_totals, allowed)
+    load_o.wait()
+
+    def project_out(i, carry):
+        lanes = tile_at(i, 256)
+        middle[:, lanes] = x[:, lanes].astype(f32) + dot_n(context[...], o_weight[:, lanes])
+        return carry
+
+    lax.fori_loop(0, D // 256, project_out, 0)
+
+    def norm_two(r):
+        rows = middle[r]
+        inverse = lax.rsqrt(jnp.mean(rows * rows, axis=-1, keepdims=True) + norm_eps)
+        normed_two[r] = (rows * inverse * gains[1:2, :]).astype(bf16)
+
+    by_rows(length, norm_two)
+    of_normed.start()
+    of_grads.pass_on()
+    of_normed.pass_on()
+    of_normed.finish()
+    of_grads.finish()
+
+
+def forward(x, grads, gains, cosine, sine, seg_col, seg_row, weights):
+    length = x.shape[0]
+    dma = pltpu.SemaphoreType.DMA
+    vmem, hbm = pl.BlockSpec(memory_space=pltpu.VMEM), pl.BlockSpec(memory_space=pl.ANY)
+    width = D + 2 * KW
+    return pl.pallas_call(
+        forward_kernel,
+        out_shape=(
+            jax.ShapeDtypeStruct((length, width), bf16),
+            jax.ShapeDtypeStruct((length, D), bf16),
+            jax.ShapeDtypeStruct((HEADS, length), f32),
+            jax.ShapeDtypeStruct((length, D), f32),
+            jax.ShapeDtypeStruct((length, D), bf16),
+            jax.ShapeDtypeStruct((4, length, D), bf16),
+            jax.ShapeDtypeStruct((4, length, D), bf16),
+        ),
+        in_specs=[vmem, hbm] + [vmem] * 5 + [hbm],
+        out_specs=(vmem,) * 5 + (hbm,) * 2,
+        scratch_shapes=[
+            pltpu.VMEM((D, width), bf16), pltpu.VMEM((D, D), bf16), pltpu.VMEM((length, D), bf16),
+            dma((2,)), dma((2, 4)), dma((2, 4)), dma((2,)),
+        ],
+        compiler_params=pltpu.CompilerParams(
+            collective_id=5, has_side_effects=True, vmem_limit_bytes=vmem_limit
+        ),
+        cost_estimate=cost(95),
+        name="forward",
+    )(x, grads, gains, cosine, sine, seg_col, seg_row, weights)
+
+
+def feed_kernel(n_hbm, g_hbm, wm_hbm, wd_hbm, grad_normed, grad_down, grad_mlp, layer, n, g, wm, wd, gh, act,
+                parts, ones, twos, stage, load_sem, out_sem, one_send, one_recv, two_send, two_recv):
+    z, c, f = place()
+    x_dev, y_dev = device(z, c, flipped(f, 1)), device(z, c, flipped(f, 2))
+    tokens = n.shape[0]
+    length = tokens // 4
+    half = length // 2
+    ff = wd.shape[0]
+    loads = [
+        pltpu.make_async_copy(src, dst, load_sem.at[i])
+        for i, (src, dst) in enumerate(((n_hbm, n), (wm_hbm, wm), (wd_hbm, wd), (g_hbm, g)))
+    ]
+    for copy in loads:
+        copy.start()
+    greet([x_dev, y_dev], [])
+    for copy in loads:
+        copy.wait()
+
+    def hidden(rows, lanes, up_lanes):
+        gate = dot_n(n[rows, :], wm[:, lanes])
+        up = dot_n(n[rows, :], wm[:, up_lanes])
+        grad = dot_t(g[rows, :], wd[lanes, :])
+        sigmoid = jax.nn.sigmoid(gate)
+        silu = gate * sigmoid
+        act[rows, lanes] = (silu * up).astype(bf16)
+        gh[rows, lanes] = (grad * up * sigmoid * (1.0 + gate * (1.0 - sigmoid))).astype(bf16)
+        gh[rows, up_lanes] = (grad * silu).astype(bf16)
+
+    wide = ff // 256
+
+    def hidden_step(i, carry):
+        rows = pl.ds(pl.multiple_of((i % 4) * length, 16), length)
+        hidden(rows, tile_at(i // 4, 256), tile_at(i // 4, 256, ff))
+        return carry
+
+    lax.fori_loop(0, 4 * wide, hidden_step, 0)
+    for k in range(4):
+        if ff % 256:
+            hidden(pl.ds(k * length, length), pl.ds(wide * 256, ff % 256), pl.ds(ff + wide * 256, ff % 256))
+
+    def back(k, store):
+        def step(i, carry):
+            tile = tile_at(i, 1024)
+            store(tile, dot_t(gh[k * length : (k + 1) * length, :], wm[tile, :]))
+            return carry
+
+        lax.fori_loop(0, D // 1024, step, 0)
+
+    def back_parts(k):
+        def store(tile, value):
+            parts[k - 1, :, tile] = value.astype(bf16)
+
+        back(k, store)
+
+    halves = (pl.ds(0, half), pl.ds(half, half))
+    step_dev = (x_dev, y_dev)
+
+    def one(way, i):
+        return pltpu.make_async_remote_copy(
+            parts.at[2 if i else way, halves[way]], ones.at[way, i], one_send.at[way, i], one_recv.at[way, i],
+            device_id=step_dev[way], device_id_type=MESH,
+        )
+
+    def two(way):
+        return pltpu.make_async_remote_copy(
+            parts.at[1 - way, halves[way]], twos.at[way], two_send.at[way], two_recv.at[way],
+            device_id=step_dev[1 - way], device_id_type=MESH,
+        )
+
+    back_parts(3)
+    one(0, 1).start()
+    one(1, 1).start()
+    back_parts(1)
+    one(0, 0).start()
+    back_parts(2)
+    one(1, 0).start()
+
+    def store_own(tile, value):
+        grad_normed[:, tile] = value
+
+    back(0, store_own)
+
+    def down_out(i, slot, width=256):
+        rows = pl.ds(pl.multiple_of((i // 2) * 256, 128), width)
+        lanes = tile_at(i % 2, D // 2)
+        return pltpu.make_async_copy(
+            stage.at[slot, pl.ds(0, width), pl.ds(0, D // 2)], grad_down.at[rows, lanes], out_sem.at[0, slot]
+        )
+
+    def down_tile(i, slot, width=256):
+        lanes = tile_at(i % 2, D // 2)
+        value = dot_tn(act[:, pl.ds(pl.multiple_of((i // 2) * 256, 128), width)], g[:, lanes])
+        stage[slot, 0:width, 0 : D // 2] = value.astype(bf16)
+        down_out(i, slot, width).start()
+
+    def down_step(i, carry):
+        slot = i % 2
+
+        @pl.when(i >= 2)
+        def _():
+            down_out(i - 2, slot).wait()
+
+        down_tile(i, slot)
+        return carry
+
+    lax.fori_loop(0, 2 * wide, down_step, 0)
+    for slot in range(2):
+        down_out(2 * wide - 2 + slot, slot).wait()
+        if ff % 256:
+            down_tile(2 * wide + slot, slot, ff % 256)
+            down_out(2 * wide + slot, slot, ff % 256).wait()
+
+    for way in range(2):
+        one(way, 1).wait_recv()
+
+        def add_far(r):
+            there = pl.ds(pl.multiple_of(r.start + way * half, 16), r.size)
+            mine = parts[1 - way, there].astype(f32)
+            parts[1 - way, there] = (mine + ones[way, 1, r].astype(f32)).astype(bf16)
+
+        by_rows(half, add_far)
+        two(way).start()
+
+    def mlp_out(i, slot):
+        rows = pl.ds(pl.multiple_of((i // 2) * 256, 256), 256)
+        return pltpu.make_async_copy(
+            stage.at[slot, :, pl.ds(0, ff)], grad_mlp.at[rows, tile_at(i % 2, ff)], out_sem.at[1, slot]
+        )
+
+    def mlp_step(i, carry):
+        slot = i % 2
+
+        @pl.when(i >= 2)
+        def _():
+            mlp_out(i - 2, slot).wait()
+
+        value = dot_tn(n[:, tile_at(i // 2, 256)], gh[:, tile_at(i % 2, ff)])
+        stage[slot, :, 0:ff] = value.astype(bf16)
+        mlp_out(i, slot).start()
+        return carry
+
+    lax.fori_loop(0, 2 * D // 256, mlp_step, 0)
+    mlp_out(2 * D // 256 - 2, 0).wait()
+    mlp_out(2 * D // 256 - 1, 1).wait()
+
+    def layer_step(i, carry):
+        g[:, tile_at(i, 256)] = dot_n(act[...], wd[:, tile_at(i, 256)]).astype(bf16)
+        return carry
+
+    lax.fori_loop(0, D // 256, layer_step, 0)
+    layer_out = pltpu.make_async_copy(g, layer, load_sem.at[0])
+    layer_out.start()
+    for way in range(2):
+        one(way, 0).wait()
+        one(way, 1).wait_send()
+        two(way).wait()
+    for way in range(2):
+
+        def add_all(r):
+            there = pl.ds(pl.multiple_of(r.start + way * half, 16), r.size)
+            grad_normed[there] += ones[way, 0, r].astype(f32) + twos[way, r].astype(f32)
+
+        by_rows(half, add_all)
+    layer_out.wait()
+
+
+def feed(normed_all, grads_all, mlp_cols, down_cols):
+    tokens, ff = 4 * normed_all.shape[1], down_cols.shape[0]
+    length = tokens // 4
+    half = length // 2
+    dma = pltpu.SemaphoreType.DMA
+    vmem, hbm = pl.BlockSpec(memory_space=pltpu.VMEM), pl.BlockSpec(memory_space=pl.ANY)
+    return pl.pallas_call(
+        feed_kernel,
+        out_shape=(
+            jax.ShapeDtypeStruct((length, D), f32),
+            jax.ShapeDtypeStruct((ff, D), bf16),
+            jax.ShapeDtypeStruct((D, 2 * ff), bf16),
+            jax.ShapeDtypeStruct((tokens, D), bf16),
+        ),
+        in_specs=[hbm] * 4,
+        out_specs=(vmem, hbm, hbm, hbm),
+        scratch_shapes=[
+            pltpu.VMEM(shape, bf16)
+            for shape in (
+                (tokens, D), (tokens, D), (D, 2 * ff), (ff, D), (tokens, 2 * ff), (tokens, ff), (3, length, D),
+                (2, 2, half, D), (2, half, D), (2, 256, max(ff, D // 2)),
+            )
+        ]
+        + [dma((4,)), dma((2, 2)), dma((2, 2)), dma((2, 2)), dma((2,)), dma((2,))],
+        compiler_params=pltpu.CompilerParams(
+            collective_id=6, has_side_effects=True, vmem_limit_bytes=feed_vmem_limit
+        ),
+        cost_estimate=cost(115),
+        name="feed",
+    )(normed_all.reshape(tokens, D), grads_all.reshape(tokens, D), mlp_cols, down_cols)
+
+
 def local(
     n_dp,
     n_tp,
@@ -894,38 +1252,44 @@
     out_full = attn_full[:, D + 2 * KW : 2 * D + 2 * KW]
     gains_full = attn_full[:, 2 * D + 2 * KW :].astype(f32).T
     mlp_cols = lax.all_gather(mlp_parts.reshape(n_tp * rows, 2 * ff), "dp", axis=0, tiled=True)
-    grads_late, _ = lax.optimization_barrier((cotangent, attn_full))
-    grads_all = plane_gather(grads_late, n_tp)
-
     tokens_f = inputs.astype(f32)
     gain_one, gain_two = gains_full[0], gains_full[1]
     inverse_one = lax.rsqrt(jnp.mean(tokens_f * tokens_f, axis=-1, keepdims=True) + norm_eps)
-    normed_one = (tokens_f * inverse_one * gain_one).astype(bf16)
-    projected = matmul(normed_one, qkv_full)
-    qkv, attended, log_totals = attend(projected, cosine, sine, seg_col, seg_row)
-    middle = tokens_f + matmul(attended, out_full)
+    if n_tp == 4:
+        qkv, attended, log_totals, middle, normed_one, normed_all, grads_all = forward(
+            inputs, cotangent, gains_full, cosine, sine, seg_col, seg_row, attn_full
+        )
+    else:
+        normed_one = (tokens_f * inverse_one * gain_one).astype(bf16)
+        projected = matmul(normed_one, qkv_full)
+        qkv, attended, log_totals = attend(projected, cosine, sine, seg_col, seg_row)
+        middle = tokens_f + matmul(attended, out_full)
     inverse_two = lax.rsqrt(jnp.mean(middle * middle, axis=-1, keepdims=True) + norm_eps)
-    normed_two = (middle * inverse_two * gain_two).astype(bf16)
-
-    normed_all = plane_gather(normed_two, n_tp)
-    hidden = matmul(normed_all, mlp_cols)
-    gate, up_part = hidden[:, :ff], hidden[:, ff:]
-    sigmoid_gate = jax.nn.sigmoid(gate)
-    silu_gate = gate * sigmoid_gate
-    activated = (silu_gate * up_part).astype(bf16)
-    grad_act = matmul_t(grads_all, down_cols)
-    grad_gate = grad_act * up_part * sigmoid_gate * (1.0 + gate * (1.0 - sigmoid_gate))
-    grad_up = grad_act * silu_gate
-    grad_hidden = jnp.concatenate([grad_gate, grad_up], axis=1).astype(bf16)
-    grad_normed = matmul_t(grad_hidden, mlp_cols).reshape(n_tp, length, D)
-    grad_normed_two = grad_normed[0]
-    for k in range(1, n_tp):
-        grad_normed_two = grad_normed_two + plane_swap(grad_normed[k].astype(bf16), k, n_tp).astype(f32)
-    grad_down = matmul_tn(activated, grads_all).astype(bf16)
-    grad_mlp = matmul_tn(normed_all, grad_hidden).astype(bf16)
-    layer_parts = matmul(activated, down_cols).astype(bf16).reshape(n_tp, length, D)
-    layer_parts, _ = lax.optimization_barrier((layer_parts, grad_normed_two))
-    layer_out = middle + layer_parts[0]
+    if n_tp == 4:
+        grad_normed_two, grad_down, grad_mlp, layer_parts = feed(normed_all, grads_all, mlp_cols, down_cols)
+        layer_parts = layer_parts.reshape(n_tp, length, D)
+    else:
+        normed_two = (middle * inverse_two * gain_two).astype(bf16)
+        normed_all = plane_gather(normed_two, n_tp)
+        grads_all = plane_gather(cotangent, n_tp)
+        hidden = matmul(normed_all, mlp_cols)
+        gate, up_part = hidden[:, :ff], hidden[:, ff:]
+        sigmoid_gate = jax.nn.sigmoid(gate)
+        silu_gate = gate * sigmoid_gate
+        activated = (silu_gate * up_part).astype(bf16)
+        grad_act = matmul_t(grads_all, down_cols)
+        grad_gate = grad_act * up_part * sigmoid_gate * (1.0 + gate * (1.0 - sigmoid_gate))
+        grad_up = grad_act * silu_gate
+        grad_hidden = jnp.concatenate([grad_gate, grad_up], axis=1).astype(bf16)
+        grad_normed = matmul_t(grad_hidden, mlp_cols).reshape(n_tp, length, D)
+        grad_normed_two = grad_normed[0]
+        for k in range(1, n_tp):
+            swapped = plane_swap(grad_normed[k].astype(bf16), k, n_tp)
+            grad_normed_two = grad_normed_two + swapped.astype(f32)
+        grad_down = matmul_tn(activated, grads_all).astype(bf16)
+        grad_mlp = matmul_tn(normed_all, grad_hidden).astype(bf16)
+        layer_parts = matmul(activated, down_cols).astype(bf16).reshape(n_tp, length, D)
+    layer_out = middle + layer_parts[0].astype(f32)
     for k in range(1, n_tp):
         layer_out = layer_out + plane_swap(layer_parts[k], k, n_tp).astype(f32)
     layer_out = layer_out.astype(bf16)

time: 813 us -> 700 us (0.86)
  Pallas kernels: 304 us -> 511 us
  waiting for transfers between devices: 212 us -> 61.2 us
  matrix products: 179 us -> 33.6 us
  starting transfers between devices: 15.3 us -> 3.61 us
  local copies, waits for them, and re-layouts: 23.2 us -> 15 us
    pallas_call x1 -> x2, Pallas kernels: 18 us -> 225 us  [the longest x1 117 us: feed(): pl.pallas_call(feed_kernel, out_shape=(jax.ShapeDtypeStruct((length, D),...]
    ppermute x14 -> x3, waiting for transfers between devices: 212 us -> 60.5 us  [plane_swap(): return lax.ppermute(block, 'fsdp', [(i, i ^ k) for i in range(n_tp)])]
    dot_general x4 -> x0, matrix products: 57.2 us -> none  [matmul(): return jnp.dot(a, b, preferred_element_type=f32)]
    dot_general x4 -> x2, matrix products: 68.1 us -> 18.9 us  [matmul_t(): lax.dot_general(a, b, (((1,), (1,)), ((), ())), preferred_element_type=f32)]
    dot_general x4 -> x2, matrix products: 54.2 us -> 14.7 us  [matmul_tn(): lax.dot_general(a, b, (((0,), (0,)), ((), ())), preferred_element_type=f32)]
    ppermute x14 -> x3, starting transfers between devices: 15.2 us -> 3.49 us  [plane_swap(): return lax.ppermute(block, 'fsdp', [(i, i ^ k) for i in range(n_tp)])]
  transfers between devices with their start and end apart: 17 -> 6, of which waited for: 9 -> 3; matrix products, arithmetic and copies ran while one was open for 20% -> 10% of each run, Pallas kernels for 21% -> 37%
where the time goes in v3:
time: 700 us; the launch traced here: 696 us
  Pallas kernels  511 us (73%)
  waiting for transfers between devices  61.2 us (9%)
  other arithmetic  52.2 us (7%)
  matrix products  33.6 us (5%)
  between operations  20.1 us (3%)
  local copies, waits for them, and re-layouts  15 us (2%)
    pallas_call x1, Pallas kernels, scatter_all(): pl.pallas_call(functools.partial(scatter_kernel, lines, n), out_shape=[ja...  121 us
    pallas_call x1, Pallas kernels, feed(): pl.pallas_call(feed_kernel, out_shape=(jax.ShapeDtypeStruct((length, D),...  117 us
    pallas_call x1, Pallas kernels, forward(): pl.pallas_call(forward_kernel, out_shape=(jax.ShapeDtypeStruct((length, w...  109 us
    pallas_call x1, Pallas kernels, gather_all(): pl.pallas_call(functools.partial(gather_kernel, lines), out_shape=(jax.Sh...  103 us
    ppermute x3, waiting for transfers between devices, plane_swap(): return lax.ppermute(block, 'fsdp', [(i, i ^ k) for i in range(n_tp)])  60.5 us
    pallas_call x1, Pallas kernels, attend_grad(): pl.pallas_call(attend_grad_kernel, out_shape=jax.ShapeDtypeStruct((length...  26.1 us
    pallas_call x1, Pallas kernels, columns_back(): pl.pallas_call(functools.partial(columns_back_kernel, n_dp, n_tp), out_sh...  21.1 us
    dot_general x2, matrix products, matmul_t(): lax.dot_general(a, b, (((1,), (1,)), ((), ())), preferred_element_type=f32)  18.9 us
  transfers between devices with their start and end apart: 6, of which 3 were waited for; matrix products, arithmetic and copies ran while one was open for 10% of the time, Pallas kernels for 37%

profile of v3, /device:TPU:0, one launch (start us, length us, event | category | flops | bytes accessed | tf_op | source)
XLA Modules:
  0.0 696.3 jit_solution(15651487740381113980)
XLA Ops:
  7.2 0.7 convert.25
  8.0 1.1 convert.24
  9.1 1.1 convert.23
  10.2 1.5 convert_element_type.56.down
  11.8 103.3 %gather_all.1 = (bf16[4,2,4,64,4736]{4,3,2,1,0:T(8,128)(2,1)}, bf16[4,64,2816]{2,1,0:T(8,128)(2,1)}, bf16[4,2,176,2048]{3,2,1,0:T(8,128)(2,1)}) custom-call(bf16[64,4736]{1,0:T(8,128)(2,1)S(1)} %fusion.25.own, f32[64,11264]{1,0:T(8,128)} %weight.1, bf16[176,2048]{1,0:T(8,128)(2,1)S(1)} %convert_element_type.56.down), custom_call_target="tpu_custom_call" | custom-call | bytes 369000000 | tf_op jit(solution)/shard_map/gather_all/pallas_call | solution.py:440
  117.0 1.1 convert_bitcast_fusion
  118.6 0.8 fusion.27
  119.8 109.0 %forward.1 = (bf16[384,2560]{1,0:T(8,128)(2,1)}, bf16[384,2048]{1,0:T(8,128)(2,1)S(1)}, f32[32,384]{1,0:T(8,128)S(1)}, f32[384,2048]{1,0:T(8,128)}, bf16[384,204...) custom-call(bf16[384,2048]{1,0:T(8,128)(2,1)} %x.5, bf16[384,2048]{1,0:T(8,128)(2,1)} %grads.1, ...), custom_call_target="tpu_custom_call" | custom-call | bytes 350550016 | tf_op jit(solution)/shard_map/forward/pallas_call | solution.py:993
  228.8 1.1 copy-done.2
  229.9 116.5 %feed.1 = (f32[384,2048]{1,0:T(8,128)}, bf16[1408,2048]{1,0:T(8,128)(2,1)}, bf16[2048,2816]{1,0:T(8,128)(2,1)}, bf16[1536,2048]{1,0:T(8,128)(2,1)}) custom-call(bf16[1536,2048]{1,0:T(8,128)(2,1)} %bitcast.47, bf16[1536,2048]{1,0:T(8,128)(2,1)} %bitcast.48, bf16[2048,2816]{1,0:T(8,128)(2,1)} %all-gather.2.cloned.1.call-done.wm_hbm, bf16[1408,2048]{1,0:T(8,128)(2,1)} %bitcast.49), custom_call_target="tpu_custom_call" | custom-call | bytes 424350016 | tf_op jit(solution)/shard_map/feed/pallas_call | solution.py:1190
  346.5 0.7 reduce-scatter.3.cloned.1.call-update
  347.3 4.7 fusion.39
  352.0 1.5 collective-permute-start
  353.5 1.5 collective-permute-start.2
  355.5 0.9 slice_reduce_fusion
  356.7 1.9 fusion.6
  358.6 2.2 multiply_reduce_fusion.2
  360.9 3.0 multiply_reduce_fusion
  363.9 25.7 %collective-permute-done = bf16[384,2048]{1,0:T(8,128)(2,1)} collective-permute-done((bf16[384,2048]{1,0:T(8,128)(2,1)}, bf16[384,2048]{1,0:T(8,128)(2,1)}, u32[]{:S(2)}, u32[]{:S(2)}) %collective-permute-start) | collective-permute-done | bytes 1572896 | tf_op jit(solution)/shard_map/ppermute | solution.py:618
  389.6 33.5 %collective-permute-done.2 = bf16[384,2048]{1,0:T(8,128)(2,1)} collective-permute-done((bf16[384,2048]{1,0:T(8,128)(2,1)}, bf16[384,2048]{1,0:T(8,128)(2,1)}, u32[]{:S(2)}, u32[]{:S(2)}) %collective-permute-start.2) | collective-permute-done | bytes 1572896 | tf_op jit(solution)/shard_map/ppermute | solution.py:618
  423.1 1.4 collective-permute-done.1
  424.4 5.5 multiply_subtract_fusion
  430.0 8.0 %fusion.14.grad_context = bf16[384,2048]{1,0:T(8,128)(2,1)S(1)} fusion(bf16[2048,4736]{1,0:T(8,128)(2,1)} %bitcast.44, f32[384,2048]{1,0:T(8,128)S(1)} %get-tuple-element.147), kind=kOutput, calls=%fused_computation.30 | convolution fusion | flops 3222798336 | bytes 13107200 | tf_op jit(solution)/shard_map/dot_general | solution.py:606
  438.0 26.1 %attend_grad.1 = bf16[384,2560]{1,0:T(8,128)(2,1)} custom-call(bf16[384,2560]{1,0:T(8,128)(2,1)} %get-tuple-element.42.qkv, bf16[384,2048]{1,0:T(8,128)(2,1)S(1)} %fusion.14.grad_context, f32[32,384]{1,0:T(8,128)S(1)} %get-tuple-element.43.log_totals, f32[384,128]{1,0:T(8,128)S(1)} %get-tuple-element.159.cosine, f32[384,128]{1,0:T(8,128)S(1)} %get-tuple-element.160.sine, ...), custom_call_target="tpu_custom_call" | custom-call | bytes 95940000 | tf_op jit(solution)/shard_map/attend_grad/pallas_call | solution.py:194
  464.1 10.9 %fusion.12 = (bf16[2048]{0:T(1024)(128)(2,1)S(1)}, f32[384]{0:T(512)S(1)}, f32[384,2048]{1,0:T(8,128)}) fusion(bf16[384,2048]{1,0:T(8,128)(2,1)S(1)} %copy-done.6, f32[384]{0:T(512)S(1)} %get-tuple-element.155, f32[2048]{0:T(1024)S(1)} %get-tuple-element.126, bf16[384,2560]{1,0:T(8,128)(2,1)} %attend_grad.1, bf16[2048,4736]{1,0:T(8,128)(2,1)} %bitcast.45), kind=kOutput, calls=%fused_computation.20 | convolution fusion | flops 4032034304 | bytes 17185792 | tf_op jit(solution)/shard_map/dot_general | solution.py:606
  475.4 8.8 %convolution_convert_fusion.1 = bf16[2048,2048]{1,0:T(8,128)(2,1)} fusion(bf16[384,2048]{1,0:T(8,128)(2,1)S(1)} %copy-done.3, f32[384,2048]{1,0:T(8,128)} %copy-done.9), kind=kOutput, calls=%fused_computation.8 | convolution fusion | flops 3226206208 | bytes 13107200 | tf_op jit(solution)/shard_map/dot_general | solution.py:610
  484.2 5.9 convolution_convert_fusion
  490.2 4.7 fusion.1
  494.9 120.5 %scatter_all.1 = (f32[64,2048]{1,0:T(8,128)S(1)}, f32[64,2688]{1,0:T(8,128)S(1)}) custom-call(bf16[4,2,4,64,2048]{4,3,2,1,0:T(8,128)(2,1)} %bitcast.46, bf16[4,2,4,64,2688]{4,3,2,1,0:T(8,128)(2,1)} %bitcast.41), custom_call_target="tpu_custom_call" | custom-call | bytes 405900000 | tf_op jit(solution)/shard_map/scatter_all/pallas_call | solution.py:842
  615.4 0.7 multiply_reduce_fusion.5
  616.1 0.8 multiply_reduce_fusion.4
  618.2 0.6 multiply_reduce_fusion.6
  618.8 4.9 fusion.9
  623.7 2.1 fusion.19
  625.8 1.4 copy-done
  627.1 21.1 %columns_back.1 = f32[64,11264]{1,0:T(8,128)} custom-call(bf16[4,64,2816]{2,1,0:T(8,128)(2,1)S(1)} %bitcast.39), custom_call_target="tpu_custom_call" | custom-call | bytes 73800000 | tf_op jit(solution)/shard_map/columns_back/pallas_call | solution.py:542
  648.3 3.3 multiply_reduce_fusion.3
  653.5 0.6 broadcast_in_dim.7.value
  654.1 14.1 %total.1 = f32[8,128]{1,0:T(8,128)} custom-call(f32[8,128]{1,0:T(8,128)} %broadcast_in_dim.7.value), custom_call_target="tpu_custom_call" | custom-call | bytes 47970000 | tf_op jit(solution)/shard_map/total/pallas_call | solution.py:579
  668.2 1.2 slice.73
  670.2 0.6 copy.103
  670.9 0.6 copy.102
  671.7 0.6 copy.101
  672.3 2.7 multiply_subtract_fusion.4
  675.1 1.6 multiply_subtract_fusion.3
  676.7 0.9 copy-done.5
  677.6 8.0 %multiply_subtract_fusion.1 = (f32[64,11264]{1,0:T(8,128)}, f32[64,11264]{1,0:T(8,128)}, f32[64,11264]{1,0:T(8,128)}) fusion(f32[64,11264]{1,0:T(8,128)S(1)} %copy-done.10, f32[64,11264]{1,0:T(8,128)S(1)} %copy-done.5, f32[]{:T(128)S(6)} %div.102, f32[64,11264]{1,0:T(8,128)} %param.28, f32[64,11264]{1,0:T(8,128)} %param.33), kind=kLoop, calls=%fused_computation.27 | loop fusion | flops 11534336 | bytes 20185092 | tf_op jit(solution)/shard_map/sub | solution.py:597
  685.6 2.8 multiply_subtract_fusion.2
  (90 shorter events, 4.0 us)
Async XLA Ops:
  7.2 222.7 %all-gather.2.cloned.1.call-start = ((), (), s32[]{:S(2)}) async-start(), calls=%async_computation.2 | async-start | bytes 12976128 | tf_op jit(solution)/shard_map/all_gather | solution.py:1254
  11.8 103.4 %copy-start.1 = (s32[1,384]{1,0:T(1,128)S(1)}, s32[1,384]{1,0:T(1,128)}, u32[]{:S(2)}) copy-start(s32[1,384]{1,0:T(1,128)} %seg_row.3) | copy-start | bytes 4612
  115.1 508.6 %reduce-scatter.5.cloned.1.call-start = ((), (), s32[]{:S(2)}) async-start(), calls=%async_computation.4 | async-start | bytes 6488064 | tf_op jit(solution)/shard_map/reduce_scatter | solution.py:1297
  228.8 1.1 copy-start.2
  346.5 279.3 %reduce-scatter.3.cloned.1.call-start = ((), (), s32[]{:S(2)}) async-start(), calls=%async_computation.3 | async-start | bytes 12976128 | tf_op jit(solution)/shard_map/reduce_scatter | solution.py:1298
  346.5 0.7 copy-start.22
  346.5 0.7 copy-start.23
  347.2 9.1 %copy-start.21 = (f32[2,64]{1,0:T(2,128)S(1)}, f32[2,64]{1,0:T(2,128)}, u32[]{:S(2)}) copy-start(f32[2,64]{1,0:T(2,128)} %param.25) | copy-start | bytes 1540
  352.0 37.6 %collective-permute-start = (bf16[384,2048]{1,0:T(8,128)(2,1)}, bf16[384,2048]{1,0:T(8,128)(2,1)}, u32[]{:S(2)}, u32[]{:S(2)}) collective-permute-start(bf16[384,2048]{1,0:T(8,128)(2,1)} %get-tuple-element.144), channel_id=1, source_target_pairs={{0,1},{1,0},{2,3},{3,2},{4,5},{5,4},{6,7},{7,6},{8,9},{9,8},{10,11... | collective-permute-start | bytes 4718600 | tf_op jit(solution)/shard_map/ppermute | solution.py:618
  353.5 69.6 %collective-permute-start.2 = (bf16[384,2048]{1,0:T(8,128)(2,1)}, bf16[384,2048]{1,0:T(8,128)(2,1)}, u32[]{:S(2)}, u32[]{:S(2)}) collective-permute-start(bf16[384,2048]{1,0:T(8,128)(2,1)} %get-tuple-element.145), channel_id=1, source_target_pairs={{0,3},{1,2},{2,1},{3,0},{4,7},{5,6},{6,5},{7,4},{8,11},{9,10},{10,... | collective-permute-start | bytes 4718600 | tf_op jit(solution)/shard_map/ppermute | solution.py:618
  354.9 69.5 %collective-permute-start.1 = (bf16[384,2048]{1,0:T(8,128)(2,1)}, bf16[384,2048]{1,0:T(8,128)(2,1)}, u32[]{:S(2)}, u32[]{:S(2)}) collective-permute-start(bf16[384,2048]{1,0:T(8,128)(2,1)} %get-tuple-element.146), channel_id=1, source_target_pairs={{0,2},{1,3},{2,0},{3,1},{4,6},{5,7},{6,4},{7,5},{8,10},{9,11},{10,... | collective-permute-start | bytes 4718600 | tf_op jit(solution)/shard_map/ppermute | solution.py:618
  356.7 4.2 copy-start.4
  360.9 63.5 %copy-start.8 = (f32[384,2048]{1,0:T(8,128)S(1)}, f32[384,2048]{1,0:T(8,128)}, u32[]{:S(2)}) copy-start(f32[384,2048]{1,0:T(8,128)} %get-tuple-element.41) | copy-start | bytes 9437188
  360.9 63.5 %copy-start.11 = (bf16[384,2048]{1,0:T(8,128)(2,1)S(1)}, bf16[384,2048]{1,0:T(8,128)(2,1)}, u32[]{:S(2)}) copy-start(bf16[384,2048]{1,0:T(8,128)(2,1)} %grads.1) | copy-start | bytes 4718596
  430.0 8.0 %copy-start.9 = (f32[384,2048]{1,0:T(8,128)}, f32[384,2048]{1,0:T(8,128)S(1)}, u32[]{:S(2)}) copy-start(f32[384,2048]{1,0:T(8,128)S(1)} %get-tuple-element.147) | copy-start | bytes 9437188
  438.0 26.1 %copy-start.6 = (bf16[384,2048]{1,0:T(8,128)(2,1)S(1)}, bf16[384,2048]{1,0:T(8,128)(2,1)}, u32[]{:S(2)}) copy-start(bf16[384,2048]{1,0:T(8,128)(2,1)} %x.5) | copy-start | bytes 4718596
  464.1 11.3 %copy-start.3 = (bf16[384,2048]{1,0:T(8,128)(2,1)S(1)}, bf16[384,2048]{1,0:T(8,128)(2,1)}, u32[]{:S(2)}) copy-start(bf16[384,2048]{1,0:T(8,128)(2,1)} %copy-done.2) | copy-start | bytes 4718596
  475.4 8.8 %copy-start.16 = (bf16[384,2560]{1,0:T(8,128)(2,1)S(1)}, bf16[384,2560]{1,0:T(8,128)(2,1)}, u32[]{:S(2)}) copy-start(bf16[384,2560]{1,0:T(8,128)(2,1)} %attend_grad.1) | copy-start | bytes 5898244
  475.4 8.8 %copy-start.24 = (bf16[384,2048]{1,0:T(8,128)(2,1)S(1)}, bf16[384,2048]{1,0:T(8,128)(2,1)}, u32[]{:S(2)}) copy-start(bf16[384,2048]{1,0:T(8,128)(2,1)} %get-tuple-element.45) | copy-start | bytes 4718596
  494.9 123.9 %copy-start.7 = (bf16[384,2048]{1,0:T(8,128)(2,1)S(1)}, bf16[384,2048]{1,0:T(8,128)(2,1)}, u32[]{:S(2)}) copy-start(bf16[384,2048]{1,0:T(8,128)(2,1)} %x.5) | copy-start | bytes 4718596
  625.8 1.4 copy-start
  627.1 45.2 %copy-start.15 = (f32[64,2048]{1,0:T(8,128)S(1)}, f32[64,2048]{1,0:T(8,128)}, u32[]{:S(2)}) copy-start(f32[64,2048]{1,0:T(8,128)} %param.22) | copy-start | bytes 1572868
  648.2 26.8 %copy-start.14 = (f32[64,2560]{1,0:T(8,128)S(1)}, f32[64,2560]{1,0:T(8,128)}, u32[]{:S(2)}) copy-start(f32[64,2560]{1,0:T(8,128)} %param.21) | copy-start | bytes 1966084
  648.2 26.8 %copy-start.19 = (f32[64,2560]{1,0:T(8,128)S(1)}, f32[64,2560]{1,0:T(8,128)}, u32[]{:S(2)}) copy-start(f32[64,2560]{1,0:T(8,128)} %param.26) | copy-start | bytes 1966084
  672.3 2.8 copy-start.20
  672.3 4.4 copy-start.10
  675.1 2.5 copy-start.5
  677.6 8.0 %copy-start.12 = (f32[176,2048]{1,0:T(8,128)S(1)}, f32[176,2048]{1,0:T(8,128)}, u32[]{:S(2)}) copy-start(f32[176,2048]{1,0:T(8,128)} %param.24) | copy-start | bytes 4325380
  677.6 8.0 %copy-start.13 = (bf16[176,2048]{1,0:T(8,128)(2,1)S(1)}, bf16[176,2048]{1,0:T(8,128)(2,1)}, u32[]{:S(2)}) copy-start(bf16[176,2048]{1,0:T(8,128)(2,1)} %reduce-scatter.5.cloned.1.call-done) | copy-start | bytes 2162692
  677.6 8.0 %copy-start.17 = (f32[176,2048]{1,0:T(8,128)S(1)}, f32[176,2048]{1,0:T(8,128)}, u32[]{:S(2)}) copy-start(f32[176,2048]{1,0:T(8,128)} %param.29) | copy-start | bytes 4325380
  677.6 8.0 %copy-start.18 = (f32[176,2048]{1,0:T(8,128)S(1)}, f32[176,2048]{1,0:T(8,128)}, u32[]{:S(2)}) copy-start(f32[176,2048]{1,0:T(8,128)} %param.34) | copy-start | bytes 4325380
Sparse Core Ops, SparseCore 0:
  115.2 108.4 all-gather.1
  346.6 65.1 reduce-scatter.4
  414.1 117.6 reduce-scatter.2

commit v4 on v3

--- a/solution.py
+++ b/solution.py
@@ -82,92 +82,18 @@
 
 
 def attend_kernel(proj, cosine, sine, seg_col, seg_row, qkv, context, log_totals):
-    length = proj.shape[0]
     cos, sin = cosine[...], sine[...]
     for c in range(0, D + KW, 128):
-        pair = proj[:, c : c + 128]
-        qkv[:, c : c + 128] = (pair * cos + halves_swapped(pair) * sin).astype(bf16)
+        qkv[:, c : c + 128] = rope_tile(proj[:, c : c + 128], cos, sin).astype(bf16)
     for c in range(D + KW, D + 2 * KW, 128):
         qkv[:, c : c + 128] = proj[:, c : c + 128].astype(bf16)
-    allowed = mask_keys_rows(seg_col[...], seg_row[...], length)
-    scale = HD ** (-0.5)
-    for group in range(KVH):
-        kc = D + (group // 2) * 128
-        keys = both_places(qkv[:, kc : kc + 128], group % 2)
-        values = both_places(qkv[:, kc + KW : kc + KW + 128], group % 2)
-
-        def pair_step(pair_index, carry):
-            pair = group * (GROUP // 2) + pair_index
-            lanes = pl.ds(pl.multiple_of(pair * 128, 128), 128)
-            queries = qkv[:, lanes]
-            total = jnp.zeros((length, 128), f32)
-            for side in range(2):
-                scores = dot_t(keys[side], queries) * scale
-                scores = jnp.where(allowed, scores, -1e30)
-                top = jnp.max(scores, axis=0, keepdims=True)
-                raised = jnp.exp(scores - top)
-                totals = jnp.sum(raised, axis=0, keepdims=True)
-                probs = (raised / totals).astype(bf16)
-                total = total + dot_tn(probs, values[side])
-                log_totals[pl.ds(2 * pair + side, 1), :] = top + jnp.log(totals)
-            context[:, lanes] = total.astype(bf16)
-            return carry
-
-        lax.fori_loop(0, GROUP // 2, pair_step, 0)
+    allowed = mask_keys_rows(seg_col[...], seg_row[...], proj.shape[0])
+    attend_heads(qkv, context, log_totals, allowed)
 
 
 def attend_grad_kernel(qkv, grad_context, log_totals, cosine, sine, seg_col, seg_row, grad_proj):
-    length = qkv.shape[0]
-    cos, sin = cosine[...], sine[...]
-    allowed = mask_keys_rows(seg_col[...], seg_row[...], length)
-    scale = HD ** (-0.5)
-
-    def unrotate(pair):
-        return pair * cos + halves_swapped(pair * sin)
-
-    key_parts, value_parts = [], []
-    for group in range(KVH):
-        kc = D + (group // 2) * 128
-        keys = both_places(qkv[:, kc : kc + 128], group % 2)
-        values = both_places(qkv[:, kc + KW : kc + KW + 128], group % 2)
-
-        def pair_step(pair_index, carry):
-            grad_keys, grad_values = list(carry[:2]), list(carry[2:])
-            pair = group * (GROUP // 2) + pair_index
-            lanes = pl.ds(pl.multiple_of(pair * 128, 128), 128)
-            queries = qkv[:, lanes]
-            grads = grad_context[:, lanes]
-            total = jnp.zeros((length, 128), f32)
-            for side in range(2):
-                scores = dot_t(keys[side], queries) * scale
-                scores = jnp.where(allowed, scores, -1e30)
-                probs = jnp.exp(scores - log_totals[pl.ds(2 * pair + side, 1), :])
-                grad_probs = dot_t(values[side], grads)
-                grad_values[side] = grad_values[side] + dot_n(probs.astype(bf16), grads)
-                inner = jnp.sum(probs * grad_probs, axis=0, keepdims=True)
-                raw = (probs * (grad_probs - inner) * scale).astype(bf16)
-                total = total + dot_tn(raw, keys[side])
-                grad_keys[side] = grad_keys[side] + dot_n(raw, queries)
-            grad_proj[:, lanes] = unrotate(total).astype(bf16)
-            return (*grad_keys, *grad_values)
-
-        empty = jnp.zeros((length, 128), f32)
-        out = lax.fori_loop(0, GROUP // 2, pair_step, (empty,) * 4)
-
-        def joined(low_side, high_side):
-            low, _ = split_pair(low_side)
-            _, high = split_pair(high_side)
-            both = low + high
-            return both + pltpu.roll(both, HD, 1)
-
-        key_parts.append(joined(out[0], out[1]))
-        value_parts.append(joined(out[2], out[3]))
-    lane = lax.broadcasted_iota(jnp.int32, (length, 128), 1)
-    for c in range(KVH // 2):
-        keys = jnp.where(lane < HD, key_parts[2 * c], key_parts[2 * c + 1])
-        values = jnp.where(lane < HD, value_parts[2 * c], value_parts[2 * c + 1])
-        grad_proj[:, D + c * 128 : D + (c + 1) * 128] = unrotate(keys).astype(bf16)
-        grad_proj[:, D + KW + c * 128 : D + KW + (c + 1) * 128] = values.astype(bf16)
+    allowed = mask_keys_rows(seg_col[...], seg_row[...], qkv.shape[0])
+    attend_heads_grad(qkv, grad_context, log_totals, grad_proj, allowed, cosine[...], sine[...])
 
 
 vmem_limit = 50 * 1024 * 1024
@@ -586,7 +512,7 @@
         cost_estimate=cost(13),
         name="total",
     )(jnp.broadcast_to(value, tile))
-    return spread[0, 0]
+    return spread
 
 
 def adam_update(weight, gradient, first, second, rate, decay):
@@ -1015,13 +941,398 @@
     )(x, grads, gains, cosine, sine, seg_col, seg_row, weights)
 
 
+class PlaneSum:
+    def __init__(self, parts, ones, twos, sems, x_dev, y_dev):
+        one_send, one_recv, two_send, two_recv = sems
+        self.half = parts.shape[1] // 2
+        self.parts, self.ones, self.twos = parts, ones, twos
+        halves = (pl.ds(0, self.half), pl.ds(self.half, self.half))
+        step_dev = (x_dev, y_dev)
+
+        def remote(src, dst, send, recv, dev):
+            return pltpu.make_async_remote_copy(src, dst, send, recv, device_id=dev, device_id_type=MESH)
+
+        self.near, self.far, self.two = [], [], []
+        for way in range(2):
+            for i, copies in enumerate((self.near, self.far)):
+                block = parts.at[2 if i else way, halves[way]]
+                copies.append(
+                    remote(block, ones.at[way, i], one_send.at[way, i], one_recv.at[way, i], step_dev[way])
+                )
+            self.two.append(
+                remote(parts.at[1 - way, halves[way]], twos.at[way], two_send.at[way], two_recv.at[way], step_dev[1 - way])
+            )
+
+    def there(self, r, way):
+        return pl.ds(pl.multiple_of(r.start + way * self.half, 16), r.size)
+
+    def pass_on(self):
+        for way in range(2):
+            self.far[way].wait_recv()
+
+            def add_far(r):
+                there = self.there(r, way)
+                mine = self.parts[1 - way, there].astype(f32)
+                self.parts[1 - way, there] = (mine + self.ones[way, 1, r].astype(f32)).astype(bf16)
+
+            by_rows(self.half, add_far)
+            self.two[way].start()
+
+    def finish(self, add):
+        for way in range(2):
+            self.near[way].wait()
+            self.far[way].wait_send()
+            self.two[way].wait()
+        for way in range(2):
+
+            def add_all(r):
+                add(self.there(r, way), self.ones[way, 0, r].astype(f32) + self.twos[way, r].astype(f32))
+
+            by_rows(self.half, add_all)
+
+
+def plane_sum_scratch(length, columns):
+    dma = pltpu.SemaphoreType.DMA
+    shapes = ((3, length, columns), (2, 2, length // 2, columns), (2, length // 2, columns))
+    return [pltpu.VMEM(shape, bf16) for shape in shapes], [dma((2, 2)), dma((2, 2)), dma((2,)), dma((2,))]
+
+
+def attend_heads_grad(qkv, grad_context, log_totals, grad_proj, allowed, cos, sin):
+    length = qkv.shape[0]
+    scale = HD ** (-0.5)
+
+    def unrotate(pair):
+        return pair * cos + halves_swapped(pair * sin)
+
+    key_parts, value_parts = [], []
+    for group in range(KVH):
+        kc = D + (group // 2) * 128
+        keys = both_places(qkv[:, kc : kc + 128], group % 2)
+        values = both_places(qkv[:, kc + KW : kc + KW + 128], group % 2)
+
+        def pair_step(pair_index, carry):
+            grad_keys, grad_values = list(carry[:2]), list(carry[2:])
+            pair = group * (GROUP // 2) + pair_index
+            lanes = pl.ds(pl.multiple_of(pair * 128, 128), 128)
+            queries = qkv[:, lanes]
+            grads = grad_context[:, lanes]
+            total = jnp.zeros((length, 128), f32)
+            for side in range(2):
+                scores = dot_t(keys[side], queries) * scale
+                scores = jnp.where(allowed, scores, -1e30)
+                probs = jnp.exp(scores - log_totals[pl.ds(2 * pair + side, 1), :])
+                grad_probs = dot_t(values[side], grads)
+                grad_values[side] = grad_values[side] + dot_n(probs.astype(bf16), grads)
+                inner = jnp.sum(probs * grad_probs, axis=0, keepdims=True)
+                raw = (probs * (grad_probs - inner) * scale).astype(bf16)
+                total = total + dot_tn(raw, keys[side])
+                grad_keys[side] = grad_keys[side] + dot_n(raw, queries)
+            grad_proj[:, lanes] = unrotate(total).astype(bf16)
+            return (*grad_keys, *grad_values)
+
+        empty = jnp.zeros((length, 128), f32)
+        out = lax.fori_loop(0, GROUP // 2, pair_step, (empty,) * 4)
+
+        def joined(low_side, high_side):
+            low, _ = split_pair(low_side)
+            _, high = split_pair(high_side)
+            both = low + high
+            return both + pltpu.roll(both, HD, 1)
+
+        key_parts.append(joined(out[0], out[1]))
+        value_parts.append(joined(out[2], out[3]))
+    lane = lax.broadcasted_iota(jnp.int32, (length, 128), 1)
+    for c in range(KVH // 2):
+        keys = jnp.where(lane < HD, key_parts[2 * c], key_parts[2 * c + 1])
+        values = jnp.where(lane < HD, value_parts[2 * c], value_parts[2 * c + 1])
+        grad_proj[:, D + c * 128 : D + (c + 1) * 128] = unrotate(keys).astype(bf16)
+        grad_proj[:, D + KW + c * 128 : D + KW + (c + 1) * 128] = values.astype(bf16)
+
+
+def backward_kernel(x, grads, grad_normed, middle, gains, cosine, sine, seg_col, seg_row, normed_one, qkv, context,
+                    log_totals, weights, layer, layer_out, input_grad, grad_o, grad_q, weight, grad_middle,
+                    grad_branch, grad_context, grad_proj, grad_one, gain_rows, gain_columns, stage, own_layer, parts,
+                    ones, twos, *sems):
+    sum_sems, (load_sem, out_sem) = sems[:4], sems[4:]
+    z, c, f = place()
+    x_dev, y_dev = device(z, c, flipped(f, 1)), device(z, c, flipped(f, 2))
+    length = x.shape[0]
+    width = D + 2 * KW
+    load_parts = pltpu.make_async_copy(layer.at[pl.ds(1, 3)], parts, load_sem.at[0])
+    load_own = pltpu.make_async_copy(layer.at[0], own_layer, load_sem.at[1])
+    load_o = pltpu.make_async_copy(weights.at[:, pl.ds(width, D)], weight.at[:, pl.ds(0, D)], load_sem.at[2])
+    load_q = pltpu.make_async_copy(weights.at[:, pl.ds(0, width)], weight, load_sem.at[2])
+    load_grads = pltpu.make_async_copy(grad_normed, grad_middle, load_sem.at[3])
+    for copy in (load_parts, load_grads, load_o, load_own):
+        copy.start()
+    greet([x_dev, y_dev], [])
+    summed = PlaneSum(parts, ones, twos, sum_sems, x_dev, y_dev)
+    load_parts.wait()
+    for copy in summed.far + summed.near:
+        copy.start()
+    gain_rows[...] = jnp.zeros_like(gain_rows)
+
+    def fold(value):
+        return jnp.sum(value, axis=0, keepdims=True)
+
+    def middle_grads(r):
+        rows, arrived = middle[r], grad_middle[r]
+        inverse = lax.rsqrt(jnp.mean(rows * rows, axis=-1, keepdims=True) + norm_eps)
+        gain_rows[1:2, :] += fold(arrived * rows * inverse)
+        weighted = arrived * gains[1:2, :]
+        inner = jnp.mean(weighted * rows, axis=-1, keepdims=True)
+        value = grads[r].astype(f32) + inverse * weighted - rows * (inverse * inverse * inverse * inner)
+        grad_middle[r] = value
+        grad_branch[r] = value.astype(bf16)
+
+    load_grads.wait()
+    by_rows(length, middle_grads)
+    load_o.wait()
+
+    def context_step(i, carry):
+        tile = tile_at(i, 512)
+        grad_context[:, tile] = dot_t(grad_branch[...], weight[tile, 0:D]).astype(bf16)
+        return carry
+
+    lax.fori_loop(0, D // 512, context_step, 0)
+    load_q.start()
+    steps = D // 256
+
+    def weight_grads(left, right, target, columns, which):
+        def out(i, slot):
+            return pltpu.make_async_copy(
+                stage.at[slot, :, pl.ds(0, columns)], target.at[tile_at(i, 256), pl.ds(0, columns)], out_sem.at[which, slot]
+            )
+
+        def step(i, carry):
+            slot = i % 2
+
+            @pl.when(i >= 2)
+            def _():
+                out(i - 2, slot).wait()
+
+            stage[slot, :, 0:columns] = dot_tn(left[:, tile_at(i, 256)], right[...]).astype(bf16)
+            out(i, slot).start()
+            return carry
+
+        lax.fori_loop(0, steps, step, 0)
+        for i in (steps - 2, steps - 1):
+            out(i, i % 2).wait()
+
+    weight_grads(context, grad_branch, grad_o, D, 0)
+    allowed = mask_keys_rows(seg_col[...], seg_row[...], length)
+    attend_heads_grad(qkv, grad_context, log_totals, grad_proj, allowed, cosine[...], sine[...])
+    summed.pass_on()
+    weight_grads(normed_one, grad_proj, grad_q, width, 1)
+    load_q.wait()
+
+    def normed_step(i, carry):
+        tile = tile_at(i, 512)
+        grad_one[:, tile] = dot_t(grad_proj[...], weight[tile, :])
+        return carry
+
+    lax.fori_loop(0, D // 512, normed_step, 0)
+
+    def input_grads(r):
+        rows, arrived = x[r].astype(f32), grad_one[r]
+        inverse = lax.rsqrt(jnp.mean(rows * rows, axis=-1, keepdims=True) + norm_eps)
+        gain_rows[0:1, :] += fold(arrived * rows * inverse)
+        weighted = arrived * gains[0:1, :]
+        inner = jnp.mean(weighted * rows, axis=-1, keepdims=True)
+        value = grad_middle[r] + inverse * weighted - rows * (inverse * inverse * inverse * inner)
+        input_grad[r] = value.astype(bf16)
+
+    by_rows(length, input_grads)
+    for i in range(D // 128):
+        rows = pl.ds(i * 128, 128)
+        square = jnp.concatenate([gain_rows[:, rows], jnp.zeros((120, 128), f32)], axis=0)
+        gain_columns[rows, :] = square.T.astype(bf16)
+    gains_out = pltpu.make_async_copy(gain_columns, grad_q.at[:, pl.ds(width, 128)], load_sem.at[0])
+    gains_out.start()
+
+    def add_layer(r, value):
+        layer_out[r] = (middle[r] + own_layer[r].astype(f32) + value).astype(bf16)
+
+    load_own.wait()
+    summed.finish(add_layer)
+    gains_out.wait()
+
+
+def backward(x, grads, grad_normed, middle, gains, cosine, sine, seg_col, seg_row, normed_one, qkv, context,
+             log_totals, weights, layer):
+    length = x.shape[0]
+    width = D + 2 * KW
+    dma = pltpu.SemaphoreType.DMA
+    vmem, hbm = pl.BlockSpec(memory_space=pltpu.VMEM), pl.BlockSpec(memory_space=pl.ANY)
+    sum_buffers, sum_sems = plane_sum_scratch(length, D)
+    return pl.pallas_call(
+        backward_kernel,
+        out_shape=(
+            jax.ShapeDtypeStruct((length, D), bf16),
+            jax.ShapeDtypeStruct((length, D), bf16),
+            jax.ShapeDtypeStruct((D, D), bf16),
+            jax.ShapeDtypeStruct((D, width + 128), bf16),
+        ),
+        in_specs=[vmem, vmem, hbm] + [vmem] * 10 + [hbm] * 2,
+        out_specs=(vmem, vmem, hbm, hbm),
+        scratch_shapes=[
+            pltpu.VMEM((D, width), bf16), pltpu.VMEM((length, D), f32), pltpu.VMEM((length, D), bf16),
+            pltpu.VMEM((length, D), bf16), pltpu.VMEM((length, width), bf16), pltpu.VMEM((length, D), f32),
+            pltpu.VMEM((8, D), f32), pltpu.VMEM((D, 128), bf16), pltpu.VMEM((2, 256, width), bf16),
+            pltpu.VMEM((length, D), bf16),
+        ]
+        + sum_buffers + sum_sems + [dma((4,)), dma((2, 2))],
+        compiler_params=pltpu.CompilerParams(
+            collective_id=7, has_side_effects=True, vmem_limit_bytes=feed_vmem_limit
+        ),
+        cost_estimate=cost(65),
+        name="backward",
+    )(x, grads, grad_normed, middle, gains, cosine, sine, seg_col, seg_row, normed_one, qkv, context, log_totals,
+      weights, layer)
+
+
+def norm_kernel(n_dp, n_tp, parts, qkv, out, down, mlp, total, got, held, got_dp, got_tp, send, recv, total_send,
+                total_recv, here_sem):
+    z, c, f = place()
+    dp = z * 2 + c
+    columns = [(f + k) % n_tp for k in range(1, n_tp)]
+    lines = [(dp + k) % n_dp for k in range(1, n_dp)]
+    greet([device(z, c, to) for to in columns] + [{"dp": to, "fsdp": f} for to in lines], [])
+    unit = mlp.shape[1] // (2 * n_dp * n_tp)
+    half = n_dp * unit
+
+    def away(k):
+        to = columns[k - 1]
+        return pltpu.make_async_remote_copy(
+            parts.at[to], got.at[f], send.at[k], recv.at[k], device_id=device(z, c, to), device_id_type=MESH
+        )
+
+    for k in range(1, n_tp):
+        away(k).start()
+    here = pltpu.make_async_copy(parts.at[f], got.at[f], here_sem)
+    here.start()
+    held[...] = jnp.zeros_like(held)
+
+    def add_squares(ref):
+        def step(r):
+            part = ref[r, :].astype(f32)
+            part = part * part
+            lanes = [part[:, i : i + 128] for i in range(0, part.shape[1], 128)]
+            held[...] += functools.reduce(jnp.add, lanes)
+
+        by_rows(ref.shape[0], step)
+
+    add_squares(qkv)
+    add_squares(out)
+    add_squares(down)
+    here.wait()
+    for k in range(1, n_tp):
+        away(k).wait()
+    for frm in range(n_tp):
+        add_squares(got.at[frm])
+
+    def spread(buffer, own, value, partners, base):
+        buffer[own] = value
+        copies = [
+            pltpu.make_async_remote_copy(
+                buffer.at[own], buffer.at[own], total_send.at[base + k], total_recv.at[base + k],
+                device_id=partner, device_id_type=MESH,
+            )
+            for k, partner in enumerate(partners)
+        ]
+        for copy in copies:
+            copy.start()
+        return copies
+
+    def summed(buffer, copies):
+        for copy in copies:
+            copy.wait()
+        return functools.reduce(jnp.add, [buffer[i] for i in range(buffer.shape[0])])
+
+    own_total = jnp.sum(jnp.sum(held[...], axis=0, keepdims=True), axis=1, keepdims=True)
+    copies = spread(
+        got_dp, dp, jnp.broadcast_to(own_total, (8, 128)), [{"dp": to, "fsdp": f} for to in lines], 0
+    )
+    for side in range(2):
+        pieces = [
+            got[frm, :, side * half + j * unit : side * half + (j + 1) * unit].astype(f32)
+            for j in range(n_dp)
+            for frm in range(n_tp)
+        ]
+        mlp[:, side * n_tp * half : (side + 1) * n_tp * half] = jnp.concatenate(pieces, axis=1)
+    line_total = summed(got_dp, copies)
+    copies = spread(got_tp, f, line_total, [device(z, c, to) for to in columns], n_dp)
+    total[...] = summed(got_tp, copies)
+
+
+def norm_parts(parts, qkv, out, down, n_dp, n_tp):
+    _, rows, width = parts.shape
+    dma = pltpu.SemaphoreType.DMA
+    vmem, hbm = pl.BlockSpec(memory_space=pltpu.VMEM), pl.BlockSpec(memory_space=pl.ANY)
+    return pl.pallas_call(
+        functools.partial(norm_kernel, n_dp, n_tp),
+        out_shape=(jax.ShapeDtypeStruct((rows, width * n_tp), f32), jax.ShapeDtypeStruct((8, 128), f32)),
+        in_specs=[hbm, vmem, vmem, vmem],
+        scratch_shapes=[
+            pltpu.VMEM(parts.shape, bf16), pltpu.VMEM((16, 128), f32), pltpu.VMEM((n_dp, 8, 128), f32),
+            pltpu.VMEM((n_tp, 8, 128), f32), dma((n_tp,)), dma((n_tp,)), dma((n_dp + n_tp,)), dma((n_dp + n_tp,)),
+            dma(()),
+        ],
+        compiler_params=pltpu.CompilerParams(
+            collective_id=8, has_side_effects=True, vmem_limit_bytes=vmem_limit
+        ),
+        cost_estimate=cost(35),
+        name="norm_parts",
+    )(parts, qkv, out, down)
+
+
+def adam_kernel(total, *refs):
+    scale = clip_norm / jnp.maximum(jnp.sqrt(total[0:1, 0:1]), clip_norm)
+    grads, refs = refs[:4], refs[4:]
+    states, news = refs[:12], refs[12:]
+    for i in range(4):
+        gradient = grads[i][...].astype(f32) * scale
+        new = adam_update(
+            states[3 * i][...], gradient, states[3 * i + 1][...], states[3 * i + 2][...], matrix_rate, weight_decay
+        )
+        for k in range(3):
+            news[3 * i + k][...] = new[k]
+
+
+def adam_all(total, grads, states):
+    shapes = [state[0].shape for state in states]
+
+    def block(shape, steps):
+        rows, columns = shape
+        if rows % (8 * steps) == 0:
+            return pl.BlockSpec((rows // steps, columns), lambda i: (i, 0))
+        if columns % (128 * steps) == 0:
+            return pl.BlockSpec((rows, columns // steps), lambda i: (0, i))
+        return None
+
+    steps = 8 if all(block(shape, 8) for shape in shapes) else 4
+    specs = [block(shape, steps) for shape in shapes]
+    flat = [array for state in states for array in state]
+    state_specs = [spec for spec in specs for _ in range(3)]
+    return pl.pallas_call(
+        adam_kernel,
+        grid=(steps,),
+        out_shape=[jax.ShapeDtypeStruct(array.shape, f32) for array in flat],
+        in_specs=[pl.BlockSpec((8, 128), lambda i: (0, 0))] + specs + state_specs,
+        out_specs=state_specs,
+        compiler_params=pltpu.CompilerParams(vmem_limit_bytes=vmem_limit),
+        cost_estimate=cost(14),
+        name="adam",
+    )(total, *grads, *flat)
+
+
 def feed_kernel(n_hbm, g_hbm, wm_hbm, wd_hbm, grad_normed, grad_down, grad_mlp, layer, n, g, wm, wd, gh, act,
-                parts, ones, twos, stage, load_sem, out_sem, one_send, one_recv, two_send, two_recv):
+                stage, parts, ones, twos, *sems):
+    sum_sems, (load_sem, out_sem) = sems[:4], sems[4:]
     z, c, f = place()
     x_dev, y_dev = device(z, c, flipped(f, 1)), device(z, c, flipped(f, 2))
     tokens = n.shape[0]
     length = tokens // 4
-    half = length // 2
     ff = wd.shape[0]
     loads = [
         pltpu.make_async_copy(src, dst, load_sem.at[i])
@@ -1069,28 +1380,14 @@
 
         back(k, store)
 
-    halves = (pl.ds(0, half), pl.ds(half, half))
-    step_dev = (x_dev, y_dev)
-
-    def one(way, i):
-        return pltpu.make_async_remote_copy(
-            parts.at[2 if i else way, halves[way]], ones.at[way, i], one_send.at[way, i], one_recv.at[way, i],
-            device_id=step_dev[way], device_id_type=MESH,
-        )
-
-    def two(way):
-        return pltpu.make_async_remote_copy(
-            parts.at[1 - way, halves[way]], twos.at[way], two_send.at[way], two_recv.at[way],
-            device_id=step_dev[1 - way], device_id_type=MESH,
-        )
-
+    summed = PlaneSum(parts, ones, twos, sum_sems, x_dev, y_dev)
     back_parts(3)
-    one(0, 1).start()
-    one(1, 1).start()
+    for copy in summed.far:
+        copy.start()
     back_parts(1)
-    one(0, 0).start()
+    summed.near[0].start()
     back_parts(2)
-    one(1, 0).start()
+    summed.near[1].start()
 
     def store_own(tile, value):
         grad_normed[:, tile] = value
@@ -1127,16 +1424,7 @@
             down_tile(2 * wide + slot, slot, ff % 256)
             down_out(2 * wide + slot, slot, ff % 256).wait()
 
-    for way in range(2):
-        one(way, 1).wait_recv()
-
-        def add_far(r):
-            there = pl.ds(pl.multiple_of(r.start + way * half, 16), r.size)
-            mine = parts[1 - way, there].astype(f32)
-            parts[1 - way, there] = (mine + ones[way, 1, r].astype(f32)).astype(bf16)
-
-        by_rows(half, add_far)
-        two(way).start()
+    summed.pass_on()
 
     def mlp_out(i, slot):
         rows = pl.ds(pl.multiple_of((i // 2) * 256, 256), 256)
@@ -1167,25 +1455,19 @@
     lax.fori_loop(0, D // 256, layer_step, 0)
     layer_out = pltpu.make_async_copy(g, layer, load_sem.at[0])
     layer_out.start()
-    for way in range(2):
-        one(way, 0).wait()
-        one(way, 1).wait_send()
-        two(way).wait()
-    for way in range(2):
-
-        def add_all(r):
-            there = pl.ds(pl.multiple_of(r.start + way * half, 16), r.size)
-            grad_normed[there] += ones[way, 0, r].astype(f32) + twos[way, r].astype(f32)
-
-        by_rows(half, add_all)
+
+    def add_normed(r, value):
+        grad_normed[r] += value
+
+    summed.finish(add_normed)
     layer_out.wait()
 
 
 def feed(normed_all, grads_all, mlp_cols, down_cols):
     tokens, ff = 4 * normed_all.shape[1], down_cols.shape[0]
     length = tokens // 4
-    half = length // 2
     dma = pltpu.SemaphoreType.DMA
+    sum_buffers, sum_sems = plane_sum_scratch(length, D)
     vmem, hbm = pl.BlockSpec(memory_space=pltpu.VMEM), pl.BlockSpec(memory_space=pl.ANY)
     return pl.pallas_call(
         feed_kernel,
@@ -1200,11 +1482,11 @@
         scratch_shapes=[
             pltpu.VMEM(shape, bf16)
             for shape in (
-                (tokens, D), (tokens, D), (D, 2 * ff), (ff, D), (tokens, 2 * ff), (tokens, ff), (3, length, D),
-                (2, 2, half, D), (2, half, D), (2, 256, max(ff, D // 2)),
+                (tokens, D), (tokens, D), (D, 2 * ff), (ff, D), (tokens, 2 * ff), (tokens, ff),
+                (2, 256, max(ff, D // 2)),
             )
         ]
-        + [dma((4,)), dma((2, 2)), dma((2, 2)), dma((2, 2)), dma((2,)), dma((2,))],
+        + sum_buffers + sum_sems + [dma((4,)), dma((2, 2))],
         compiler_params=pltpu.CompilerParams(
             collective_id=6, has_side_effects=True, vmem_limit_bytes=feed_vmem_limit
         ),
@@ -1289,66 +1571,63 @@
         grad_down = matmul_tn(activated, grads_all).astype(bf16)
         grad_mlp = matmul_tn(normed_all, grad_hidden).astype(bf16)
         layer_parts = matmul(activated, down_cols).astype(bf16).reshape(n_tp, length, D)
-    layer_out = middle + layer_parts[0].astype(f32)
-    for k in range(1, n_tp):
-        layer_out = layer_out + plane_swap(layer_parts[k], k, n_tp).astype(f32)
-    layer_out = layer_out.astype(bf16)
-
-    down_sum = lax.psum_scatter(grad_down, "dp", scatter_dimension=0, tiled=True).astype(f32)
-    mlp_sum = lax.psum_scatter(grad_mlp, "dp", scatter_dimension=0, tiled=True)
-    mlp_sum = columns_back(mlp_sum.reshape(n_tp, rows, 2 * ff), n_dp, n_tp)
-
-    gain_grad_two = jnp.sum(grad_normed_two * middle * inverse_two, axis=0)
-    weighted_two = grad_normed_two * gain_two
-    grad_middle = (
-        cotangent.astype(f32)
-        + inverse_two * weighted_two
-        - middle * inverse_two**3 * jnp.mean(weighted_two * middle, axis=-1, keepdims=True)
+    down_sum = lax.psum_scatter(grad_down, "dp", scatter_dimension=0, tiled=True)
+    mlp_sum = lax.psum_scatter(grad_mlp, "dp", scatter_dimension=0, tiled=True).reshape(n_tp, rows, 2 * ff)
+
+    if n_tp == 4:
+        layer_out, input_grad, grad_out, grad_qkv = backward(
+            inputs, cotangent, grad_normed_two, middle, gains_full, cosine, sine, seg_col, seg_row, normed_one, qkv,
+            attended, log_totals, attn_full, layer_parts,
+        )
+        out_sum, qkv_sum = scatter_all([grad_out, grad_qkv], n_dp, n_tp)
+        mlp_sum, total = norm_parts(mlp_sum, qkv_sum, out_sum, down_sum, n_dp, n_tp)
+    else:
+        layer_out = middle + layer_parts[0].astype(f32)
+        for k in range(1, n_tp):
+            layer_out = layer_out + plane_swap(layer_parts[k], k, n_tp).astype(f32)
+        layer_out = layer_out.astype(bf16)
+        gain_grad_two = jnp.sum(grad_normed_two * middle * inverse_two, axis=0)
+        weighted_two = grad_normed_two * gain_two
+        grad_middle = (
+            cotangent.astype(f32)
+            + inverse_two * weighted_two
+            - middle * inverse_two**3 * jnp.mean(weighted_two * middle, axis=-1, keepdims=True)
+        )
+        grad_branch = grad_middle.astype(bf16)
+        grad_context = matmul_t(grad_branch, out_full).astype(bf16)
+        grad_projected = attend_grad(qkv, grad_context, log_totals, cosine, sine, seg_col, seg_row)
+        grad_out = matmul_tn(attended, grad_branch).astype(bf16)
+        grad_qkv = matmul_tn(normed_one, grad_projected)
+        grad_normed_one = matmul_t(grad_projected, qkv_full)
+        gain_grad_one = jnp.sum(grad_normed_one * tokens_f * inverse_one, axis=0)
+        weighted_one = grad_normed_one * gain_one
+        grad_inputs = (
+            grad_middle
+            + inverse_one * weighted_one
+            - tokens_f * inverse_one**3 * jnp.mean(weighted_one * tokens_f, axis=-1, keepdims=True)
+        )
+        input_grad = grad_inputs.astype(bf16)
+        gain_grads = jnp.pad(jnp.stack([gain_grad_one, gain_grad_two], axis=1), ((0, 0), (0, 126)))
+        grad_qkv = jnp.concatenate([grad_qkv.astype(bf16), gain_grads.astype(bf16)], axis=1)
+        out_sum, qkv_sum = scatter_all([grad_out, grad_qkv], n_dp, n_tp)
+        mlp_sum = columns_back(mlp_sum, n_dp, n_tp)
+        squares = jnp.sum(qkv_sum * qkv_sum) + jnp.sum(out_sum * out_sum) + jnp.sum(mlp_sum * mlp_sum)
+        squares = squares + jnp.sum(jnp.square(down_sum.astype(f32)))
+        total = total_over_devices(squares, n_dp, n_tp)
+    gains_sum = qkv_sum[:, D + 2 * KW : D + 2 * KW + 2].T
+    grad_norm = jnp.sqrt(total[0, 0])
+    clip_scale = clip_norm / jnp.maximum(grad_norm, clip_norm)
+    states = (
+        (qkv_weight, qkv_first, qkv_second),
+        (out_weight, out_first, out_second),
+        (mlp_weight, mlp_first, mlp_second),
+        (down_weight, down_first, down_second),
     )
-    grad_branch = grad_middle.astype(bf16)
-    grad_context = matmul_t(grad_branch, out_full).astype(bf16)
-    grad_projected = attend_grad(qkv, grad_context, log_totals, cosine, sine, seg_col, seg_row)
-
-    grad_out = matmul_tn(attended, grad_branch).astype(bf16)
-    grad_qkv = matmul_tn(normed_one, grad_projected)
-    grad_normed_one = matmul_t(grad_projected, qkv_full)
-    gain_grad_one = jnp.sum(grad_normed_one * tokens_f * inverse_one, axis=0)
-    weighted_one = grad_normed_one * gain_one
-    grad_inputs = (
-        grad_middle
-        + inverse_one * weighted_one
-        - tokens_f * inverse_one**3 * jnp.mean(weighted_one * tokens_f, axis=-1, keepdims=True)
-    )
-    input_grad = grad_inputs.astype(bf16)
-    gain_grads = jnp.pad(jnp.stack([gain_grad_one, gain_grad_two], axis=1), ((0, 0), (0, 126)))
-    grad_qkv = jnp.concatenate([grad_qkv.astype(bf16), gain_grads.astype(bf16)], axis=1)
-    out_sum, qkv_sum = scatter_all([grad_out, grad_qkv], n_dp, n_tp)
-    gains_sum = qkv_sum[:, D + 2 * KW : D + 2 * KW + 2].T
-    qkv_sum = qkv_sum[:, : D + 2 * KW]
-
-    local_squares = (
-        jnp.sum(qkv_sum * qkv_sum) + jnp.sum(out_sum * out_sum) + jnp.sum(mlp_sum * mlp_sum)
-    )
-    local_squares = local_squares + jnp.sum(down_sum * down_sum) + jnp.sum(gains_sum * gains_sum)
-    total_squares = total_over_devices(local_squares, n_dp, n_tp)
-    grad_norm = jnp.sqrt(total_squares)
-    clip_scale = clip_norm / jnp.maximum(grad_norm, clip_norm)
-    qkv_out = adam_update(
-        qkv_weight, qkv_sum * clip_scale, qkv_first, qkv_second, matrix_rate, weight_decay
-    )
-    out_out = adam_update(
-        out_weight, out_sum * clip_scale, out_first, out_second, matrix_rate, weight_decay
-    )
-    mlp_out = adam_update(
-        mlp_weight, mlp_sum * clip_scale, mlp_first, mlp_second, matrix_rate, weight_decay
-    )
-    down_out = adam_update(
-        down_weight, down_sum * clip_scale, down_first, down_second, matrix_rate, weight_decay
-    )
+    stepped = adam_all(total, (qkv_sum, out_sum, mlp_sum, down_sum), states)
     gains_out = adam_update(
         norm_gains, gains_sum * clip_scale, gains_first, gains_second, gain_rate, 0.0
     )
-    news = [[new[i] for new in (qkv_out, out_out, mlp_out, down_out, gains_out)] for i in range(3)]
+    news = [[*stepped[i::3], gains_out[i]] for i in range(3)]
     return (layer_out, input_grad, grad_norm, *news[0], *news[1], *news[2])
 
 

time: 700 us -> 643 us (0.919)
  Pallas kernels: 511 us -> 601 us
  waiting for transfers between devices: 61.2 us -> 0.73 us
  other arithmetic: 52.2 us -> 5.29 us
  matrix products: 33.6 us -> 0 us
    ppermute x3 -> x0, waiting for transfers between devices: 60.5 us -> none  [plane_swap(): return lax.ppermute(block, 'fsdp', [(i, i ^ k) for i in range(n_tp)])]
    pallas_call x3, Pallas kernels: 61.3 us -> 112 us  [the longest x1 69 us: backward(): pl.pallas_call(backward_kernel, out_shape=(jax.ShapeDtypeStruct((length,...]
    pallas_call x1, Pallas kernels: 121 us -> 160 us  [scatter_all(): pl.pallas_call(functools.partial(scatter_kernel, lines, n), out_shape=[ja...]
    dot_general x4 -> x0, matrix products: 33.6 us -> none  [the longest x2 18.9 us: matmul_t(): lax.dot_general(a, b, (((1,), (1,)), ((), ())), preferred_element_type=f32)]
    sub x5 -> x1, other arithmetic: 15.2 us -> 0.02 us  [adam_update(): weight - rate * (first_hat / (jnp.sqrt(second_hat) + adam_eps) + decay *...]
    reduce_sum x8 -> x0, other arithmetic: 14.6 us -> none  [the longest x1 3.26 us: local(): jnp.sum(mlp_sum * mlp_sum)]
    unnamed x54 -> x50, local copies, waits for them, and re-layouts: 5.54 us -> 12.8 us
  transfers between devices with their start and end apart: 6 -> 3, of which waited for: 3 -> 0; matrix products, arithmetic and copies ran while one was open for 10% -> 1% of each run, Pallas kernels for 37% -> 53%
where the time goes in v4:
time: 643 us; the launch traced here: 639 us
  Pallas kernels  601 us (93%)
  between operations  16.9 us (3%)
  local copies, waits for them, and re-layouts  15 us (2%)
    pallas_call x1, Pallas kernels, scatter_all(): pl.pallas_call(functools.partial(scatter_kernel, lines, n), out_shape=[ja...  160 us
    pallas_call x1, Pallas kernels, feed(): pl.pallas_call(feed_kernel, out_shape=(jax.ShapeDtypeStruct((length, D),...  116 us
    pallas_call x1, Pallas kernels, forward(): pl.pallas_call(forward_kernel, out_shape=(jax.ShapeDtypeStruct((length, w...  109 us
    pallas_call x1, Pallas kernels, gather_all(): pl.pallas_call(functools.partial(gather_kernel, lines), out_shape=(jax.Sh...  103 us
    pallas_call x1, Pallas kernels, backward(): pl.pallas_call(backward_kernel, out_shape=(jax.ShapeDtypeStruct((length,...  69 us
    pallas_call x1, Pallas kernels, norm_parts(): pl.pallas_call(functools.partial(norm_kernel, n_dp, n_tp), out_shape=(jax...  28.8 us
    pallas_call x1, Pallas kernels, adam_all(): pl.pallas_call(adam_kernel, grid=(steps,), out_shape=[jax.ShapeDtypeStruc...  14.6 us
  transfers between devices with their start and end apart: 3, of which 0 were waited for; matrix products, arithmetic and copies ran while one was open for 1% of the time, Pallas kernels for 53%

profile of v4, /device:TPU:0, one launch (start us, length us, event | category | flops | bytes accessed | tf_op | source)
XLA Modules:
  0.0 638.9 jit_solution(16960725392173147780)
XLA Ops:
  7.2 0.0 all-gather.2.cloned.1.call-start
  7.3 1.2 convert.13
  8.5 1.1 convert.14
  9.6 0.1 copy.70
  9.7 0.1 convert_element_type.14.down
  9.9 103.3 %gather_all.1 = (bf16[4,2,4,64,4736]{4,3,2,1,0:T(8,128)(2,1)}, bf16[4,64,2816]{2,1,0:T(8,128)(2,1)}, bf16[4,2,176,2048]{3,2,1,0:T(8,128)(2,1)}) custom-call(bf16[64,4736]{1,0:T(8,128)(2,1)S(1)} %fusion.1.own, f32[64,11264]{1,0:T(8,128)} %refs_10_.1, bf16[176,2048]{1,0:T(8,128)(2,1)S(1)} %convert_element_type.14.down), custom_call_target="tpu_custom_call" | custom-call | bytes 369000000 | tf_op jit(solution)/shard_map/gather_all/pallas_call | solution.py:366
  113.2 0.0 reduce-scatter.5.cloned.1.call-start
  113.2 0.5 slice.27
  114.4 0.1 add_select_fusion
  114.5 0.3 reduce-window.9
  114.8 0.1 slice.30
  114.9 1.1 convert_bitcast_fusion
  116.0 0.3 copy.72.gains
  116.4 0.1 copy.73.seg_col
  116.6 0.1 slice_reduce_fusion
  116.7 0.1 fusion.6
  116.8 0.8 fusion.2
  117.5 0.4 pad_maximum_fusion
  117.9 109.0 %forward.1 = (bf16[384,2560]{1,0:T(8,128)(2,1)}, bf16[384,2048]{1,0:T(8,128)(2,1)S(1)}, f32[32,384]{1,0:T(8,128)S(1)}, f32[384,2048]{1,0:T(8,128)}, bf16[384,204...) custom-call(bf16[384,2048]{1,0:T(8,128)(2,1)} %x.5, bf16[384,2048]{1,0:T(8,128)(2,1)} %grads.3, ...), custom_call_target="tpu_custom_call" | custom-call | bytes 350550016 | tf_op jit(solution)/shard_map/forward/pallas_call | solution.py:919
  227.0 1.1 copy-done.8
  228.1 0.6 copy-done.14
  228.7 116.3 %feed.1 = (f32[384,2048]{1,0:T(8,128)}, bf16[1408,2048]{1,0:T(8,128)(2,1)}, bf16[2048,2816]{1,0:T(8,128)(2,1)}, bf16[1536,2048]{1,0:T(8,128)(2,1)}) custom-call(bf16[1536,2048]{1,0:T(8,128)(2,1)} %bitcast.43, bf16[1536,2048]{1,0:T(8,128)(2,1)} %bitcast.44, bf16[2048,2816]{1,0:T(8,128)(2,1)} %all-gather.2.cloned.1.call-done.wm_hbm, bf16[1408,2048]{1,0:T(8,128)(2,1)} %bitcast.46), custom_call_target="tpu_custom_call" | custom-call | bytes 424350016 | tf_op jit(solution)/shard_map/feed/pallas_call | solution.py:1472
  345.1 0.0 reduce-scatter.3.cloned.1.call-start
  345.1 0.7 reduce-scatter.3.cloned.1.call-update
  345.8 0.1 copy.81
  345.9 0.1 copy.76
  346.0 0.1 copy.78
  346.1 69.0 %backward.1 = (bf16[384,2048]{1,0:T(8,128)(2,1)}, bf16[384,2048]{1,0:T(8,128)(2,1)}, bf16[2048,2048]{1,0:T(8,128)(2,1)}, bf16[2048,2688]{1,0:T(8,128)(2,1)}) custom-call(bf16[384,2048]{1,0:T(8,128)(2,1)} %x.5, bf16[384,2048]{1,0:T(8,128)(2,1)} %grads.3, f32[384,2048]{1,0:T(8,128)} %get-tuple-element.57.grad_normed, f32[384,2048]{1,0:T(8,128)} %get-tuple-element.58.middle, ...), custom_call_target="tpu_custom_call" | custom-call | bytes 239850000 | tf_op jit(solution)/shard_map/backward/pallas_call | solution.py:1168
  415.2 159.8 %scatter_all.1 = (f32[64,2048]{1,0:T(8,128)S(1)}, f32[64,2688]{1,0:T(8,128)S(1)}) custom-call(bf16[4,2,4,64,2048]{4,3,2,1,0:T(8,128)(2,1)} %bitcast.42, bf16[4,2,4,64,2688]{4,3,2,1,0:T(8,128)(2,1)} %bitcast.41), custom_call_target="tpu_custom_call" | custom-call | bytes 405900000 | tf_op jit(solution)/shard_map/scatter_all/pallas_call | solution.py:768
  575.0 0.0 reduce-scatter.5.cloned.1.call-done.down.refs_3_
  575.0 0.0 reduce-scatter.3.cloned.1.call-done
  575.1 1.3 copy-done.2
  576.4 1.4 copy-done.9
  577.7 28.8 %norm_parts.1 = (f32[64,11264]{1,0:T(8,128)}, f32[8,128]{1,0:T(8,128)S(1)}) custom-call(bf16[4,64,2816]{2,1,0:T(8,128)(2,1)S(1)} %bitcast.36, f32[64,2688]{1,0:T(8,128)S(1)} %get-tuple-element.69.qkv.refs_0_, f32[64,2048]{1,0:T(8,128)S(1)} %get-tuple-element.70.out.refs_1_, bf16[176,2048]{1,0:T(8,128)(2,1)S(1)} %copy-done.2), custom_call_target="tpu_custom_call" | custom-call | bytes 129150000 | tf_op jit(solution)/shard_map/norm_parts/pallas_call | solution.py:1272
  606.6 0.5 slice.32
  607.9 0.1 copy.79
  608.0 0.1 copy.80
  608.0 0.1 copy.82
  608.2 0.6 copy.83
  608.8 0.6 copy.84
  609.4 0.6 copy.85
  610.1 1.1 copy-done.11
  611.2 1.0 copy-done.12
  612.2 1.0 copy-done.13
  613.3 14.6 %adam.1 = (f32[64,2560]{1,0:T(8,128)}, f32[64,2560]{1,0:T(8,128)}, f32[64,2560]{1,0:T(8,128)}, f32[64,2048]{1,0:T(8,128)}, f32[64,2048]{1,0:T(8,128)}, /*index=5...) custom-call(f32[8,128]{1,0:T(8,128)S(1)} %get-tuple-element.72.total, ...), custom_call_target="tpu_custom_call" | custom-call | bytes 51660000 | tf_op jit(solution)/shard_map/adam/pallas_call | solution.py:1317
  627.9 1.1 copy.88
  629.1 0.8 copy-done.17
  629.9 1.1 copy.89
  (50 shorter events, 0.3 us)
Async XLA Ops:
  7.2 2.4 copy-start.19
  7.2 2.5 copy-start.16
  7.2 221.5 %all-gather.2.cloned.1.call-start = ((), (), s32[]{:S(2)}) async-start(), calls=%async_computation.2 | async-start | bytes 12976128 | tf_op jit(solution)/shard_map/all_gather | solution.py:1536
  9.9 103.4 %copy-start.15 = (s32[1,384]{1,0:T(1,128)S(1)}, s32[1,384]{1,0:T(1,128)}, u32[]{:S(2)}) copy-start(s32[1,384]{1,0:T(1,128)} %seg_row.3) | copy-start | bytes 4612
  113.2 461.9 %reduce-scatter.5.cloned.1.call-start = ((), (), s32[]{:S(2)}) async-start(), calls=%async_computation.4 | async-start | bytes 6488064 | tf_op jit(solution)/shard_map/reduce_scatter | solution.py:1574
  116.4 110.5 %copy-start = (f32[128,2048]{1,0:T(8,128)}, f32[128,2048]{1,0:T(8,128)S(1)}, u32[]{:S(2)}) copy-start(f32[128,2048]{1,0:T(8,128)S(1)} %copy.72.gains) | copy-start | bytes 3145732
  116.5 110.4 %copy-start.5 = (s32[384,1]{1,0:T(8,128)}, s32[384,1]{1,0:T(8,128)S(1)}, u32[]{:S(2)}) copy-start(s32[384,1]{1,0:T(8,128)S(1)} %copy.73.seg_col) | copy-start | bytes 4612
  117.9 109.0 %copy-start.6 = (f32[384,128]{1,0:T(8,128)}, f32[384,128]{1,0:T(8,128)S(1)}, u32[]{:S(2)}) copy-start(f32[384,128]{1,0:T(8,128)S(1)} %get-tuple-element.149.cosine) | copy-start | bytes 589828
  117.9 109.0 %copy-start.7 = (f32[384,128]{1,0:T(8,128)}, f32[384,128]{1,0:T(8,128)S(1)}, u32[]{:S(2)}) copy-start(f32[384,128]{1,0:T(8,128)S(1)} %get-tuple-element.150.sine) | copy-start | bytes 589828
  226.9 1.1 copy-start.8
  228.1 0.6 copy-start.14
  345.1 230.0 %reduce-scatter.3.cloned.1.call-start = ((), (), s32[]{:S(2)}) async-start(), calls=%async_computation.3 | async-start | bytes 12976128 | tf_op jit(solution)/shard_map/reduce_scatter | solution.py:1575
  345.1 0.8 copy-start.20
  345.1 0.9 copy-start.21
  575.0 32.8 %copy-start.1 = (f32[64,2688]{1,0:T(8,128)}, f32[64,2688]{1,0:T(8,128)S(1)}, u32[]{:S(2)}) copy-start(f32[64,2688]{1,0:T(8,128)S(1)} %get-tuple-element.69.qkv.refs_0_) | copy-start | bytes 2064388
  575.1 1.3 copy-start.2
  576.4 1.4 copy-start.9
  577.7 32.3 %copy-start.3 = (f32[64,2560]{1,0:T(8,128)S(1)}, f32[64,2560]{1,0:T(8,128)}, u32[]{:S(2)}) copy-start(f32[64,2560]{1,0:T(8,128)} %refs_4_.1) | copy-start | bytes 1966084
  577.7 32.3 %copy-start.4 = (f32[64,2048]{1,0:T(8,128)S(1)}, f32[64,2048]{1,0:T(8,128)}, u32[]{:S(2)}) copy-start(f32[64,2048]{1,0:T(8,128)} %refs_7_.1) | copy-start | bytes 1572868
  577.7 32.3 %copy-start.10 = (f32[64,2560]{1,0:T(8,128)S(1)}, f32[64,2560]{1,0:T(8,128)}, u32[]{:S(2)}) copy-start(f32[64,2560]{1,0:T(8,128)} %refs_5_.1) | copy-start | bytes 1966084
  610.1 1.1 copy-start.11
  611.2 1.0 copy-start.12
  612.2 1.0 copy-start.13
  613.3 14.6 %copy-start.18 = (bf16[384,2048]{1,0:T(8,128)(2,1)S(1)}, bf16[384,2048]{1,0:T(8,128)(2,1)}, u32[]{:S(2)}) copy-start(bf16[384,2048]{1,0:T(8,128)(2,1)} %get-tuple-element.169) | copy-start | bytes 4718596
  627.9 2.0 copy-start.17
Sparse Core Ops, SparseCore 0:
  113.3 108.4 all-gather.1
  345.2 65.1 reduce-scatter.4
  412.7 156.5 reduce-scatter.2

commit v5 on v4

--- a/solution.py
+++ b/solution.py
@@ -595,191 +595,188 @@
     lax.fori_loop(0, rows // 16, step, 0)
 
 
-def scatter_kernel(lines, n_arrays, *refs):
-    groups = [refs[i * n_arrays : (i + 1) * n_arrays] for i in range(8)]
-    arrays, outs, sums, others, firsts, seconds, alongs, leaving = groups
-    load_sem, core_send, core_recv, one_send, one_recv, two_send, two_recv, line_send, line_recv = refs[8 * n_arrays :]
-    z, c, f = place()
-    planes, rows = sums[0].shape[1:3]
-    half = rows // 2
-    fx, fy = flipped(f, 1), flipped(f, 2)
-    fd = flipped(fx, 2)
-    x_dev, y_dev, core_dev = device(z, c, fx), device(z, c, fy), device(z, 1 - c, f)
-    has_left = jnp.minimum(z, 1)
-    has_right = jnp.minimum(lines - 1 - z, 1)
-    left_dev = device(jnp.maximum(z - 1, 0), c, f)
-    right_dev = device(jnp.minimum(z + 1, lines - 1), c, f)
-    greet([x_dev, y_dev, core_dev], [(has_left, left_dev), (has_right, right_dev)])
-    halves = (pl.ds(0, half), pl.ds(half, half))
-    near, next_near, step_dev = (fx, fy), (fy, fx), (x_dev, y_dev)
-
-    def remote(src, dst, send, recv, dev):
-        return pltpu.make_async_remote_copy(src, dst, send, recv, device_id=dev, device_id_type=MESH)
-
-    def to_core(a, d):
-        return remote(arrays[a].at[d, 1 - c], others[a].at[d], core_send.at[a, d], core_recv.at[a, d], core_dev)
-
-    def load(a, d):
-        return pltpu.make_async_copy(arrays[a].at[d, c], sums[a].at[d], load_sem.at[a, d])
-
-    def one(a, d, way, i):
-        block = (near[way], fd)[i]
-        return remote(
-            sums[a].at[d, block, halves[way]], firsts[a].at[way, d, i],
-            one_send.at[a, d, way, i], one_recv.at[a, d, way, i], step_dev[way],
-        )
-
-    def two(a, d, way):
-        return remote(
-            sums[a].at[d, next_near[way], halves[way]], seconds[a].at[way, d],
-            two_send.at[a, d, way], two_recv.at[a, d, way], step_dev[1 - way],
-        )
-
-    def to_right(a, d):
-        return remote(leaving[a].at[d], alongs[a].at[d], line_send.at[a, d], line_recv.at[a, d], right_dev)
-
-    def to_left(a, d, slot):
-        return remote(leaving[a].at[d], alongs[a].at[slot], line_send.at[a, d], line_recv.at[a, slot], left_dev)
-
-    def add_along(a, slot):
+class Scatter:
+    def __init__(self, lines, groups, sems):
+        self.sums, self.others, self.firsts, self.seconds, self.alongs, self.leaving, self.outs = groups
+        core_send, core_recv, one_send, one_recv, two_send, two_recv, line_send, line_recv = sems
+        z, c, f = place()
+        self.z, self.f, self.lines = z, f, lines
+        self.planes, self.rows = self.sums[0].shape[1:3]
+        self.half = self.rows // 2
+        fx, fy = flipped(f, 1), flipped(f, 2)
+        fd = flipped(fx, 2)
+        x_dev, y_dev, core_dev = device(z, c, fx), device(z, c, fy), device(z, 1 - c, f)
+        self.has_left = jnp.minimum(z, 1)
+        self.has_right = jnp.minimum(lines - 1 - z, 1)
+        left_dev = device(jnp.maximum(z - 1, 0), c, f)
+        right_dev = device(jnp.minimum(z + 1, lines - 1), c, f)
+        greet([x_dev, y_dev, core_dev], [(self.has_left, left_dev), (self.has_right, right_dev)])
+        halves = (pl.ds(0, self.half), pl.ds(self.half, self.half))
+        near, self.next_near, step_dev = (fx, fy), (fy, fx), (x_dev, y_dev)
+        self.order = []
+        for t in reversed(range(lines)):
+            line = z
+            for b in range(lines.bit_length() - 1):
+                if t >> b & 1:
+                    line = flipped(line, 1 << b)
+            self.order.append(line)
+
+        def remote(src, dst, send, recv, dev):
+            return pltpu.make_async_remote_copy(src, dst, send, recv, device_id=dev, device_id_type=MESH)
+
+        def to_core(a, d, src):
+            return remote(src, self.others[a].at[d], core_send.at[a, d], core_recv.at[a, d], core_dev)
+
+        def one(a, d, way, i):
+            block = (near[way], fd)[i]
+            return remote(
+                self.sums[a].at[d, block, halves[way]], self.firsts[a].at[way, d, i],
+                one_send.at[a, d, way, i], one_recv.at[a, d, way, i], step_dev[way],
+            )
+
+        def two(a, d, way):
+            return remote(
+                self.sums[a].at[d, self.next_near[way], halves[way]], self.seconds[a].at[way, d],
+                two_send.at[a, d, way], two_recv.at[a, d, way], step_dev[1 - way],
+            )
+
+        def to_right(a, d):
+            return remote(
+                self.leaving[a].at[d], self.alongs[a].at[d], line_send.at[a, d], line_recv.at[a, d], right_dev
+            )
+
+        def to_left(a, d, slot):
+            return remote(
+                self.leaving[a].at[d], self.alongs[a].at[slot], line_send.at[a, d], line_recv.at[a, slot], left_dev
+            )
+
+        self.to_core, self.one, self.two, self.to_right, self.to_left = to_core, one, two, to_right, to_left
+
+    def add_along(self, a, slot):
         def step(r):
-            outs[a][r] += alongs[a][slot, r].astype(f32)
-
-        by_rows(rows, step)
-
-    order = []
-    for t in reversed(range(lines)):
-        line = z
-        for b in range(lines.bit_length() - 1):
-            if t >> b & 1:
-                line = flipped(line, 1 << b)
-        order.append(line)
-    chunks = [(a, d) for d in order for a in range(n_arrays)]
-    for a, d in chunks:
-        to_core(a, d).start()
-        load(a, d).start()
-    for a, d in chunks:
-        load(a, d).wait()
-        to_core(a, d).wait_recv()
+            self.outs[a][r] += self.alongs[a][slot, r].astype(f32)
+
+        by_rows(self.rows, step)
+
+    def over_core(self, a, d):
+        sums, others = self.sums[a], self.others[a]
+        self.to_core(a, d, others.at[d]).wait_recv()
 
         def core_add(r):
-            for plane in range(planes):
-                sums[a][d, plane, r] = (sums[a][d, plane, r].astype(f32) + others[a][d, plane, r].astype(f32)).astype(bf16)
-
-        by_rows(rows, core_add)
+            for plane in range(self.planes):
+                sums[d, plane, r] = (sums[d, plane, r].astype(f32) + others[d, plane, r].astype(f32)).astype(bf16)
+
+        by_rows(self.rows, core_add)
         for i in (1, 0):
             for way in range(2):
-                one(a, d, way, i).start()
-    for a, d in chunks:
+                self.one(a, d, way, i).start()
+
+    def there(self, r, way):
+        return pl.ds(pl.multiple_of(r.start + way * self.half, 16), r.size)
+
+    def over_first(self, a, d):
+        sums, firsts = self.sums[a], self.firsts[a]
         for way in range(2):
-            one(a, d, way, 1).wait_recv()
+            self.one(a, d, way, 1).wait_recv()
+            block = self.next_near[way]
 
             def first_add(r):
-                there = pl.ds(pl.multiple_of(r.start + way * half, 16), r.size)
-                mine = sums[a][d, next_near[way], there].astype(f32)
-                sums[a][d, next_near[way], there] = (mine + firsts[a][way, d, 1, r].astype(f32)).astype(bf16)
-
-            by_rows(half, first_add)
-            two(a, d, way).start()
-    for a, d in chunks:
+                there = self.there(r, way)
+                mine = sums[d, block, there].astype(f32)
+                sums[d, block, there] = (mine + firsts[way, d, 1, r].astype(f32)).astype(bf16)
+
+            by_rows(self.half, first_add)
+            self.two(a, d, way).start()
+
+    def over_second(self, a, d):
+        sums, firsts, seconds, outs, z = self.sums[a], self.firsts[a], self.seconds[a], self.outs[a], self.z
         for way in range(2):
-            one(a, d, way, 0).wait_recv()
-            two(a, d, way).wait_recv()
+            self.one(a, d, way, 0).wait_recv()
+            self.two(a, d, way).wait_recv()
 
             def second_add(r):
-                there = pl.ds(pl.multiple_of(r.start + way * half, 16), r.size)
-                outs[a][there] = (
-                    sums[a][d, f, there].astype(f32)
-                    + firsts[a][way, d, 0, r].astype(f32)
-                    + seconds[a][way, d, r].astype(f32)
+                there = self.there(r, way)
+                outs[there] = (
+                    sums[d, self.f, there].astype(f32)
+                    + firsts[way, d, 0, r].astype(f32)
+                    + seconds[way, d, r].astype(f32)
                 )
 
-            by_rows(half, second_add)
-
-        @pl.when((d > z) & (has_left == 1))
+            by_rows(self.half, second_add)
+
+        @pl.when((d > z) & (self.has_left == 1))
         def _():
-            to_right(a, d).wait_recv()
-            add_along(a, d)
-
-        @pl.when((d < z) & (has_right == 1))
+            self.to_right(a, d).wait_recv()
+            self.add_along(a, d)
+
+        @pl.when((d < z) & (self.has_right == 1))
         def _():
-            to_left(a, d, d).wait_recv()
-            add_along(a, d)
+            self.to_left(a, d, d).wait_recv()
+            self.add_along(a, d)
 
         @pl.when(d != z)
         def _():
             def leave(r):
-                leaving[a][d, r] = outs[a][r].astype(bf16)
-
-            by_rows(rows, leave)
+                self.leaving[a][d, r] = outs[r].astype(bf16)
+
+            by_rows(self.rows, leave)
 
         @pl.when(d > z)
         def _():
-            to_right(a, d).start()
+            self.to_right(a, d).start()
 
         @pl.when((d < z) & (d + 1 < z))
         def _():
-            to_left(a, d, d).start()
+            self.to_left(a, d, d).start()
 
         @pl.when(d + 1 == z)
         def _():
-            to_left(a, d, lines).start()
-
-    for a in range(n_arrays):
-
-        @pl.when(has_left == 1)
-        def _():
-            to_right(a, z).wait_recv()
-            add_along(a, z)
-
-        @pl.when(has_right == 1)
-        def _():
-            to_left(a, z, lines).wait_recv()
-            add_along(a, lines)
-
-    for a, d in chunks:
-        to_core(a, d).wait_send()
-        for way in range(2):
-            one(a, d, way, 0).wait_send()
-            one(a, d, way, 1).wait_send()
-            two(a, d, way).wait_send()
-
-        @pl.when(d != z)
-        def _():
-            to_right(a, d).wait_send()
-
-
-def scatter_all(arrays, n_dp, n_tp):
-    lines = n_dp // 2
-    rows = arrays[0].shape[0] // (n_dp * n_tp)
-    if n_tp != 4 or rows % 32:
-        results = []
-        for array in arrays:
-            parts = core_sum(array.reshape(lines, 2, n_tp, rows, -1), n_dp)
-            results.append(line_sum(plane_sum(parts.transpose(1, 0, 2, 3), n_tp), n_dp))
-        return results
+            self.to_left(a, d, self.lines).start()
+
+    def finish(self):
+        for a in range(len(self.sums)):
+
+            @pl.when(self.has_left == 1)
+            def _():
+                self.to_right(a, self.z).wait_recv()
+                self.add_along(a, self.z)
+
+            @pl.when(self.has_right == 1)
+            def _():
+                self.to_left(a, self.z, self.lines).wait_recv()
+                self.add_along(a, self.lines)
+
+            for d in self.order:
+                for way in range(2):
+                    self.one(a, d, way, 0).wait_send()
+                    self.one(a, d, way, 1).wait_send()
+                    self.two(a, d, way).wait_send()
+
+                @pl.when(d != self.z)
+                def _():
+                    self.to_right(a, d).wait_send()
+
+
+def scatter_scratch(lines, n_tp, rows, widths):
     dma = pltpu.SemaphoreType.DMA
-    widths = [array.shape[1] for array in arrays]
     n = len(widths)
     shapes = [
         (lines, n_tp, rows), (lines, n_tp, rows), (2, lines, 2, rows // 2), (2, lines, rows // 2),
         (lines + 1, rows), (lines, rows),
     ]
-    return pl.pallas_call(
-        functools.partial(scatter_kernel, lines, n),
-        out_shape=[jax.ShapeDtypeStruct((rows, width), f32) for width in widths],
-        in_specs=[pl.BlockSpec(memory_space=pl.ANY)] * n,
-        scratch_shapes=[pltpu.VMEM((*shape, width), bf16) for shape in shapes for width in widths]
-        + [dma((n, lines))] * 3
-        + [dma((n, lines, 2, 2))] * 2
-        + [dma((n, lines, 2))] * 2
-        + [dma((n, lines)), dma((n, lines + 1))],
-        compiler_params=pltpu.CompilerParams(
-            collective_id=4, has_side_effects=True, vmem_limit_bytes=vmem_limit
-        ),
-        cost_estimate=cost(110),
-        name="scatter_all",
-    )(*[array.reshape(lines, 2, n_tp, rows, -1) for array in arrays])
+    buffers = [pltpu.VMEM((*shape, width), bf16) for shape in shapes for width in widths]
+    sems = [dma((n, lines))] * 2 + [dma((n, lines, 2, 2))] * 2 + [dma((n, lines, 2))] * 2
+    return buffers, sems + [dma((n, lines)), dma((n, lines + 1))]
+
+
+def scatter_all(arrays, n_dp, n_tp):
+    lines = n_dp // 2
+    rows = arrays[0].shape[0] // (n_dp * n_tp)
+    results = []
+    for array in arrays:
+        parts = core_sum(array.reshape(lines, 2, n_tp, rows, -1), n_dp)
+        results.append(line_sum(plane_sum(parts.transpose(1, 0, 2, 3), n_tp), n_dp))
+    return results
 
 
 def rope_tile(tile, cos, sin):
@@ -934,7 +931,7 @@
             dma((2,)), dma((2, 4)), dma((2, 4)), dma((2,)),
         ],
         compiler_params=pltpu.CompilerParams(
-            collective_id=5, has_side_effects=True, vmem_limit_bytes=vmem_limit
+            collective_id=5, has_side_effects=True, vmem_limit_bytes=feed_vmem_limit
         ),
         cost_estimate=cost(95),
         name="forward",
@@ -997,7 +994,7 @@
     return [pltpu.VMEM(shape, bf16) for shape in shapes], [dma((2, 2)), dma((2, 2)), dma((2,)), dma((2,))]
 
 
-def attend_heads_grad(qkv, grad_context, log_totals, grad_proj, allowed, cos, sin):
+def attend_heads_grad(qkv, grad_context, log_totals, grad_proj, allowed, cos, sin, between=None):
     length = qkv.shape[0]
     scale = HD ** (-0.5)
 
@@ -1041,6 +1038,8 @@
 
         key_parts.append(joined(out[0], out[1]))
         value_parts.append(joined(out[2], out[3]))
+        if between is not None:
+            between(group)
     lane = lax.broadcasted_iota(jnp.int32, (length, 128), 1)
     for c in range(KVH // 2):
         keys = jnp.where(lane < HD, key_parts[2 * c], key_parts[2 * c + 1])
@@ -1049,146 +1048,208 @@
         grad_proj[:, D + KW + c * 128 : D + KW + (c + 1) * 128] = values.astype(bf16)
 
 
-def backward_kernel(x, grads, grad_normed, middle, gains, cosine, sine, seg_col, seg_row, normed_one, qkv, context,
-                    log_totals, weights, layer, layer_out, input_grad, grad_o, grad_q, weight, grad_middle,
-                    grad_branch, grad_context, grad_proj, grad_one, gain_rows, gain_columns, stage, own_layer, parts,
-                    ones, twos, *sems):
-    sum_sems, (load_sem, out_sem) = sems[:4], sems[4:]
-    z, c, f = place()
-    x_dev, y_dev = device(z, c, flipped(f, 1)), device(z, c, flipped(f, 2))
-    length = x.shape[0]
-    width = D + 2 * KW
-    load_parts = pltpu.make_async_copy(layer.at[pl.ds(1, 3)], parts, load_sem.at[0])
-    load_own = pltpu.make_async_copy(layer.at[0], own_layer, load_sem.at[1])
-    load_o = pltpu.make_async_copy(weights.at[:, pl.ds(width, D)], weight.at[:, pl.ds(0, D)], load_sem.at[2])
-    load_q = pltpu.make_async_copy(weights.at[:, pl.ds(0, width)], weight, load_sem.at[2])
-    load_grads = pltpu.make_async_copy(grad_normed, grad_middle, load_sem.at[3])
-    for copy in (load_parts, load_grads, load_o, load_own):
-        copy.start()
-    greet([x_dev, y_dev], [])
-    summed = PlaneSum(parts, ones, twos, sum_sems, x_dev, y_dev)
-    load_parts.wait()
-    for copy in summed.far + summed.near:
-        copy.start()
+def fold(value):
+    return jnp.sum(value, axis=0, keepdims=True)
+
+
+def branch_kernel(grads, grad_normed, middle, gains, context, weights, layer, layer_out, grad_branch, grad_context,
+                  grad_o, gain_rows, weight, stage, load_sem, out_sem):
+    length, width = middle.shape[0], D + 2 * KW
+    load_o = pltpu.make_async_copy(weights.at[:, pl.ds(width, D)], weight, load_sem.at[0])
+    load_o.start()
     gain_rows[...] = jnp.zeros_like(gain_rows)
 
-    def fold(value):
-        return jnp.sum(value, axis=0, keepdims=True)
-
     def middle_grads(r):
-        rows, arrived = middle[r], grad_middle[r]
+        rows, arrived = middle[r], grad_normed[r]
         inverse = lax.rsqrt(jnp.mean(rows * rows, axis=-1, keepdims=True) + norm_eps)
         gain_rows[1:2, :] += fold(arrived * rows * inverse)
         weighted = arrived * gains[1:2, :]
         inner = jnp.mean(weighted * rows, axis=-1, keepdims=True)
         value = grads[r].astype(f32) + inverse * weighted - rows * (inverse * inverse * inverse * inner)
-        grad_middle[r] = value
         grad_branch[r] = value.astype(bf16)
-
-    load_grads.wait()
+        layer_out[r] = (rows + layer[r].astype(f32)).astype(bf16)
+
     by_rows(length, middle_grads)
     load_o.wait()
 
     def context_step(i, carry):
         tile = tile_at(i, 512)
-        grad_context[:, tile] = dot_t(grad_branch[...], weight[tile, 0:D]).astype(bf16)
+        grad_context[:, tile] = dot_t(grad_branch[...], weight[tile, :]).astype(bf16)
         return carry
 
     lax.fori_loop(0, D // 512, context_step, 0)
-    load_q.start()
-    steps = D // 256
-
-    def weight_grads(left, right, target, columns, which):
-        def out(i, slot):
-            return pltpu.make_async_copy(
-                stage.at[slot, :, pl.ds(0, columns)], target.at[tile_at(i, 256), pl.ds(0, columns)], out_sem.at[which, slot]
-            )
-
-        def step(i, carry):
-            slot = i % 2
-
-            @pl.when(i >= 2)
-            def _():
-                out(i - 2, slot).wait()
-
-            stage[slot, :, 0:columns] = dot_tn(left[:, tile_at(i, 256)], right[...]).astype(bf16)
-            out(i, slot).start()
-            return carry
-
-        lax.fori_loop(0, steps, step, 0)
-        for i in (steps - 2, steps - 1):
-            out(i, i % 2).wait()
-
-    weight_grads(context, grad_branch, grad_o, D, 0)
+    steps = D // 512
+
+    def out(i, slot):
+        return pltpu.make_async_copy(stage.at[slot], grad_o.at[tile_at(i, 512)], out_sem.at[slot])
+
+    def step(i, carry):
+        slot = i % 2
+
+        @pl.when(i >= 2)
+        def _():
+            out(i - 2, slot).wait()
+
+        stage[slot] = dot_tn(context[:, tile_at(i, 512)], grad_branch[...]).astype(bf16)
+        out(i, slot).start()
+        return carry
+
+    lax.fori_loop(0, steps, step, 0)
+    out(steps - 2, 0).wait()
+    out(steps - 1, 1).wait()
+
+
+def branch(grads, grad_normed, middle, gains, context, weights, layer):
+    length = middle.shape[0]
+    dma = pltpu.SemaphoreType.DMA
+    vmem, hbm = pl.BlockSpec(memory_space=pltpu.VMEM), pl.BlockSpec(memory_space=pl.ANY)
+    rows = jax.ShapeDtypeStruct((length, D), bf16)
+    return pl.pallas_call(
+        branch_kernel,
+        out_shape=(rows, rows, rows, jax.ShapeDtypeStruct((D, D), bf16), jax.ShapeDtypeStruct((8, D), f32)),
+        in_specs=[vmem] * 5 + [hbm, vmem],
+        out_specs=(vmem, vmem, vmem, hbm, vmem),
+        scratch_shapes=[pltpu.VMEM((D, D), bf16), pltpu.VMEM((2, 512, D), bf16), dma((1,)), dma((2,))],
+        compiler_params=pltpu.CompilerParams(vmem_limit_bytes=feed_vmem_limit),
+        cost_estimate=cost(22),
+        name="branch",
+    )(grads, grad_normed, middle, gains, context, weights, layer)
+
+
+def backward_kernel(lines, x, normed_one, qkv, grad_context, log_totals, gains, cosine, sine, seg_col, seg_row, gain_two,
+                    grad_o, branch_hbm, weights, input_grad, out_o, out_q, weight, grad_proj, grad_one, gain_rows,
+                    gain_columns, staged, *refs):
+    groups = [refs[i * 2 : i * 2 + 2] for i in range(6)] + [(out_o, out_q)]
+    scatter_sems, (load_sem, weight_sem) = refs[12:20], refs[20:]
+    scatter = Scatter(lines, groups, scatter_sems)
+    z, c, f = place()
+    length, width = x.shape[0], D + 2 * KW
+    order = scatter.order
+    rows = scatter.rows
+
+    def load(d):
+        return pltpu.make_async_copy(grad_o.at[d, c], scatter.sums[0].at[d], load_sem.at[d])
+
+    def load_weight(i):
+        tile = pl.ds(i * 512, 512)
+        return pltpu.make_async_copy(weights.at[tile, pl.ds(0, width)], weight.at[i % 2], weight_sem.at[i % 2])
+
+    for d in order:
+        scatter.to_core(0, d, grad_o.at[d, 1 - c]).start()
+        load(d).start()
+    load_branch = pltpu.make_async_copy(branch_hbm, input_grad, load_sem.at[lines])
+    load_branch.start()
+    load_weight(0).start()
+    load_weight(1).start()
+    gain_rows[...] = gain_two[...]
+
+    def between(group):
+        if group == 0:
+            for d in order:
+                load(d).wait()
+                scatter.over_core(0, d)
+        elif group == 1:
+            scatter.over_first(0, order[0])
+            scatter.over_first(0, order[1])
+        elif group == 2:
+            for d in order[2:]:
+                scatter.over_first(0, d)
+        else:
+            scatter.over_second(0, order[0])
+
     allowed = mask_keys_rows(seg_col[...], seg_row[...], length)
-    attend_heads_grad(qkv, grad_context, log_totals, grad_proj, allowed, cosine[...], sine[...])
-    summed.pass_on()
-    weight_grads(normed_one, grad_proj, grad_q, width, 1)
-    load_q.wait()
-
-    def normed_step(i, carry):
-        tile = tile_at(i, 512)
-        grad_one[:, tile] = dot_t(grad_proj[...], weight[tile, :])
-        return carry
-
-    lax.fori_loop(0, D // 512, normed_step, 0)
+    attend_heads_grad(
+        qkv, grad_context, log_totals, grad_proj, allowed, cosine[...], sine[...], between if lines > 1 else None
+    )
+    for i in range(D // 512):
+        load_weight(i).wait()
+        grad_one[:, i * 512 : (i + 1) * 512] = dot_t(grad_proj[...], weight[i % 2])
+        if i + 2 < D // 512:
+            load_weight(i + 2).start()
+    load_branch.wait()
 
     def input_grads(r):
-        rows, arrived = x[r].astype(f32), grad_one[r]
-        inverse = lax.rsqrt(jnp.mean(rows * rows, axis=-1, keepdims=True) + norm_eps)
-        gain_rows[0:1, :] += fold(arrived * rows * inverse)
+        values, arrived = x[r].astype(f32), grad_one[r]
+        inverse = lax.rsqrt(jnp.mean(values * values, axis=-1, keepdims=True) + norm_eps)
+        gain_rows[0:1, :] += fold(arrived * values * inverse)
         weighted = arrived * gains[0:1, :]
-        inner = jnp.mean(weighted * rows, axis=-1, keepdims=True)
-        value = grad_middle[r] + inverse * weighted - rows * (inverse * inverse * inverse * inner)
-        input_grad[r] = value.astype(bf16)
+        inner = jnp.mean(weighted * values, axis=-1, keepdims=True)
+        value = inverse * weighted - values * (inverse * inverse * inverse * inner)
+        input_grad[r] = (input_grad[r].astype(f32) + value).astype(bf16)
 
     by_rows(length, input_grads)
     for i in range(D // 128):
-        rows = pl.ds(i * 128, 128)
-        square = jnp.concatenate([gain_rows[:, rows], jnp.zeros((120, 128), f32)], axis=0)
-        gain_columns[rows, :] = square.T.astype(bf16)
-    gains_out = pltpu.make_async_copy(gain_columns, grad_q.at[:, pl.ds(width, 128)], load_sem.at[0])
-    gains_out.start()
-
-    def add_layer(r, value):
-        layer_out[r] = (middle[r] + own_layer[r].astype(f32) + value).astype(bf16)
-
-    load_own.wait()
-    summed.finish(add_layer)
-    gains_out.wait()
-
-
-def backward(x, grads, grad_normed, middle, gains, cosine, sine, seg_col, seg_row, normed_one, qkv, context,
-             log_totals, weights, layer):
+        lanes = pl.ds(i * 128, 128)
+        square = jnp.concatenate([gain_rows[:, lanes], jnp.zeros((120, 128), f32)], axis=0)
+        gain_columns[lanes, :] = square.T.astype(bf16)
+
+    def blocks(d, core):
+        start = pl.multiple_of((2 * d + core) * (4 * rows), 128)
+        tile = pl.ds(start, 4 * rows)
+        value = dot_tn(normed_one[:, tile], grad_proj[...]).astype(bf16)
+        return value.reshape(4, rows, width), gain_columns[tile, :].reshape(4, rows, 128)
+
+    def put(target, value):
+        target[:, :, 0:width] = value[0]
+        target[:, :, width:] = value[1]
+
+    def staged_copy(j):
+        return scatter.to_core(1, order[j], staged.at[j % 2])
+
+    for j, d in enumerate(order):
+        if j >= 2:
+            staged_copy(j - 2).wait_send()
+        put(staged.at[j % 2], blocks(d, 1 - c))
+        staged_copy(j).start()
+        put(scatter.sums[1].at[d], blocks(d, c))
+        if j:
+            scatter.over_core(1, order[j - 1])
+        if j == 1:
+            scatter.over_second(0, order[1])
+    scatter.over_core(1, order[-1])
+    for d in order[2:]:
+        scatter.over_second(0, d)
+    for j in range(len(order) + 1):
+        if j < len(order):
+            scatter.over_first(1, order[j])
+        if j:
+            scatter.over_second(1, order[j - 1])
+    for d in order:
+        scatter.to_core(0, d, grad_o.at[d, 1 - c]).wait_send()
+    for j in range(max(0, len(order) - 2), len(order)):
+        staged_copy(j).wait_send()
+    scatter.finish()
+
+
+def backward(x, normed_one, qkv, grad_context, log_totals, gains, cosine, sine, seg_col, seg_row, gain_two, grad_o,
+             grad_branch, weights, n_dp, n_tp):
     length = x.shape[0]
+    lines, rows = n_dp // 2, D // (n_dp * n_tp)
     width = D + 2 * KW
     dma = pltpu.SemaphoreType.DMA
     vmem, hbm = pl.BlockSpec(memory_space=pltpu.VMEM), pl.BlockSpec(memory_space=pl.ANY)
-    sum_buffers, sum_sems = plane_sum_scratch(length, D)
+    buffers, sems = scatter_scratch(lines, n_tp, rows, (D, width + 128))
     return pl.pallas_call(
-        backward_kernel,
+        functools.partial(backward_kernel, lines),
         out_shape=(
             jax.ShapeDtypeStruct((length, D), bf16),
-            jax.ShapeDtypeStruct((length, D), bf16),
-            jax.ShapeDtypeStruct((D, D), bf16),
-            jax.ShapeDtypeStruct((D, width + 128), bf16),
+            jax.ShapeDtypeStruct((rows, D), f32),
+            jax.ShapeDtypeStruct((rows, width + 128), f32),
         ),
-        in_specs=[vmem, vmem, hbm] + [vmem] * 10 + [hbm] * 2,
-        out_specs=(vmem, vmem, hbm, hbm),
+        in_specs=[vmem] * 11 + [hbm] * 3,
+        out_specs=(vmem,) * 3,
         scratch_shapes=[
-            pltpu.VMEM((D, width), bf16), pltpu.VMEM((length, D), f32), pltpu.VMEM((length, D), bf16),
-            pltpu.VMEM((length, D), bf16), pltpu.VMEM((length, width), bf16), pltpu.VMEM((length, D), f32),
-            pltpu.VMEM((8, D), f32), pltpu.VMEM((D, 128), bf16), pltpu.VMEM((2, 256, width), bf16),
-            pltpu.VMEM((length, D), bf16),
+            pltpu.VMEM((2, 512, width), bf16), pltpu.VMEM((length, width), bf16), pltpu.VMEM((length, D), f32),
+            pltpu.VMEM((8, D), f32), pltpu.VMEM((D, 128), bf16), pltpu.VMEM((2, n_tp, rows, width + 128), bf16),
         ]
-        + sum_buffers + sum_sems + [dma((4,)), dma((2, 2))],
+        + buffers + sems + [dma((lines + 1,)), dma((2,))],
         compiler_params=pltpu.CompilerParams(
             collective_id=7, has_side_effects=True, vmem_limit_bytes=feed_vmem_limit
         ),
-        cost_estimate=cost(65),
+        cost_estimate=cost(105),
         name="backward",
-    )(x, grads, grad_normed, middle, gains, cosine, sine, seg_col, seg_row, normed_one, qkv, context, log_totals,
-      weights, layer)
+    )(x, normed_one, qkv, grad_context, log_totals, gains, cosine, sine, seg_col, seg_row, gain_two,
+      grad_o.reshape(lines, 2, n_tp, rows, D), grad_branch, weights)
 
 
 def norm_kernel(n_dp, n_tp, parts, qkv, out, down, mlp, total, got, held, got_dp, got_tp, send, recv, total_send,
@@ -1279,28 +1340,37 @@
             dma(()),
         ],
         compiler_params=pltpu.CompilerParams(
-            collective_id=8, has_side_effects=True, vmem_limit_bytes=vmem_limit
+            collective_id=8, has_side_effects=True, vmem_limit_bytes=feed_vmem_limit
         ),
         cost_estimate=cost(35),
         name="norm_parts",
     )(parts, qkv, out, down)
 
 
-def adam_kernel(total, *refs):
+def adam_kernel(total, gain_block, *refs):
     scale = clip_norm / jnp.maximum(jnp.sqrt(total[0:1, 0:1]), clip_norm)
     grads, refs = refs[:4], refs[4:]
-    states, news = refs[:12], refs[12:]
-    for i in range(4):
-        gradient = grads[i][...].astype(f32) * scale
+    states, news = refs[:15], refs[15:]
+
+    def update(i, gradient, rate, decay):
         new = adam_update(
-            states[3 * i][...], gradient, states[3 * i + 1][...], states[3 * i + 2][...], matrix_rate, weight_decay
+            states[3 * i][...], gradient * scale, states[3 * i + 1][...], states[3 * i + 2][...], rate, decay
         )
         for k in range(3):
             news[3 * i + k][...] = new[k]
 
+    for i in range(4):
+        update(i, grads[i][...].astype(f32), matrix_rate, weight_decay)
+
+    @pl.when(pl.program_id(0) == 0)
+    def _():
+        rows = gain_block.shape[0]
+        square = jnp.concatenate([gain_block[...], jnp.zeros((128 - rows, 128), f32)], axis=0)
+        update(4, square.T[0:2, 0:rows], gain_rate, 0.0)
+
 
 def adam_all(total, grads, states):
-    shapes = [state[0].shape for state in states]
+    shapes = [state[0].shape for state in states[:4]]
 
     def block(shape, steps):
         rows, columns = shape
@@ -1313,98 +1383,122 @@
     steps = 8 if all(block(shape, 8) for shape in shapes) else 4
     specs = [block(shape, steps) for shape in shapes]
     flat = [array for state in states for array in state]
-    state_specs = [spec for spec in specs for _ in range(3)]
+    gains = pl.BlockSpec(states[4][0].shape, lambda i: (0, 0))
+    state_specs = [spec for spec in specs + [gains] for _ in range(3)]
+    last = grads[0].shape[1] // 128 - 1
+    gain_block = pl.BlockSpec((grads[0].shape[0], 128), lambda i: (0, last))
     return pl.pallas_call(
         adam_kernel,
         grid=(steps,),
         out_shape=[jax.ShapeDtypeStruct(array.shape, f32) for array in flat],
-        in_specs=[pl.BlockSpec((8, 128), lambda i: (0, 0))] + specs + state_specs,
+        in_specs=[pl.BlockSpec((8, 128), lambda i: (0, 0)), gain_block] + specs + state_specs,
         out_specs=state_specs,
-        compiler_params=pltpu.CompilerParams(vmem_limit_bytes=vmem_limit),
+        compiler_params=pltpu.CompilerParams(vmem_limit_bytes=feed_vmem_limit),
         cost_estimate=cost(14),
         name="adam",
-    )(total, *grads, *flat)
-
-
-def feed_kernel(n_hbm, g_hbm, wm_hbm, wd_hbm, grad_normed, grad_down, grad_mlp, layer, n, g, wm, wd, gh, act,
-                stage, parts, ones, twos, *sems):
-    sum_sems, (load_sem, out_sem) = sems[:4], sems[4:]
+    )(total, grads[0], *grads, *flat)
+
+
+def feed_front_kernel(n_hbm, g_hbm, wm_hbm, wd_hbm, gh_hbm, grad_down, layer_sum, n, g, wm, wd, act, gh, stage, parts,
+                      ones, twos, *sems):
+    sum_sems, (load_sem, weight_sem, out_sem) = sems[:4], sems[4:]
     z, c, f = place()
     x_dev, y_dev = device(z, c, flipped(f, 1)), device(z, c, flipped(f, 2))
     tokens = n.shape[0]
     length = tokens // 4
     ff = wd.shape[0]
-    loads = [
-        pltpu.make_async_copy(src, dst, load_sem.at[i])
-        for i, (src, dst) in enumerate(((n_hbm, n), (wm_hbm, wm), (wd_hbm, wd), (g_hbm, g)))
-    ]
-    for copy in loads:
-        copy.start()
+    order = (3, 1, 2, 0)
+
+    def rows_of(k):
+        return pl.ds(k * length, length)
+
+    load_n = [pltpu.make_async_copy(n_hbm.at[rows_of(k)], n.at[rows_of(k)], load_sem.at[0, k]) for k in range(4)]
+    load_g = [pltpu.make_async_copy(g_hbm.at[rows_of(k)], g.at[rows_of(k)], load_sem.at[1, k]) for k in range(4)]
+    tiles = [(start, min(256, ff - start)) for start in range(0, ff, 256)]
+    load_w = []
+    for t, (start, size) in enumerate(tiles):
+        gate, up = pl.ds(start, size), pl.ds(ff + start, size)
+        load_w.append(
+            [
+                pltpu.make_async_copy(wm_hbm.at[:, gate], wm.at[:, gate], weight_sem.at[0, t]),
+                pltpu.make_async_copy(wm_hbm.at[:, up], wm.at[:, up], weight_sem.at[1, t]),
+                pltpu.make_async_copy(wd_hbm.at[gate], wd.at[gate], weight_sem.at[2, t]),
+            ]
+        )
+    load_n[order[0]].start()
+    load_g[order[0]].start()
+    for copies in load_w:
+        for copy in copies:
+            copy.start()
+    for k in order[1:]:
+        load_n[k].start()
+        load_g[k].start()
     greet([x_dev, y_dev], [])
-    for copy in loads:
-        copy.wait()
-
-    def hidden(rows, lanes, up_lanes):
+    summed = PlaneSum(parts, ones, twos, sum_sems, x_dev, y_dev)
+
+    def hidden(k, slot, lanes, up_lanes):
+        rows = rows_of(k)
         gate = dot_n(n[rows, :], wm[:, lanes])
         up = dot_n(n[rows, :], wm[:, up_lanes])
         grad = dot_t(g[rows, :], wd[lanes, :])
         sigmoid = jax.nn.sigmoid(gate)
         silu = gate * sigmoid
         act[rows, lanes] = (silu * up).astype(bf16)
-        gh[rows, lanes] = (grad * up * sigmoid * (1.0 + gate * (1.0 - sigmoid))).astype(bf16)
-        gh[rows, up_lanes] = (grad * silu).astype(bf16)
-
+        gh[slot, :, lanes] = (grad * up * sigmoid * (1.0 + gate * (1.0 - sigmoid))).astype(bf16)
+        gh[slot, :, up_lanes] = (grad * silu).astype(bf16)
+
+    def hidden_out(i):
+        return pltpu.make_async_copy(gh.at[i % 2], gh_hbm.at[rows_of(order[i])], out_sem.at[1, i % 2])
+
+    for i, k in enumerate(order):
+        load_n[k].wait()
+        load_g[k].wait()
+        if i >= 2:
+            hidden_out(i - 2).wait()
+        if i == 0:
+            for copies, (start, size) in zip(load_w, tiles):
+                for copy in copies:
+                    copy.wait()
+                hidden(k, 0, pl.ds(start, size), pl.ds(ff + start, size))
+        else:
+
+            def hidden_step(t, carry):
+                hidden(k, i % 2, tile_at(t, 256), tile_at(t, 256, ff))
+                return carry
+
+            lax.fori_loop(0, ff // 256, hidden_step, 0)
+            if ff % 256:
+                start, size = tiles[-1]
+                hidden(k, i % 2, pl.ds(start, size), pl.ds(ff + start, size))
+        hidden_out(i).start()
+
+        def layer_step(t, carry):
+            value = dot_n(act[rows_of(k), :], wd[:, tile_at(t, 512)]).astype(bf16)
+            if k:
+                parts[k - 1, :, tile_at(t, 512)] = value
+            else:
+                layer_sum[:, tile_at(t, 512)] = value
+            return carry
+
+        lax.fori_loop(0, D // 512, layer_step, 0)
+        if k == 3:
+            for copy in summed.far:
+                copy.start()
+        elif k:
+            summed.near[k - 1].start()
+        if k == 2:
+            summed.pass_on()
     wide = ff // 256
-
-    def hidden_step(i, carry):
-        rows = pl.ds(pl.multiple_of((i % 4) * length, 16), length)
-        hidden(rows, tile_at(i // 4, 256), tile_at(i // 4, 256, ff))
-        return carry
-
-    lax.fori_loop(0, 4 * wide, hidden_step, 0)
-    for k in range(4):
-        if ff % 256:
-            hidden(pl.ds(k * length, length), pl.ds(wide * 256, ff % 256), pl.ds(ff + wide * 256, ff % 256))
-
-    def back(k, store):
-        def step(i, carry):
-            tile = tile_at(i, 1024)
-            store(tile, dot_t(gh[k * length : (k + 1) * length, :], wm[tile, :]))
-            return carry
-
-        lax.fori_loop(0, D // 1024, step, 0)
-
-    def back_parts(k):
-        def store(tile, value):
-            parts[k - 1, :, tile] = value.astype(bf16)
-
-        back(k, store)
-
-    summed = PlaneSum(parts, ones, twos, sum_sems, x_dev, y_dev)
-    back_parts(3)
-    for copy in summed.far:
-        copy.start()
-    back_parts(1)
-    summed.near[0].start()
-    back_parts(2)
-    summed.near[1].start()
-
-    def store_own(tile, value):
-        grad_normed[:, tile] = value
-
-    back(0, store_own)
 
     def down_out(i, slot, width=256):
         rows = pl.ds(pl.multiple_of((i // 2) * 256, 128), width)
         lanes = tile_at(i % 2, D // 2)
-        return pltpu.make_async_copy(
-            stage.at[slot, pl.ds(0, width), pl.ds(0, D // 2)], grad_down.at[rows, lanes], out_sem.at[0, slot]
-        )
+        return pltpu.make_async_copy(stage.at[slot, pl.ds(0, width)], grad_down.at[rows, lanes], out_sem.at[0, slot])
 
     def down_tile(i, slot, width=256):
         lanes = tile_at(i % 2, D // 2)
         value = dot_tn(act[:, pl.ds(pl.multiple_of((i // 2) * 256, 128), width)], g[:, lanes])
-        stage[slot, 0:width, 0 : D // 2] = value.astype(bf16)
+        stage[slot, 0:width] = value.astype(bf16)
         down_out(i, slot, width).start()
 
     def down_step(i, carry):
@@ -1422,15 +1516,58 @@
         down_out(2 * wide - 2 + slot, slot).wait()
         if ff % 256:
             down_tile(2 * wide + slot, slot, ff % 256)
+    for slot in range(2):
+        if ff % 256:
             down_out(2 * wide + slot, slot, ff % 256).wait()
-
+        hidden_out(2 + slot).wait()
+
+    def add_layer(r, value):
+        layer_sum[r] = (layer_sum[r].astype(f32) + value).astype(bf16)
+
+    summed.finish(add_layer)
+
+
+def feed_back_kernel(gh_hbm, wm_hbm, n_hbm, grad_normed, grad_mlp, gh, wm, n, stage, parts, ones, twos, *sems):
+    sum_sems, (load_sem, out_sem) = sems[:4], sems[4:]
+    z, c, f = place()
+    x_dev, y_dev = device(z, c, flipped(f, 1)), device(z, c, flipped(f, 2))
+    tokens = n.shape[0]
+    length = tokens // 4
+    ff = gh.shape[1] // 2
+    order = (3, 1, 2, 0)
+    rows_of = [pl.ds(k * length, length) for k in range(4)]
+    load_gh = [pltpu.make_async_copy(gh_hbm.at[rows_of[k]], gh.at[rows_of[k]], load_sem.at[0, k]) for k in range(4)]
+    wide_tiles = [pl.ds(start, 1024) for start in range(0, D, 1024)]
+    load_w = [
+        pltpu.make_async_copy(wm_hbm.at[tile], wm.at[tile], load_sem.at[1, t]) for t, tile in enumerate(wide_tiles)
+    ]
+    load_n = pltpu.make_async_copy(n_hbm, n, load_sem.at[1, 3])
+    for copy in [load_gh[order[0]]] + load_w + [load_gh[k] for k in order[1:]] + [load_n]:
+        copy.start()
+    greet([x_dev, y_dev], [])
+    summed = PlaneSum(parts, ones, twos, sum_sems, x_dev, y_dev)
+    for k in order:
+        load_gh[k].wait()
+        for t, tile in enumerate(wide_tiles):
+            if k == order[0]:
+                load_w[t].wait()
+            value = dot_t(gh[rows_of[k], :], wm[tile, :])
+            if k:
+                parts[k - 1, :, tile] = value.astype(bf16)
+            else:
+                grad_normed[:, tile] = value
+        if k == 3:
+            for copy in summed.far:
+                copy.start()
+        elif k:
+            summed.near[k - 1].start()
     summed.pass_on()
+    load_n.wait()
+    steps = 2 * D // 512
 
     def mlp_out(i, slot):
-        rows = pl.ds(pl.multiple_of((i // 2) * 256, 256), 256)
-        return pltpu.make_async_copy(
-            stage.at[slot, :, pl.ds(0, ff)], grad_mlp.at[rows, tile_at(i % 2, ff)], out_sem.at[1, slot]
-        )
+        rows = pl.ds(pl.multiple_of((i // 2) * 512, 512), 512)
+        return pltpu.make_async_copy(stage.at[slot], grad_mlp.at[rows, tile_at(i % 2, ff)], out_sem.at[slot])
 
     def mlp_step(i, carry):
         slot = i % 2
@@ -1439,60 +1576,64 @@
         def _():
             mlp_out(i - 2, slot).wait()
 
-        value = dot_tn(n[:, tile_at(i // 2, 256)], gh[:, tile_at(i % 2, ff)])
-        stage[slot, :, 0:ff] = value.astype(bf16)
+        stage[slot] = dot_tn(n[:, tile_at(i // 2, 512)], gh[:, tile_at(i % 2, ff)]).astype(bf16)
         mlp_out(i, slot).start()
         return carry
 
-    lax.fori_loop(0, 2 * D // 256, mlp_step, 0)
-    mlp_out(2 * D // 256 - 2, 0).wait()
-    mlp_out(2 * D // 256 - 1, 1).wait()
-
-    def layer_step(i, carry):
-        g[:, tile_at(i, 256)] = dot_n(act[...], wd[:, tile_at(i, 256)]).astype(bf16)
-        return carry
-
-    lax.fori_loop(0, D // 256, layer_step, 0)
-    layer_out = pltpu.make_async_copy(g, layer, load_sem.at[0])
-    layer_out.start()
+    lax.fori_loop(0, steps, mlp_step, 0)
 
     def add_normed(r, value):
         grad_normed[r] += value
 
     summed.finish(add_normed)
-    layer_out.wait()
+    mlp_out(steps - 2, 0).wait()
+    mlp_out(steps - 1, 1).wait()
 
 
 def feed(normed_all, grads_all, mlp_cols, down_cols):
     tokens, ff = 4 * normed_all.shape[1], down_cols.shape[0]
     length = tokens // 4
     dma = pltpu.SemaphoreType.DMA
+    vmem, hbm = pl.BlockSpec(memory_space=pltpu.VMEM), pl.BlockSpec(memory_space=pl.ANY)
     sum_buffers, sum_sems = plane_sum_scratch(length, D)
-    vmem, hbm = pl.BlockSpec(memory_space=pltpu.VMEM), pl.BlockSpec(memory_space=pl.ANY)
-    return pl.pallas_call(
-        feed_kernel,
+    normed_all = normed_all.reshape(tokens, D)
+
+    def buffers(*shapes):
+        return [pltpu.VMEM(shape, bf16) for shape in shapes] + sum_buffers + sum_sems
+
+    grad_hidden, grad_down, layer_sum = pl.pallas_call(
+        feed_front_kernel,
         out_shape=(
-            jax.ShapeDtypeStruct((length, D), f32),
+            jax.ShapeDtypeStruct((tokens, 2 * ff), bf16),
             jax.ShapeDtypeStruct((ff, D), bf16),
-            jax.ShapeDtypeStruct((D, 2 * ff), bf16),
-            jax.ShapeDtypeStruct((tokens, D), bf16),
+            jax.ShapeDtypeStruct((length, D), bf16),
         ),
         in_specs=[hbm] * 4,
-        out_specs=(vmem, hbm, hbm, hbm),
-        scratch_shapes=[
-            pltpu.VMEM(shape, bf16)
-            for shape in (
-                (tokens, D), (tokens, D), (D, 2 * ff), (ff, D), (tokens, 2 * ff), (tokens, ff),
-                (2, 256, max(ff, D // 2)),
-            )
-        ]
-        + sum_buffers + sum_sems + [dma((4,)), dma((2, 2))],
+        out_specs=(hbm, hbm, vmem),
+        scratch_shapes=buffers(
+            (tokens, D), (tokens, D), (D, 2 * ff), (ff, D), (tokens, ff), (2, length, 2 * ff), (2, 256, D // 2)
+        )
+        + [dma((2, 4)), dma((3, -(-ff // 256))), dma((2, 2))],
         compiler_params=pltpu.CompilerParams(
             collective_id=6, has_side_effects=True, vmem_limit_bytes=feed_vmem_limit
         ),
-        cost_estimate=cost(115),
-        name="feed",
-    )(normed_all.reshape(tokens, D), grads_all.reshape(tokens, D), mlp_cols, down_cols)
+        cost_estimate=cost(65),
+        name="feed_front",
+    )(normed_all, grads_all.reshape(tokens, D), mlp_cols, down_cols)
+    grad_normed, grad_mlp = pl.pallas_call(
+        feed_back_kernel,
+        out_shape=(jax.ShapeDtypeStruct((length, D), f32), jax.ShapeDtypeStruct((D, 2 * ff), bf16)),
+        in_specs=[hbm] * 3,
+        out_specs=(vmem, hbm),
+        scratch_shapes=buffers((tokens, 2 * ff), (D, 2 * ff), (tokens, D), (2, 512, ff))
+        + [dma((2, 4)), dma((2,))],
+        compiler_params=pltpu.CompilerParams(
+            collective_id=9, has_side_effects=True, vmem_limit_bytes=feed_vmem_limit
+        ),
+        cost_estimate=cost(60),
+        name="feed_back",
+    )(grad_hidden, mlp_cols, normed_all)
+    return grad_normed, grad_down, grad_mlp, layer_sum
 
 
 def local(
@@ -1549,7 +1690,6 @@
     inverse_two = lax.rsqrt(jnp.mean(middle * middle, axis=-1, keepdims=True) + norm_eps)
     if n_tp == 4:
         grad_normed_two, grad_down, grad_mlp, layer_parts = feed(normed_all, grads_all, mlp_cols, down_cols)
-        layer_parts = layer_parts.reshape(n_tp, length, D)
     else:
         normed_two = (middle * inverse_two * gain_two).astype(bf16)
         normed_all = plane_gather(normed_two, n_tp)
@@ -1575,11 +1715,13 @@
     mlp_sum = lax.psum_scatter(grad_mlp, "dp", scatter_dimension=0, tiled=True).reshape(n_tp, rows, 2 * ff)
 
     if n_tp == 4:
-        layer_out, input_grad, grad_out, grad_qkv = backward(
-            inputs, cotangent, grad_normed_two, middle, gains_full, cosine, sine, seg_col, seg_row, normed_one, qkv,
-            attended, log_totals, attn_full, layer_parts,
+        layer_out, grad_branch, grad_context, grad_out, gain_two_rows = branch(
+            cotangent, grad_normed_two, middle, gains_full, attended, attn_full, layer_parts
         )
-        out_sum, qkv_sum = scatter_all([grad_out, grad_qkv], n_dp, n_tp)
+        input_grad, out_sum, qkv_sum = backward(
+            inputs, normed_one, qkv, grad_context, log_totals, gains_full, cosine, sine, seg_col, seg_row,
+            gain_two_rows, grad_out, grad_branch, attn_full, n_dp, n_tp,
+        )
         mlp_sum, total = norm_parts(mlp_sum, qkv_sum, out_sum, down_sum, n_dp, n_tp)
     else:
         layer_out = middle + layer_parts[0].astype(f32)
@@ -1614,20 +1756,16 @@
         squares = jnp.sum(qkv_sum * qkv_sum) + jnp.sum(out_sum * out_sum) + jnp.sum(mlp_sum * mlp_sum)
         squares = squares + jnp.sum(jnp.square(down_sum.astype(f32)))
         total = total_over_devices(squares, n_dp, n_tp)
-    gains_sum = qkv_sum[:, D + 2 * KW : D + 2 * KW + 2].T
     grad_norm = jnp.sqrt(total[0, 0])
-    clip_scale = clip_norm / jnp.maximum(grad_norm, clip_norm)
     states = (
         (qkv_weight, qkv_first, qkv_second),
         (out_weight, out_first, out_second),
         (mlp_weight, mlp_first, mlp_second),
         (down_weight, down_first, down_second),
+        (norm_gains, gains_first, gains_second),
     )
     stepped = adam_all(total, (qkv_sum, out_sum, mlp_sum, down_sum), states)
-    gains_out = adam_update(
-        norm_gains, gains_sum * clip_scale, gains_first, gains_second, gain_rate, 0.0
-    )
-    news = [[*stepped[i::3], gains_out[i]] for i in range(3)]
+    news = [stepped[i::3] for i in range(3)]
     return (layer_out, input_grad, grad_norm, *news[0], *news[1], *news[2])
 
 

time: 643 us -> 614 us (0.955)
  Pallas kernels: 601 us -> 581 us
  local copies, waits for them, and re-layouts: 15 us -> 5.32 us
    pallas_call x3 -> x4, Pallas kernels: 345 us -> 319 us  [the longest x1 155 us: backward(): pl.pallas_call(functools.partial(backward_kernel, lines), out_shape=(jax....]
    unnamed x50 -> x7, local copies, waits for them, and re-layouts: 12.8 us -> 1.16 us
  transfers between devices with their start and end apart: 3 -> 3, of which waited for: 0 -> 0; matrix products, arithmetic and copies ran while one was open for 1% -> 1% of each run, Pallas kernels for 53% -> 57%
where the time goes in v5:
time: 614 us; the launch traced here: 610 us
  Pallas kernels  581 us (95%)
  between operations  16.9 us (3%)
  other arithmetic  6.65 us (1%)
    pallas_call x1, Pallas kernels, backward(): pl.pallas_call(functools.partial(backward_kernel, lines), out_shape=(jax....  155 us
    pallas_call x1, Pallas kernels, forward(): pl.pallas_call(forward_kernel, out_shape=(jax.ShapeDtypeStruct((length, w...  110 us
    pallas_call x1, Pallas kernels, gather_all(): pl.pallas_call(functools.partial(gather_kernel, lines), out_shape=(jax.Sh...  103 us
    pallas_call x1, Pallas kernels, feed(): pl.pallas_call(feed_front_kernel, out_shape=(jax.ShapeDtypeStruct((tokens...  81.2 us
    pallas_call x1, Pallas kernels, feed(): pl.pallas_call(feed_back_kernel, out_shape=(jax.ShapeDtypeStruct((length,...  61.4 us
    pallas_call x1, Pallas kernels, norm_parts(): pl.pallas_call(functools.partial(norm_kernel, n_dp, n_tp), out_shape=(jax...  30.5 us
    pallas_call x1, Pallas kernels, branch(): pl.pallas_call(branch_kernel, out_shape=(rows, rows, rows, jax.ShapeDtype...  21.1 us
    pallas_call x1, Pallas kernels, adam_all(): pl.pallas_call(adam_kernel, grid=(steps,), out_shape=[jax.ShapeDtypeStruc...  18.2 us
  transfers between devices with their start and end apart: 3, of which 0 were waited for; matrix products, arithmetic and copies ran while one was open for 1% of the time, Pallas kernels for 57%

profile of v5, /device:TPU:0, one launch (start us, length us, event | category | flops | bytes accessed | tf_op | source)
XLA Modules:
  0.0 610.1 jit_solution(2196700157973104851)
XLA Ops:
  7.2 0.0 copy-start
  7.2 0.0 all-gather.2.cloned.1.call-start
  7.2 0.8 convert.15
  8.0 0.1 copy.46
  8.1 1.1 convert.14
  9.2 1.1 convert.13
  10.3 0.0 copy-done
  10.4 0.1 convert_element_type.14.down
  10.5 0.0 copy-start.2
  10.5 103.3 %gather_all.1 = (bf16[4,2,4,64,4736]{4,3,2,1,0:T(8,128)(2,1)}, bf16[4,64,2816]{2,1,0:T(8,128)(2,1)}, bf16[4,2,176,2048]{3,2,1,0:T(8,128)(2,1)}) custom-call(bf16[64,4736]{1,0:T(8,128)(2,1)S(1)} %fusion.1.own, f32[64,11264]{1,0:T(8,128)} %refs_10_.1, bf16[176,2048]{1,0:T(8,128)(2,1)S(1)} %convert_element_type.14.down), custom_call_target="tpu_custom_call" | custom-call | bytes 369000000 | tf_op jit(solution)/shard_map/gather_all/pallas_call | solution.py:366
  113.8 0.0 all-gather.2.cloned.1.call-update
  113.8 0.0 reduce-scatter.5.cloned.1.call-start
  113.9 0.0 copy-done.2
  113.9 0.5 slice.24
  115.1 0.1 add_select_fusion
  115.2 0.3 reduce-window.9
  115.5 0.1 slice.27
  115.6 0.8 copy.49.seg_col
  116.4 1.1 convert_bitcast_fusion
  117.5 1.3 copy.48.gains
  118.8 0.1 slice_reduce_fusion
  119.0 0.1 fusion.4
  119.0 0.8 fusion.2
  119.8 1.1 pad_maximum_fusion
  120.9 110.1 %forward.1 = (bf16[384,2560]{1,0:T(8,128)(2,1)}, bf16[384,2048]{1,0:T(8,128)(2,1)}, f32[32,384]{1,0:T(8,128)}, f32[384,2048]{1,0:T(8,128)}, bf16[384,2048]{1,0:T...) custom-call(bf16[384,2048]{1,0:T(8,128)(2,1)} %x.5, bf16[384,2048]{1,0:T(8,128)(2,1)} %grads.3, ...), custom_call_target="tpu_custom_call" | custom-call | bytes 350550016 | tf_op jit(solution)/shard_map/forward/pallas_call | solution.py:916
  231.1 0.0 all-gather.2.cloned.1.call-done.wm_hbm
  231.1 81.2 %feed_front.1 = (bf16[1536,2816]{1,0:T(8,128)(2,1)}, bf16[1408,2048]{1,0:T(8,128)(2,1)}, bf16[384,2048]{1,0:T(8,128)(2,1)}) custom-call(bf16[1536,2048]{1,0:T(8,128)(2,1)} %bitcast.31, bf16[1536,2048]{1,0:T(8,128)(2,1)} %bitcast.34, bf16[2048,2816]{1,0:T(8,128)(2,1)} %all-gather.2.cloned.1.call-done.wm_hbm, bf16[1408,2048]{1,0:T(8,128)(2,1)} %bitcast.35), custom_call_target="tpu_custom_call" | custom-call | bytes 239850000 | tf_op jit(solution)/shard_map/feed_front/pallas_call | solution.py:1604
  312.3 0.0 reduce-scatter.5.cloned.1.call-update
  312.4 0.2 reduce-scatter.3.cloned.1.call-start
  312.6 61.4 %feed_back.1 = (f32[384,2048]{1,0:T(8,128)}, bf16[2048,2816]{1,0:T(8,128)(2,1)}) custom-call(bf16[1536,2816]{1,0:T(8,128)(2,1)} %get-tuple-element.63.gh_hbm, bf16[2048,2816]{1,0:T(8,128)(2,1)} %all-gather.2.cloned.1.call-done.wm_hbm, bf16[1536,2048]{1,0:T(8,128)(2,1)} %bitcast.32), custom_call_target="tpu_custom_call" | custom-call | bytes 221400000 | tf_op jit(solution)/shard_map/feed_back/pallas_call | solution.py:1623
  374.0 0.0 reduce-scatter.3.cloned.1.call-update
  374.0 21.1 %branch.1 = (bf16[384,2048]{1,0:T(8,128)(2,1)}, bf16[384,2048]{1,0:T(8,128)(2,1)}, bf16[384,2048]{1,0:T(8,128)(2,1)}, bf16[2048,2048]{1,0:T(8,128)(2,1)}, f32[8,2048]{1,0:T(8,128)}) custom-call(bf16[384,2048]{1,0:T(8,128)(2,1)} %grads.3, f32[384,2048]{1,0:T(8,128)} %get-tuple-element.64.grad_normed, f32[384,2048]{1,0:T(8,128)} %get-tuple-element.65.middle, ...), custom_call_target="tpu_custom_call" | custom-call | bytes 81180000 | tf_op jit(solution)/shard_map/branch/pallas_call | solution.py:1107
  395.1 155.0 %backward.1 = (bf16[384,2048]{1,0:T(8,128)(2,1)}, f32[64,2048]{1,0:T(8,128)}, f32[64,2688]{1,0:T(8,128)}) custom-call(bf16[384,2048]{1,0:T(8,128)(2,1)} %x.5, bf16[384,2048]{1,0:T(8,128)(2,1)} %get-tuple-element.69.normed_one, bf16[384,2560]{1,0:T(8,128)(2,1)} %get-tuple-element.70.qkv, bf16[384,2048]{1,0:T(8,128)(2,1)} %get-tuple-element.71.grad_context, ...), custom_call_target="tpu_custom_call" | custom-call | bytes 387449984 | tf_op jit(solution)/shard_map/backward/pallas_call | solution.py:1232
  550.1 0.0 reduce-scatter.5.cloned.1.call-done.down.refs_3_
  550.2 0.0 reduce-scatter.3.cloned.1.call-done
  550.2 30.5 %norm_parts.1 = (f32[64,11264]{1,0:T(8,128)}, f32[8,128]{1,0:T(8,128)}) custom-call(bf16[4,64,2816]{2,1,0:T(8,128)(2,1)} %bitcast.36, f32[64,2688]{1,0:T(8,128)} %get-tuple-element.78.qkv.gain_block.refs_0_, f32[64,2048]{1,0:T(8,128)} %get-tuple-element.79.out.refs_1_, bf16[176,2048]{1,0:T(8,128)(2,1)} %reduce-scatter.5.cloned.1.call-done.down.refs_3_), custom_call_target="tpu_custom_call" | custom-call | bytes 129150000 | tf_op jit(solution)/shard_map/norm_parts/pallas_call | solution.py:1333
  580.7 1.2 slice.29
  582.6 0.0 copy-start.1
  582.6 18.2 %adam.1 = (f32[64,2560]{1,0:T(8,128)}, f32[64,2560]{1,0:T(8,128)}, f32[64,2560]{1,0:T(8,128)}, f32[64,2048]{1,0:T(8,128)}, f32[64,2048]{1,0:T(8,128)}, /*index=5...) custom-call(f32[8,128]{1,0:T(8,128)} %get-tuple-element.81.total, ...), custom_call_target="tpu_custom_call" | custom-call | bytes 51660000 | tf_op jit(solution)/shard_map/adam/pallas_call | solution.py:1390
  600.8 0.0 copy-done.1
  600.8 1.1 copy.54
  (5 shorter events, 0.1 us)
Async XLA Ops:
  7.2 3.2 copy-start
  7.2 223.9 %all-gather.2.cloned.1.call-start = ((), (), s32[]{:S(2)}) async-start(), calls=%async_computation.2 | async-start | bytes 12976128 | tf_op jit(solution)/shard_map/all_gather | solution.py:1677
  10.5 103.4 %copy-start.2 = (s32[1,384]{1,0:T(1,128)S(1)}, s32[1,384]{1,0:T(1,128)}, u32[]{:S(2)}) copy-start(s32[1,384]{1,0:T(1,128)} %seg_row.3) | copy-start | bytes 4612
  113.8 436.3 %reduce-scatter.5.cloned.1.call-start = ((), (), s32[]{:S(2)}) async-start(), calls=%async_computation.4 | async-start | bytes 6488064 | tf_op jit(solution)/shard_map/reduce_scatter | solution.py:1714
  312.4 237.8 %reduce-scatter.3.cloned.1.call-start = ((), (), s32[]{:S(2)}) async-start(), calls=%async_computation.3 | async-start | bytes 12976128 | tf_op jit(solution)/shard_map/reduce_scatter | solution.py:1715
  582.6 18.2 %copy-start.1 = (bf16[384,2048]{1,0:T(8,128)(2,1)S(1)}, bf16[384,2048]{1,0:T(8,128)(2,1)}, u32[]{:S(2)}) copy-start(bf16[384,2048]{1,0:T(8,128)(2,1)} %get-tuple-element.122) | copy-start | bytes 4718596
Sparse Core Ops, SparseCore 0:
  113.9 108.4 all-gather.1
  312.5 65.2 reduce-scatter.4
  380.0 156.6 reduce-scatter.2

commit v6 on v5

--- a/solution.py
+++ b/solution.py
@@ -595,6 +595,16 @@
     lax.fori_loop(0, rows // 16, step, 0)
 
 
+def places_by_distance(z, lines):
+    tables = [
+        sorted(range(lines), key=lambda d: (-abs(d - here), min(d, lines - 1 - d), d)) for here in range(lines)
+    ]
+    power = 1
+    for bit in range(lines.bit_length() - 1):
+        power = power * (1 + (lines ** (1 << bit) - 1) * (z // (1 << bit) % 2))
+    return [sum(table[t] * lines**here for here, table in enumerate(tables)) // power % lines for t in range(lines)]
+
+
 class Scatter:
     def __init__(self, lines, groups, sems):
         self.sums, self.others, self.firsts, self.seconds, self.alongs, self.leaving, self.outs = groups
@@ -613,13 +623,7 @@
         greet([x_dev, y_dev, core_dev], [(self.has_left, left_dev), (self.has_right, right_dev)])
         halves = (pl.ds(0, self.half), pl.ds(self.half, self.half))
         near, self.next_near, step_dev = (fx, fy), (fy, fx), (x_dev, y_dev)
-        self.order = []
-        for t in reversed(range(lines)):
-            line = z
-            for b in range(lines.bit_length() - 1):
-                if t >> b & 1:
-                    line = flipped(line, 1 << b)
-            self.order.append(line)
+        self.order = places_by_distance(z, lines)
 
         def remote(src, dst, send, recv, dev):
             return pltpu.make_async_remote_copy(src, dst, send, recv, device_id=dev, device_id_type=MESH)
@@ -689,37 +693,52 @@
             self.two(a, d, way).start()
 
     def over_second(self, a, d):
-        sums, firsts, seconds, outs, z = self.sums[a], self.firsts[a], self.seconds[a], self.outs[a], self.z
+        sums, firsts, seconds, z = self.sums[a], self.firsts[a], self.seconds[a], self.z
         for way in range(2):
             self.one(a, d, way, 0).wait_recv()
             self.two(a, d, way).wait_recv()
 
-            def second_add(r):
-                there = self.there(r, way)
-                outs[there] = (
+            def total(r, there):
+                return (
                     sums[d, self.f, there].astype(f32)
                     + firsts[way, d, 0, r].astype(f32)
                     + seconds[way, d, r].astype(f32)
                 )
 
-            by_rows(self.half, second_add)
+            @pl.when(d == z)
+            def _():
+                def stay(r):
+                    there = self.there(r, way)
+                    self.outs[a][there] = total(r, there)
+
+                by_rows(self.half, stay)
+
+            @pl.when(d != z)
+            def _():
+                def leave(r):
+                    there = self.there(r, way)
+                    self.leaving[a][d, there] = total(r, there).astype(bf16)
+
+                by_rows(self.half, leave)
+
+    def over_line(self, a, d):
+        leaving, alongs, z = self.leaving[a], self.alongs[a], self.z
+
+        def add_arrived():
+            def step(r):
+                leaving[d, r] = (leaving[d, r].astype(f32) + alongs[d, r].astype(f32)).astype(bf16)
+
+            by_rows(self.rows, step)
 
         @pl.when((d > z) & (self.has_left == 1))
         def _():
             self.to_right(a, d).wait_recv()
-            self.add_along(a, d)
+            add_arrived()
 
         @pl.when((d < z) & (self.has_right == 1))
         def _():
             self.to_left(a, d, d).wait_recv()
-            self.add_along(a, d)
-
-        @pl.when(d != z)
-        def _():
-            def leave(r):
-                self.leaving[a][d, r] = outs[r].astype(bf16)
-
-            by_rows(self.rows, leave)
+            add_arrived()
 
         @pl.when(d > z)
         def _():
@@ -956,9 +975,9 @@
                 copies.append(
                     remote(block, ones.at[way, i], one_send.at[way, i], one_recv.at[way, i], step_dev[way])
                 )
-            self.two.append(
-                remote(parts.at[1 - way, halves[way]], twos.at[way], two_send.at[way], two_recv.at[way], step_dev[1 - way])
-            )
+            if twos is not None:
+                block = parts.at[1 - way, halves[way]]
+                self.two.append(remote(block, twos.at[way], two_send.at[way], two_recv.at[way], step_dev[1 - way]))
 
     def there(self, r, way):
         return pl.ds(pl.multiple_of(r.start + way * self.half, 16), r.size)
@@ -1052,9 +1071,21 @@
     return jnp.sum(value, axis=0, keepdims=True)
 
 
-def branch_kernel(grads, grad_normed, middle, gains, context, weights, layer, layer_out, grad_branch, grad_context,
-                  grad_o, gain_rows, weight, stage, load_sem, out_sem):
+def branch_kernel(grads, grad_normed, middle, gains, context, weights, layer, onward, layer_out, grad_branch,
+                  grad_context, grad_o, gain_rows, weight, stage, arrived_layer, load_sem, out_sem, send, recv):
     length, width = middle.shape[0], D + 2 * KW
+    half = length // 2
+    z, c, f = place()
+    near = (device(z, c, flipped(f, 1)), device(z, c, flipped(f, 2)))
+    greet(near, [])
+    last = [
+        pltpu.make_async_remote_copy(
+            onward.at[way], arrived_layer.at[way], send.at[way], recv.at[way], device_id=near[1 - way], device_id_type=MESH
+        )
+        for way in range(2)
+    ]
+    for copy in last:
+        copy.start()
     load_o = pltpu.make_async_copy(weights.at[:, pl.ds(width, D)], weight, load_sem.at[0])
     load_o.start()
     gain_rows[...] = jnp.zeros_like(gain_rows)
@@ -1067,7 +1098,6 @@
         inner = jnp.mean(weighted * rows, axis=-1, keepdims=True)
         value = grads[r].astype(f32) + inverse * weighted - rows * (inverse * inverse * inverse * inner)
         grad_branch[r] = value.astype(bf16)
-        layer_out[r] = (rows + layer[r].astype(f32)).astype(bf16)
 
     by_rows(length, middle_grads)
     load_o.wait()
@@ -1095,11 +1125,19 @@
         return carry
 
     lax.fori_loop(0, steps, step, 0)
+    for way in range(2):
+        last[way].wait()
+
+        def add_last(r):
+            there = pl.ds(pl.multiple_of(r.start + way * half, 16), r.size)
+            layer_out[there] = (middle[there] + layer[there].astype(f32) + arrived_layer[way, r].astype(f32)).astype(bf16)
+
+        by_rows(half, add_last)
     out(steps - 2, 0).wait()
     out(steps - 1, 1).wait()
 
 
-def branch(grads, grad_normed, middle, gains, context, weights, layer):
+def branch(grads, grad_normed, middle, gains, context, weights, layer, onward):
     length = middle.shape[0]
     dma = pltpu.SemaphoreType.DMA
     vmem, hbm = pl.BlockSpec(memory_space=pltpu.VMEM), pl.BlockSpec(memory_space=pl.ANY)
@@ -1107,13 +1145,18 @@
     return pl.pallas_call(
         branch_kernel,
         out_shape=(rows, rows, rows, jax.ShapeDtypeStruct((D, D), bf16), jax.ShapeDtypeStruct((8, D), f32)),
-        in_specs=[vmem] * 5 + [hbm, vmem],
+        in_specs=[vmem] * 5 + [hbm, vmem, vmem],
         out_specs=(vmem, vmem, vmem, hbm, vmem),
-        scratch_shapes=[pltpu.VMEM((D, D), bf16), pltpu.VMEM((2, 512, D), bf16), dma((1,)), dma((2,))],
-        compiler_params=pltpu.CompilerParams(vmem_limit_bytes=feed_vmem_limit),
+        scratch_shapes=[
+            pltpu.VMEM((D, D), bf16), pltpu.VMEM((2, 512, D), bf16), pltpu.VMEM((2, length // 2, D), bf16),
+            dma((1,)), dma((2,)), dma((2,)), dma((2,)),
+        ],
+        compiler_params=pltpu.CompilerParams(
+            collective_id=4, has_side_effects=True, vmem_limit_bytes=feed_vmem_limit
+        ),
         cost_estimate=cost(22),
         name="branch",
-    )(grads, grad_normed, middle, gains, context, weights, layer)
+    )(grads, grad_normed, middle, gains, context, weights, layer, onward)
 
 
 def backward_kernel(lines, x, normed_one, qkv, grad_context, log_totals, gains, cosine, sine, seg_col, seg_row, gain_two,
@@ -1156,6 +1199,7 @@
                 scatter.over_first(0, d)
         else:
             scatter.over_second(0, order[0])
+            scatter.over_second(0, order[1])
 
     allowed = mask_keys_rows(seg_col[...], seg_row[...], length)
     attend_heads_grad(
@@ -1166,6 +1210,8 @@
         grad_one[:, i * 512 : (i + 1) * 512] = dot_t(grad_proj[...], weight[i % 2])
         if i + 2 < D // 512:
             load_weight(i + 2).start()
+    for d in order[2:]:
+        scatter.over_second(0, d)
     load_branch.wait()
 
     def input_grads(r):
@@ -1204,16 +1250,16 @@
         put(scatter.sums[1].at[d], blocks(d, c))
         if j:
             scatter.over_core(1, order[j - 1])
-        if j == 1:
-            scatter.over_second(0, order[1])
+        if j < len(order) - 1:
+            scatter.over_line(0, d)
     scatter.over_core(1, order[-1])
-    for d in order[2:]:
-        scatter.over_second(0, d)
-    for j in range(len(order) + 1):
+    for j in range(len(order) + 2):
         if j < len(order):
             scatter.over_first(1, order[j])
-        if j:
+        if 0 <= j - 1 < len(order):
             scatter.over_second(1, order[j - 1])
+        if 0 <= j - 2 < len(order) - 1:
+            scatter.over_line(1, order[j - 2])
     for d in order:
         scatter.to_core(0, d, grad_o.at[d, 1 - c]).wait_send()
     for j in range(max(0, len(order) - 2), len(order)):
@@ -1399,9 +1445,9 @@
     )(total, grads[0], *grads, *flat)
 
 
-def feed_front_kernel(n_hbm, g_hbm, wm_hbm, wd_hbm, gh_hbm, grad_down, layer_sum, n, g, wm, wd, act, gh, stage, parts,
-                      ones, twos, *sems):
-    sum_sems, (load_sem, weight_sem, out_sem) = sems[:4], sems[4:]
+def feed_front_kernel(n_hbm, g_hbm, wm_hbm, wd_hbm, gh_hbm, grad_down, layer_sum, onward, n, g, wm, wd, act, gh, stage,
+                      parts, ones, *sems):
+    sum_sems, (load_sem, weight_sem, out_sem) = sems[:2], sems[2:]
     z, c, f = place()
     x_dev, y_dev = device(z, c, flipped(f, 1)), device(z, c, flipped(f, 2))
     tokens = n.shape[0]
@@ -1434,7 +1480,7 @@
         load_n[k].start()
         load_g[k].start()
     greet([x_dev, y_dev], [])
-    summed = PlaneSum(parts, ones, twos, sum_sems, x_dev, y_dev)
+    summed = PlaneSum(parts, ones, None, (*sum_sems, None, None), x_dev, y_dev)
 
     def hidden(k, slot, lanes, up_lanes):
         rows = rows_of(k)
@@ -1486,8 +1532,6 @@
                 copy.start()
         elif k:
             summed.near[k - 1].start()
-        if k == 2:
-            summed.pass_on()
     wide = ff // 256
 
     def down_out(i, slot, width=256):
@@ -1521,10 +1565,22 @@
             down_out(2 * wide + slot, slot, ff % 256).wait()
         hidden_out(2 + slot).wait()
 
-    def add_layer(r, value):
-        layer_sum[r] = (layer_sum[r].astype(f32) + value).astype(bf16)
-
-    summed.finish(add_layer)
+    for way in range(2):
+        summed.far[way].wait()
+
+        def add_far(r):
+            mine = parts[1 - way, summed.there(r, way)].astype(f32)
+            onward[way, r] = (mine + ones[way, 1, r].astype(f32)).astype(bf16)
+
+        by_rows(summed.half, add_far)
+    for way in range(2):
+        summed.near[way].wait()
+
+        def add_near(r):
+            there = summed.there(r, way)
+            layer_sum[there] = (layer_sum[there].astype(f32) + ones[way, 0, r].astype(f32)).astype(bf16)
+
+        by_rows(summed.half, add_near)
 
 
 def feed_back_kernel(gh_hbm, wm_hbm, n_hbm, grad_normed, grad_mlp, gh, wm, n, stage, parts, ones, twos, *sems):
@@ -1599,21 +1655,22 @@
     normed_all = normed_all.reshape(tokens, D)
 
     def buffers(*shapes):
-        return [pltpu.VMEM(shape, bf16) for shape in shapes] + sum_buffers + sum_sems
-
-    grad_hidden, grad_down, layer_sum = pl.pallas_call(
+        return [pltpu.VMEM(shape, bf16) for shape in shapes]
+
+    grad_hidden, grad_down, layer_sum, onward = pl.pallas_call(
         feed_front_kernel,
         out_shape=(
             jax.ShapeDtypeStruct((tokens, 2 * ff), bf16),
             jax.ShapeDtypeStruct((ff, D), bf16),
             jax.ShapeDtypeStruct((length, D), bf16),
+            jax.ShapeDtypeStruct((2, length // 2, D), bf16),
         ),
         in_specs=[hbm] * 4,
-        out_specs=(hbm, hbm, vmem),
+        out_specs=(hbm, hbm, vmem, vmem),
         scratch_shapes=buffers(
             (tokens, D), (tokens, D), (D, 2 * ff), (ff, D), (tokens, ff), (2, length, 2 * ff), (2, 256, D // 2)
         )
-        + [dma((2, 4)), dma((3, -(-ff // 256))), dma((2, 2))],
+        + sum_buffers[:2] + sum_sems[:2] + [dma((2, 4)), dma((3, -(-ff // 256))), dma((2, 2))],
         compiler_params=pltpu.CompilerParams(
             collective_id=6, has_side_effects=True, vmem_limit_bytes=feed_vmem_limit
         ),
@@ -1626,14 +1683,14 @@
         in_specs=[hbm] * 3,
         out_specs=(vmem, hbm),
         scratch_shapes=buffers((tokens, 2 * ff), (D, 2 * ff), (tokens, D), (2, 512, ff))
-        + [dma((2, 4)), dma((2,))],
+        + sum_buffers + sum_sems + [dma((2, 4)), dma((2,))],
         compiler_params=pltpu.CompilerParams(
             collective_id=9, has_side_effects=True, vmem_limit_bytes=feed_vmem_limit
         ),
         cost_estimate=cost(60),
         name="feed_back",
     )(grad_hidden, mlp_cols, normed_all)
-    return grad_normed, grad_down, grad_mlp, layer_sum
+    return grad_normed, grad_down, grad_mlp, layer_sum, onward
 
 
 def local(
@@ -1689,7 +1746,7 @@
         middle = tokens_f + matmul(attended, out_full)
     inverse_two = lax.rsqrt(jnp.mean(middle * middle, axis=-1, keepdims=True) + norm_eps)
     if n_tp == 4:
-        grad_normed_two, grad_down, grad_mlp, layer_parts = feed(normed_all, grads_all, mlp_cols, down_cols)
+        grad_normed_two, grad_down, grad_mlp, layer_sum, onward = feed(normed_all, grads_all, mlp_cols, down_cols)
     else:
         normed_two = (middle * inverse_two * gain_two).astype(bf16)
         normed_all = plane_gather(normed_two, n_tp)
@@ -1716,7 +1773,7 @@
 
     if n_tp == 4:
         layer_out, grad_branch, grad_context, grad_out, gain_two_rows = branch(
-            cotangent, grad_normed_two, middle, gains_full, attended, attn_full, layer_parts
+            cotangent, grad_normed_two, middle, gains_full, attended, attn_full, layer_sum, onward
         )
         input_grad, out_sum, qkv_sum = backward(
             inputs, normed_one, qkv, grad_context, log_totals, gains_full, cosine, sine, seg_col, seg_row,

time: 614 us -> 594 us (0.967)
  Pallas kernels: 581 us -> 559 us
    pallas_call x1, Pallas kernels: 155 us -> 135 us  [backward(): pl.pallas_call(functools.partial(backward_kernel, lines), out_shape=(jax....]
    pallas_call x1, Pallas kernels: 81.2 us -> 70.5 us  [feed(): pl.pallas_call(feed_front_kernel, out_shape=(jax.ShapeDtypeStruct((tokens...]
where the time goes in v6:
time: 594 us; the launch traced here: 590 us
  Pallas kernels  559 us (94%)
  between operations  16.9 us (3%)
  local copies, waits for them, and re-layouts  7.28 us (1%)
  other arithmetic  6.65 us (1%)
    pallas_call x1, Pallas kernels, backward(): pl.pallas_call(functools.partial(backward_kernel, lines), out_shape=(jax....  135 us
    pallas_call x1, Pallas kernels, forward(): pl.pallas_call(forward_kernel, out_shape=(jax.ShapeDtypeStruct((length, w...  110 us
    pallas_call x1, Pallas kernels, gather_all(): pl.pallas_call(functools.partial(gather_kernel, lines), out_shape=(jax.Sh...  103 us
    pallas_call x1, Pallas kernels, feed(): pl.pallas_call(feed_front_kernel, out_shape=(jax.ShapeDtypeStruct((tokens...  70.5 us
    pallas_call x1, Pallas kernels, feed(): pl.pallas_call(feed_back_kernel, out_shape=(jax.ShapeDtypeStruct((length,...  63 us
    pallas_call x1, Pallas kernels, norm_parts(): pl.pallas_call(functools.partial(norm_kernel, n_dp, n_tp), out_shape=(jax...  32.6 us
    pallas_call x1, Pallas kernels, branch(): pl.pallas_call(branch_kernel, out_shape=(rows, rows, rows, jax.ShapeDtype...  26.5 us
    pallas_call x1, Pallas kernels, adam_all(): pl.pallas_call(adam_kernel, grid=(steps,), out_shape=[jax.ShapeDtypeStruc...  18.2 us
  transfers between devices with their start and end apart: 3, of which 0 were waited for; matrix products, arithmetic and copies ran while one was open for 1% of the time, Pallas kernels for 57%

profile of v6, /device:TPU:0, one launch (start us, length us, event | category | flops | bytes accessed | tf_op | source)
XLA Modules:
  0.0 590.3 jit_solution(8159944021785044166)
XLA Ops:
  7.2 0.0 copy-start
  7.2 0.0 all-gather.2.cloned.1.call-start
  7.2 0.8 convert.15
  8.0 0.1 copy.46
  8.1 1.1 convert.14
  9.2 1.1 convert.13
  10.3 0.0 copy-done
  10.4 0.1 convert_element_type.14.down
  10.5 0.0 copy-start.3
  10.5 103.3 %gather_all.1 = (bf16[4,2,4,64,4736]{4,3,2,1,0:T(8,128)(2,1)}, bf16[4,64,2816]{2,1,0:T(8,128)(2,1)}, bf16[4,2,176,2048]{3,2,1,0:T(8,128)(2,1)}) custom-call(bf16[64,4736]{1,0:T(8,128)(2,1)S(1)} %fusion.1.own, f32[64,11264]{1,0:T(8,128)} %refs_10_.1, bf16[176,2048]{1,0:T(8,128)(2,1)S(1)} %convert_element_type.14.down), custom_call_target="tpu_custom_call" | custom-call | bytes 369000000 | tf_op jit(solution)/shard_map/gather_all/pallas_call | solution.py:366
  113.8 0.0 all-gather.2.cloned.1.call-update
  113.8 0.0 reduce-scatter.5.cloned.1.call-start
  113.9 0.0 copy-done.3
  113.9 0.5 slice.24
  115.1 0.1 add_select_fusion
  115.2 0.3 reduce-window.9
  115.5 0.1 slice.27
  115.6 0.8 copy.49.seg_col
  116.4 1.1 convert_bitcast_fusion
  117.5 1.3 copy.48.gains
  118.8 0.1 slice_reduce_fusion
  119.0 0.1 fusion.4
  119.0 0.8 fusion.2
  119.8 1.1 pad_maximum_fusion
  120.9 110.1 %forward.1 = (bf16[384,2560]{1,0:T(8,128)(2,1)}, bf16[384,2048]{1,0:T(8,128)(2,1)}, f32[32,384]{1,0:T(8,128)}, f32[384,2048]{1,0:T(8,128)}, bf16[384,2048]{1,0:T...) custom-call(bf16[384,2048]{1,0:T(8,128)(2,1)} %x.5, bf16[384,2048]{1,0:T(8,128)(2,1)} %grads.3, ...), custom_call_target="tpu_custom_call" | custom-call | bytes 350550016 | tf_op jit(solution)/shard_map/forward/pallas_call | solution.py:935
  231.0 0.0 all-gather.2.cloned.1.call-done.wm_hbm
  231.1 70.5 %feed_front.1 = (bf16[1536,2816]{1,0:T(8,128)(2,1)}, bf16[1408,2048]{1,0:T(8,128)(2,1)}, bf16[384,2048]{1,0:T(8,128)(2,1)}, bf16[2,192,2048]{2,1,0:T(8,128)(2,1)}) custom-call(bf16[1536,2048]{1,0:T(8,128)(2,1)} %bitcast.31, bf16[1536,2048]{1,0:T(8,128)(2,1)} %bitcast.34, bf16[2048,2816]{1,0:T(8,128)(2,1)} %all-gather.2.cloned.1.call-done.wm_hbm, ...), custom_call_target="tpu_custom_call" | custom-call | bytes 239850000 | tf_op jit(solution)/shard_map/feed_front/pallas_call | solution.py:1660
  301.6 0.0 reduce-scatter.5.cloned.1.call-update
  301.6 0.2 reduce-scatter.3.cloned.1.call-start
  301.8 63.0 %feed_back.1 = (f32[384,2048]{1,0:T(8,128)}, bf16[2048,2816]{1,0:T(8,128)(2,1)}) custom-call(bf16[1536,2816]{1,0:T(8,128)(2,1)} %get-tuple-element.64.gh_hbm, bf16[2048,2816]{1,0:T(8,128)(2,1)} %all-gather.2.cloned.1.call-done.wm_hbm, bf16[1536,2048]{1,0:T(8,128)(2,1)} %bitcast.32), custom_call_target="tpu_custom_call" | custom-call | bytes 221400000 | tf_op jit(solution)/shard_map/feed_back/pallas_call | solution.py:1680
  364.8 0.0 reduce-scatter.3.cloned.1.call-update
  364.9 26.5 %branch.1 = (bf16[384,2048]{1,0:T(8,128)(2,1)}, bf16[384,2048]{1,0:T(8,128)(2,1)}, bf16[384,2048]{1,0:T(8,128)(2,1)}, bf16[2048,2048]{1,0:T(8,128)(2,1)}, f32[8,2048]{1,0:T(8,128)}) custom-call(bf16[384,2048]{1,0:T(8,128)(2,1)} %grads.3, f32[384,2048]{1,0:T(8,128)} %get-tuple-element.65.grad_normed, f32[384,2048]{1,0:T(8,128)} %get-tuple-element.66.middle, ...), custom_call_target="tpu_custom_call" | custom-call | bytes 81180000 | tf_op jit(solution)/shard_map/branch/pallas_call | solution.py:1145
  391.3 135.0 %backward.1 = (bf16[384,2048]{1,0:T(8,128)(2,1)}, f32[64,2048]{1,0:T(8,128)}, f32[64,2688]{1,0:T(8,128)}) custom-call(bf16[384,2048]{1,0:T(8,128)(2,1)} %x.5, bf16[384,2048]{1,0:T(8,128)(2,1)} %get-tuple-element.71.normed_one, bf16[384,2560]{1,0:T(8,128)(2,1)} %get-tuple-element.72.qkv, bf16[384,2048]{1,0:T(8,128)(2,1)} %get-tuple-element.73.grad_context, ...), custom_call_target="tpu_custom_call" | custom-call | bytes 387449984 | tf_op jit(solution)/shard_map/backward/pallas_call | solution.py:1278
  526.3 0.0 reduce-scatter.5.cloned.1.call-done.down.refs_3_
  526.3 0.0 reduce-scatter.3.cloned.1.call-done
  526.4 32.6 %norm_parts.1 = (f32[64,11264]{1,0:T(8,128)}, f32[8,128]{1,0:T(8,128)}) custom-call(bf16[4,64,2816]{2,1,0:T(8,128)(2,1)} %bitcast.36, f32[64,2688]{1,0:T(8,128)} %get-tuple-element.80.qkv.gain_block.refs_0_, f32[64,2048]{1,0:T(8,128)} %get-tuple-element.81.out.refs_1_, bf16[176,2048]{1,0:T(8,128)(2,1)} %reduce-scatter.5.cloned.1.call-done.down.refs_3_), custom_call_target="tpu_custom_call" | custom-call | bytes 129150000 | tf_op jit(solution)/shard_map/norm_parts/pallas_call | solution.py:1379
  558.9 1.2 slice.29
  560.8 0.0 copy-start.1
  560.8 18.2 %adam.1 = (f32[64,2560]{1,0:T(8,128)}, f32[64,2560]{1,0:T(8,128)}, f32[64,2560]{1,0:T(8,128)}, f32[64,2048]{1,0:T(8,128)}, f32[64,2048]{1,0:T(8,128)}, /*index=5...) custom-call(f32[8,128]{1,0:T(8,128)} %get-tuple-element.83.total, ...), custom_call_target="tpu_custom_call" | custom-call | bytes 51660000 | tf_op jit(solution)/shard_map/adam/pallas_call | solution.py:1436
  579.0 0.0 copy-done.1
  579.0 0.0 copy-start.2
  579.0 1.1 copy.55
  580.2 0.8 copy-done.2
  581.0 1.1 copy.56
  (5 shorter events, 0.1 us)
Async XLA Ops:
  7.2 3.2 copy-start
  7.2 223.9 %all-gather.2.cloned.1.call-start = ((), (), s32[]{:S(2)}) async-start(), calls=%async_computation.2 | async-start | bytes 12976128 | tf_op jit(solution)/shard_map/all_gather | solution.py:1734
  10.5 103.4 %copy-start.3 = (s32[1,384]{1,0:T(1,128)S(1)}, s32[1,384]{1,0:T(1,128)}, u32[]{:S(2)}) copy-start(s32[1,384]{1,0:T(1,128)} %seg_row.3) | copy-start | bytes 4612
  113.8 412.5 %reduce-scatter.5.cloned.1.call-start = ((), (), s32[]{:S(2)}) async-start(), calls=%async_computation.4 | async-start | bytes 6488064 | tf_op jit(solution)/shard_map/reduce_scatter | solution.py:1771
  301.6 224.8 %reduce-scatter.3.cloned.1.call-start = ((), (), s32[]{:S(2)}) async-start(), calls=%async_computation.3 | async-start | bytes 12976128 | tf_op jit(solution)/shard_map/reduce_scatter | solution.py:1772
  560.8 18.2 %copy-start.1 = (bf16[384,2048]{1,0:T(8,128)(2,1)S(1)}, bf16[384,2048]{1,0:T(8,128)(2,1)}, u32[]{:S(2)}) copy-start(bf16[384,2048]{1,0:T(8,128)(2,1)} %get-tuple-element.123) | copy-start | bytes 4718596
  579.0 2.0 copy-start.2
Sparse Core Ops, SparseCore 0:
  113.9 108.4 all-gather.1
  301.7 65.1 reduce-scatter.4
  369.3 146.7 reduce-scatter.2

commit v7 on v6

--- a/solution.py
+++ b/solution.py
@@ -847,10 +847,12 @@
 
         low, high = pl.ds(0, half), pl.ds(half, half)
         self.near = [remote(own, whole.at[1], 0, x_dev), remote(own, whole.at[2], 1, y_dev)]
-        self.far = [
-            remote(whole.at[2, low], whole.at[3, low], 2, x_dev),
-            remote(whole.at[1, high], whole.at[3, high], 3, y_dev),
-        ]
+        self.far = []
+        if whole.shape[0] > 3:
+            self.far = [
+                remote(whole.at[2, low], whole.at[3, low], 2, x_dev),
+                remote(whole.at[1, high], whole.at[3, high], 3, y_dev),
+            ]
         self.here = pltpu.make_async_copy(own, whole.at[0], here.at[i])
 
     def start(self):
@@ -941,7 +943,7 @@
             jax.ShapeDtypeStruct((length, D), f32),
             jax.ShapeDtypeStruct((length, D), bf16),
             jax.ShapeDtypeStruct((4, length, D), bf16),
-            jax.ShapeDtypeStruct((4, length, D), bf16),
+            jax.ShapeDtypeStruct((3, length, D), bf16),
         ),
         in_specs=[vmem, hbm] + [vmem] * 5 + [hbm],
         out_specs=(vmem,) * 5 + (hbm,) * 2,
@@ -1447,19 +1449,20 @@
 
 def feed_front_kernel(n_hbm, g_hbm, wm_hbm, wd_hbm, gh_hbm, grad_down, layer_sum, onward, n, g, wm, wd, act, gh, stage,
                       parts, ones, *sems):
-    sum_sems, (load_sem, weight_sem, out_sem) = sems[:2], sems[2:]
+    sum_sems, (load_sem, weight_sem, out_sem, far_send, far_recv) = sems[:2], sems[2:]
     z, c, f = place()
     x_dev, y_dev = device(z, c, flipped(f, 1)), device(z, c, flipped(f, 2))
     tokens = n.shape[0]
     length = tokens // 4
     ff = wd.shape[0]
-    order = (3, 1, 2, 0)
+    half = length // 2
+    order = (1, 2, 3, 0)
 
     def rows_of(k):
         return pl.ds(k * length, length)
 
     load_n = [pltpu.make_async_copy(n_hbm.at[rows_of(k)], n.at[rows_of(k)], load_sem.at[0, k]) for k in range(4)]
-    load_g = [pltpu.make_async_copy(g_hbm.at[rows_of(k)], g.at[rows_of(k)], load_sem.at[1, k]) for k in range(4)]
+    load_g = [pltpu.make_async_copy(g_hbm.at[rows_of(k)], g.at[rows_of(k)], load_sem.at[1, k]) for k in range(3)]
     tiles = [(start, min(256, ff - start)) for start in range(0, ff, 256)]
     load_w = []
     for t, (start, size) in enumerate(tiles):
@@ -1478,8 +1481,20 @@
             copy.start()
     for k in order[1:]:
         load_n[k].start()
-        load_g[k].start()
+        if k < 3:
+            load_g[k].start()
     greet([x_dev, y_dev], [])
+    far_grads = [
+        pltpu.make_async_remote_copy(
+            g_hbm.at[pl.ds(start, half)], g.at[pl.ds(to, half)], far_send.at[i], far_recv.at[i], device_id=dev,
+            device_id_type=MESH,
+        )
+        for i, (start, to, dev) in enumerate(
+            ((2 * length, 3 * length, x_dev), (length + half, 3 * length + half, y_dev))
+        )
+    ]
+    for copy in far_grads:
+        copy.start()
     summed = PlaneSum(parts, ones, None, (*sum_sems, None, None), x_dev, y_dev)
 
     def hidden(k, slot, lanes, up_lanes):
@@ -1498,7 +1513,8 @@
 
     for i, k in enumerate(order):
         load_n[k].wait()
-        load_g[k].wait()
+        for copy in load_g[k : k + 1] or far_grads:
+            copy.wait()
         if i >= 2:
             hidden_out(i - 2).wait()
         if i == 0:
@@ -1670,13 +1686,14 @@
         scratch_shapes=buffers(
             (tokens, D), (tokens, D), (D, 2 * ff), (ff, D), (tokens, ff), (2, length, 2 * ff), (2, 256, D // 2)
         )
-        + sum_buffers[:2] + sum_sems[:2] + [dma((2, 4)), dma((3, -(-ff // 256))), dma((2, 2))],
+        + sum_buffers[:2] + sum_sems[:2]
+        + [dma((2, 4)), dma((3, -(-ff // 256))), dma((2, 2)), dma((2,)), dma((2,))],
         compiler_params=pltpu.CompilerParams(
             collective_id=6, has_side_effects=True, vmem_limit_bytes=feed_vmem_limit
         ),
         cost_estimate=cost(65),
         name="feed_front",
-    )(normed_all, grads_all.reshape(tokens, D), mlp_cols, down_cols)
+    )(normed_all, grads_all.reshape(-1, D), mlp_cols, down_cols)
     grad_normed, grad_mlp = pl.pallas_call(
         feed_back_kernel,
         out_shape=(jax.ShapeDtypeStruct((length, D), f32), jax.ShapeDtypeStruct((D, 2 * ff), bf16)),

time: 594 us -> 584 us (0.983)
  Pallas kernels: 559 us -> 543 us
    pallas_call x1, Pallas kernels: 110 us -> 95.5 us  [forward(): pl.pallas_call(forward_kernel, out_shape=(jax.ShapeDtypeStruct((length, w...]
  transfers between devices with their start and end apart: 3 -> 3, of which waited for: 0 -> 1; matrix products, arithmetic and copies ran while one was open for 1% -> 1% of each run, Pallas kernels for 57% -> 55%
where the time goes in v7:
time: 584 us; the launch traced here: 580 us
  Pallas kernels  543 us (93%)
  between operations  16.9 us (3%)
  local copies, waits for them, and re-layouts  7.28 us (1%)
  other arithmetic  6.65 us (1%)
  waiting for transfers between devices  6.01 us (1%)
    pallas_call x1, Pallas kernels, backward(): pl.pallas_call(functools.partial(backward_kernel, lines), out_shape=(jax....  131 us
    pallas_call x1, Pallas kernels, gather_all(): pl.pallas_call(functools.partial(gather_kernel, lines), out_shape=(jax.Sh...  103 us
    pallas_call x1, Pallas kernels, forward(): pl.pallas_call(forward_kernel, out_shape=(jax.ShapeDtypeStruct((length, w...  95.5 us
    pallas_call x1, Pallas kernels, feed(): pl.pallas_call(feed_front_kernel, out_shape=(jax.ShapeDtypeStruct((tokens...  71 us
    pallas_call x1, Pallas kernels, feed(): pl.pallas_call(feed_back_kernel, out_shape=(jax.ShapeDtypeStruct((length,...  63.6 us
    pallas_call x1, Pallas kernels, norm_parts(): pl.pallas_call(functools.partial(norm_kernel, n_dp, n_tp), out_shape=(jax...  32.6 us
    pallas_call x1, Pallas kernels, branch(): pl.pallas_call(branch_kernel, out_shape=(rows, rows, rows, jax.ShapeDtype...  27.2 us
    pallas_call x1, Pallas kernels, adam_all(): pl.pallas_call(adam_kernel, grid=(steps,), out_shape=[jax.ShapeDtypeStruc...  18.2 us
  transfers between devices with their start and end apart: 3, of which 1 were waited for; matrix products, arithmetic and copies ran while one was open for 1% of the time, Pallas kernels for 55%

profile of v7, /device:TPU:0, one launch (start us, length us, event | category | flops | bytes accessed | tf_op | source)
XLA Modules:
  0.0 580.0 jit_solution(11008634002837554577)
XLA Ops:
  7.2 0.0 copy-start
  7.2 0.0 all-gather.2.cloned.1.call-start
  7.2 0.8 convert.15
  8.0 0.1 copy.46
  8.1 1.1 convert.14
  9.2 1.1 convert.13
  10.3 0.0 copy-done
  10.4 0.1 convert_element_type.14.down
  10.5 0.0 copy-start.3
  10.5 103.3 %gather_all.1 = (bf16[4,2,4,64,4736]{4,3,2,1,0:T(8,128)(2,1)}, bf16[4,64,2816]{2,1,0:T(8,128)(2,1)}, bf16[4,2,176,2048]{3,2,1,0:T(8,128)(2,1)}) custom-call(bf16[64,4736]{1,0:T(8,128)(2,1)S(1)} %fusion.1.own, f32[64,11264]{1,0:T(8,128)} %refs_10_.1, bf16[176,2048]{1,0:T(8,128)(2,1)S(1)} %convert_element_type.14.down), custom_call_target="tpu_custom_call" | custom-call | bytes 369000000 | tf_op jit(solution)/shard_map/gather_all/pallas_call | solution.py:366
  113.8 0.0 all-gather.2.cloned.1.call-update
  113.8 0.0 reduce-scatter.5.cloned.1.call-start
  113.9 0.0 copy-done.3
  113.9 0.5 slice.24
  115.1 0.1 add_select_fusion
  115.2 0.3 reduce-window.9
  115.5 0.1 slice.27
  115.6 0.8 copy.49.seg_col
  116.4 1.1 convert_bitcast_fusion
  117.5 1.3 copy.48.gains
  118.8 0.1 slice_reduce_fusion
  119.0 0.1 fusion.4
  119.0 0.8 fusion.2
  119.8 1.1 pad_maximum_fusion
  120.9 95.5 %forward.1 = (bf16[384,2560]{1,0:T(8,128)(2,1)}, bf16[384,2048]{1,0:T(8,128)(2,1)}, f32[32,384]{1,0:T(8,128)}, f32[384,2048]{1,0:T(8,128)}, bf16[384,2048]{1,0:T...) custom-call(bf16[384,2048]{1,0:T(8,128)(2,1)} %x.5, bf16[384,2048]{1,0:T(8,128)(2,1)} %grads.3, ...), custom_call_target="tpu_custom_call" | custom-call | bytes 350550016 | tf_op jit(solution)/shard_map/forward/pallas_call | solution.py:937
  216.5 5.9 %all-gather.2.cloned.1.call-done.wm_hbm = bf16[2048,2816]{1,0:T(8,128)(2,1)} async-done(((bf16[256,2816]{1,0:T(8,128)(2,1)}), bf16[2048,2816]{1,0:T(8,128)(2,1)}) %all-gather.2.cloned.1.call-update) | async-done | bytes 11534352 | tf_op jit(solution)/shard_map/all_gather | solution.py:1751
  222.4 71.0 %feed_front.1 = (bf16[1536,2816]{1,0:T(8,128)(2,1)}, bf16[1408,2048]{1,0:T(8,128)(2,1)}, bf16[384,2048]{1,0:T(8,128)(2,1)}, bf16[2,192,2048]{2,1,0:T(8,128)(2,1)}) custom-call(bf16[1536,2048]{1,0:T(8,128)(2,1)} %bitcast.31, bf16[1152,2048]{1,0:T(8,128)(2,1)} %bitcast.35, bf16[2048,2816]{1,0:T(8,128)(2,1)} %all-gather.2.cloned.1.call-done.wm_hbm, ...), custom_call_target="tpu_custom_call" | custom-call | bytes 239850000 | tf_op jit(solution)/shard_map/feed_front/pallas_call | solution.py:1676
  293.4 0.0 reduce-scatter.5.cloned.1.call-update
  293.4 0.2 reduce-scatter.3.cloned.1.call-start
  293.6 63.6 %feed_back.1 = (f32[384,2048]{1,0:T(8,128)}, bf16[2048,2816]{1,0:T(8,128)(2,1)}) custom-call(bf16[1536,2816]{1,0:T(8,128)(2,1)} %get-tuple-element.64.gh_hbm, bf16[2048,2816]{1,0:T(8,128)(2,1)} %all-gather.2.cloned.1.call-done.wm_hbm, bf16[1536,2048]{1,0:T(8,128)(2,1)} %bitcast.32), custom_call_target="tpu_custom_call" | custom-call | bytes 221400000 | tf_op jit(solution)/shard_map/feed_back/pallas_call | solution.py:1697
  357.2 0.0 reduce-scatter.3.cloned.1.call-update
  357.3 27.2 %branch.1 = (bf16[384,2048]{1,0:T(8,128)(2,1)}, bf16[384,2048]{1,0:T(8,128)(2,1)}, bf16[384,2048]{1,0:T(8,128)(2,1)}, bf16[2048,2048]{1,0:T(8,128)(2,1)}, f32[8,2048]{1,0:T(8,128)}) custom-call(bf16[384,2048]{1,0:T(8,128)(2,1)} %grads.3, f32[384,2048]{1,0:T(8,128)} %get-tuple-element.65.grad_normed, f32[384,2048]{1,0:T(8,128)} %get-tuple-element.66.middle, ...), custom_call_target="tpu_custom_call" | custom-call | bytes 81180000 | tf_op jit(solution)/shard_map/branch/pallas_call | solution.py:1147
  384.4 131.4 %backward.1 = (bf16[384,2048]{1,0:T(8,128)(2,1)}, f32[64,2048]{1,0:T(8,128)}, f32[64,2688]{1,0:T(8,128)}) custom-call(bf16[384,2048]{1,0:T(8,128)(2,1)} %x.5, bf16[384,2048]{1,0:T(8,128)(2,1)} %get-tuple-element.71.normed_one, bf16[384,2560]{1,0:T(8,128)(2,1)} %get-tuple-element.72.qkv, bf16[384,2048]{1,0:T(8,128)(2,1)} %get-tuple-element.73.grad_context, ...), custom_call_target="tpu_custom_call" | custom-call | bytes 387449984 | tf_op jit(solution)/shard_map/backward/pallas_call | solution.py:1280
  515.9 0.0 reduce-scatter.5.cloned.1.call-done.down.refs_3_
  515.9 0.0 reduce-scatter.3.cloned.1.call-done
  515.9 32.6 %norm_parts.1 = (f32[64,11264]{1,0:T(8,128)}, f32[8,128]{1,0:T(8,128)}) custom-call(bf16[4,64,2816]{2,1,0:T(8,128)(2,1)} %bitcast.36, f32[64,2688]{1,0:T(8,128)} %get-tuple-element.80.qkv.gain_block.refs_0_, f32[64,2048]{1,0:T(8,128)} %get-tuple-element.81.out.refs_1_, bf16[176,2048]{1,0:T(8,128)(2,1)} %reduce-scatter.5.cloned.1.call-done.down.refs_3_), custom_call_target="tpu_custom_call" | custom-call | bytes 129150000 | tf_op jit(solution)/shard_map/norm_parts/pallas_call | solution.py:1381
  548.6 1.2 slice.29
  550.5 0.0 copy-start.1
  550.5 18.2 %adam.1 = (f32[64,2560]{1,0:T(8,128)}, f32[64,2560]{1,0:T(8,128)}, f32[64,2560]{1,0:T(8,128)}, f32[64,2048]{1,0:T(8,128)}, f32[64,2048]{1,0:T(8,128)}, /*index=5...) custom-call(f32[8,128]{1,0:T(8,128)} %get-tuple-element.83.total, ...), custom_call_target="tpu_custom_call" | custom-call | bytes 51660000 | tf_op jit(solution)/shard_map/adam/pallas_call | solution.py:1438
  568.7 0.0 copy-done.1
  568.7 0.0 copy-start.2
  568.7 1.1 copy.55
  569.8 0.8 copy-done.2
  570.7 1.1 copy.56
  (5 shorter events, 0.1 us)
Async XLA Ops:
  7.2 3.2 copy-start
  7.2 215.2 %all-gather.2.cloned.1.call-start = ((), (), s32[]{:S(2)}) async-start(), calls=%async_computation.2 | async-start | bytes 12976128 | tf_op jit(solution)/shard_map/all_gather | solution.py:1751
  10.5 103.4 %copy-start.3 = (s32[1,384]{1,0:T(1,128)S(1)}, s32[1,384]{1,0:T(1,128)}, u32[]{:S(2)}) copy-start(s32[1,384]{1,0:T(1,128)} %seg_row.3) | copy-start | bytes 4612
  113.8 402.1 %reduce-scatter.5.cloned.1.call-start = ((), (), s32[]{:S(2)}) async-start(), calls=%async_computation.4 | async-start | bytes 6488064 | tf_op jit(solution)/shard_map/reduce_scatter | solution.py:1788
  293.4 222.5 %reduce-scatter.3.cloned.1.call-start = ((), (), s32[]{:S(2)}) async-start(), calls=%async_computation.3 | async-start | bytes 12976128 | tf_op jit(solution)/shard_map/reduce_scatter | solution.py:1789
  550.5 18.2 %copy-start.1 = (bf16[384,2048]{1,0:T(8,128)(2,1)S(1)}, bf16[384,2048]{1,0:T(8,128)(2,1)}, u32[]{:S(2)}) copy-start(bf16[384,2048]{1,0:T(8,128)(2,1)} %get-tuple-element.123) | copy-start | bytes 4718596
  568.7 2.0 copy-start.2
Sparse Core Ops, SparseCore 0:
  113.9 108.4 all-gather.1
  293.5 63.0 reduce-scatter.4
  358.9 145.3 reduce-scatter.2

commit v8 on v7

--- a/solution.py
+++ b/solution.py
@@ -1073,8 +1073,8 @@
     return jnp.sum(value, axis=0, keepdims=True)
 
 
-def branch_kernel(grads, grad_normed, middle, gains, context, weights, layer, onward, layer_out, grad_branch,
-                  grad_context, grad_o, gain_rows, weight, stage, arrived_layer, load_sem, out_sem, send, recv):
+def branch_kernel(grads, grad_normed, middle, gains, context_hbm, weights, layer_hbm, onward, layer_out, grad_branch,
+                  grad_context, grad_o, gain_rows, weight, stage, arrived_layer, context, layer, load_sem, out_sem, send, recv):
     length, width = middle.shape[0], D + 2 * KW
     half = length // 2
     z, c, f = place()
@@ -1090,6 +1090,10 @@
         copy.start()
     load_o = pltpu.make_async_copy(weights.at[:, pl.ds(width, D)], weight, load_sem.at[0])
     load_o.start()
+    load_context = pltpu.make_async_copy(context_hbm, context, load_sem.at[1])
+    load_layer = pltpu.make_async_copy(layer_hbm, layer, load_sem.at[2])
+    load_context.start()
+    load_layer.start()
     gain_rows[...] = jnp.zeros_like(gain_rows)
 
     def middle_grads(r):
@@ -1126,7 +1130,9 @@
         out(i, slot).start()
         return carry
 
+    load_context.wait()
     lax.fori_loop(0, steps, step, 0)
+    load_layer.wait()
     for way in range(2):
         last[way].wait()
 
@@ -1147,11 +1153,11 @@
     return pl.pallas_call(
         branch_kernel,
         out_shape=(rows, rows, rows, jax.ShapeDtypeStruct((D, D), bf16), jax.ShapeDtypeStruct((8, D), f32)),
-        in_specs=[vmem] * 5 + [hbm, vmem, vmem],
+        in_specs=[vmem] * 4 + [hbm] * 4,
         out_specs=(vmem, vmem, vmem, hbm, vmem),
         scratch_shapes=[
             pltpu.VMEM((D, D), bf16), pltpu.VMEM((2, 512, D), bf16), pltpu.VMEM((2, length // 2, D), bf16),
-            dma((1,)), dma((2,)), dma((2,)), dma((2,)),
+            pltpu.VMEM((length, D), bf16), pltpu.VMEM((length, D), bf16), dma((3,)), dma((2,)), dma((2,)), dma((2,)),
         ],
         compiler_params=pltpu.CompilerParams(
             collective_id=4, has_side_effects=True, vmem_limit_bytes=feed_vmem_limit
@@ -1161,9 +1167,9 @@
     )(grads, grad_normed, middle, gains, context, weights, layer, onward)
 
 
-def backward_kernel(lines, x, normed_one, qkv, grad_context, log_totals, gains, cosine, sine, seg_col, seg_row, gain_two,
+def backward_kernel(lines, x_hbm, normed_hbm, qkv, grad_context, log_totals, gains, cosine, sine, seg_col, seg_row, gain_two,
                     grad_o, branch_hbm, weights, input_grad, out_o, out_q, weight, grad_proj, grad_one, gain_rows,
-                    gain_columns, staged, *refs):
+                    gain_columns, staged, x, normed_one, *refs):
     groups = [refs[i * 2 : i * 2 + 2] for i in range(6)] + [(out_o, out_q)]
     scatter_sems, (load_sem, weight_sem) = refs[12:20], refs[20:]
     scatter = Scatter(lines, groups, scatter_sems)
@@ -1184,6 +1190,10 @@
         load(d).start()
     load_branch = pltpu.make_async_copy(branch_hbm, input_grad, load_sem.at[lines])
     load_branch.start()
+    load_x = pltpu.make_async_copy(x_hbm, x, load_sem.at[lines + 1])
+    load_normed = pltpu.make_async_copy(normed_hbm, normed_one, load_sem.at[lines + 2])
+    load_x.start()
+    load_normed.start()
     load_weight(0).start()
     load_weight(1).start()
     gain_rows[...] = gain_two[...]
@@ -1215,6 +1225,8 @@
     for d in order[2:]:
         scatter.over_second(0, d)
     load_branch.wait()
+    load_x.wait()
+    load_normed.wait()
 
     def input_grads(r):
         values, arrived = x[r].astype(f32), grad_one[r]
@@ -1284,13 +1296,14 @@
             jax.ShapeDtypeStruct((rows, D), f32),
             jax.ShapeDtypeStruct((rows, width + 128), f32),
         ),
-        in_specs=[vmem] * 11 + [hbm] * 3,
+        in_specs=[hbm] * 2 + [vmem] * 9 + [hbm] * 3,
         out_specs=(vmem,) * 3,
         scratch_shapes=[
             pltpu.VMEM((2, 512, width), bf16), pltpu.VMEM((length, width), bf16), pltpu.VMEM((length, D), f32),
             pltpu.VMEM((8, D), f32), pltpu.VMEM((D, 128), bf16), pltpu.VMEM((2, n_tp, rows, width + 128), bf16),
+            pltpu.VMEM((length, D), bf16), pltpu.VMEM((length, D), bf16),
         ]
-        + buffers + sems + [dma((lines + 1,)), dma((2,))],
+        + buffers + sems + [dma((lines + 3,)), dma((2,))],
         compiler_params=pltpu.CompilerParams(
             collective_id=7, has_side_effects=True, vmem_limit_bytes=feed_vmem_limit
         ),
@@ -1428,7 +1441,7 @@
             return pl.BlockSpec((rows, columns // steps), lambda i: (0, i))
         return None
 
-    steps = 8 if all(block(shape, 8) for shape in shapes) else 4
+    steps = 4
     specs = [block(shape, steps) for shape in shapes]
     flat = [array for state in states for array in state]
     gains = pl.BlockSpec(states[4][0].shape, lambda i: (0, 0))

time: 584 us -> 583 us (level)
  no operation moved by 1% of the time
where the time goes in v8:
time: 583 us; the launch traced here: 579 us
  Pallas kernels  542 us (93%)
  between operations  16.6 us (3%)
  local copies, waits for them, and re-layouts  7.28 us (1%)
  other arithmetic  6.65 us (1%)
  waiting for transfers between devices  6.01 us (1%)
    pallas_call x1, Pallas kernels, backward(): pl.pallas_call(functools.partial(backward_kernel, lines), out_shape=(jax....  131 us
    pallas_call x1, Pallas kernels, gather_all(): pl.pallas_call(functools.partial(gather_kernel, lines), out_shape=(jax.Sh...  103 us
    pallas_call x1, Pallas kernels, forward(): pl.pallas_call(forward_kernel, out_shape=(jax.ShapeDtypeStruct((length, w...  95.5 us
    pallas_call x1, Pallas kernels, feed(): pl.pallas_call(feed_front_kernel, out_shape=(jax.ShapeDtypeStruct((tokens...  71.1 us
    pallas_call x1, Pallas kernels, feed(): pl.pallas_call(feed_back_kernel, out_shape=(jax.ShapeDtypeStruct((length,...  63.6 us
    pallas_call x1, Pallas kernels, norm_parts(): pl.pallas_call(functools.partial(norm_kernel, n_dp, n_tp), out_shape=(jax...  34.2 us
    pallas_call x1, Pallas kernels, branch(): pl.pallas_call(branch_kernel, out_shape=(rows, rows, rows, jax.ShapeDtype...  25.9 us
    pallas_call x1, Pallas kernels, adam_all(): pl.pallas_call(adam_kernel, grid=(steps,), out_shape=[jax.ShapeDtypeStruc...  17.2 us
  transfers between devices with their start and end apart: 3, of which 1 were waited for; matrix products, arithmetic and copies ran while one was open for 1% of the time, Pallas kernels for 55%

profile of v8, /device:TPU:0, one launch (start us, length us, event | category | flops | bytes accessed | tf_op | source)
XLA Modules:
  0.0 578.6 jit_solution(9131763895601846023)
XLA Ops:
  7.2 0.0 copy-start
  7.2 0.0 all-gather.2.cloned.1.call-start
  7.2 0.8 convert.15
  8.0 0.1 copy.46
  8.1 1.1 convert.14
  9.2 1.1 convert.13
  10.3 0.0 copy-done
  10.4 0.1 convert_element_type.14.down
  10.5 0.0 copy-start.3
  10.5 103.3 %gather_all.1 = (bf16[4,2,4,64,4736]{4,3,2,1,0:T(8,128)(2,1)}, bf16[4,64,2816]{2,1,0:T(8,128)(2,1)}, bf16[4,2,176,2048]{3,2,1,0:T(8,128)(2,1)}) custom-call(bf16[64,4736]{1,0:T(8,128)(2,1)S(1)} %fusion.1.own, f32[64,11264]{1,0:T(8,128)} %refs_10_.1, bf16[176,2048]{1,0:T(8,128)(2,1)S(1)} %convert_element_type.14.down), custom_call_target="tpu_custom_call" | custom-call | bytes 369000000 | tf_op jit(solution)/shard_map/gather_all/pallas_call | solution.py:366
  113.8 0.0 all-gather.2.cloned.1.call-update
  113.8 0.0 reduce-scatter.5.cloned.1.call-start
  113.9 0.0 copy-done.3
  113.9 0.5 slice.24
  115.1 0.1 add_select_fusion
  115.2 0.3 reduce-window.9
  115.5 0.1 slice.27
  115.6 0.8 copy.49.seg_col
  116.4 1.1 convert_bitcast_fusion
  117.5 1.3 copy.48.gains
  118.8 0.1 slice_reduce_fusion
  119.0 0.1 fusion.4
  119.0 0.8 fusion.2
  119.8 1.1 pad_maximum_fusion
  120.9 95.5 %forward.1 = (bf16[384,2560]{1,0:T(8,128)(2,1)}, bf16[384,2048]{1,0:T(8,128)(2,1)}, f32[32,384]{1,0:T(8,128)}, f32[384,2048]{1,0:T(8,128)}, bf16[384,2048]{1,0:T...) custom-call(bf16[384,2048]{1,0:T(8,128)(2,1)} %x_hbm.1, bf16[384,2048]{1,0:T(8,128)(2,1)} %grads.3, ...), custom_call_target="tpu_custom_call" | custom-call | bytes 350550016 | tf_op jit(solution)/shard_map/forward/pallas_call | solution.py:937
  216.5 5.9 %all-gather.2.cloned.1.call-done.wm_hbm = bf16[2048,2816]{1,0:T(8,128)(2,1)} async-done(((bf16[256,2816]{1,0:T(8,128)(2,1)}), bf16[2048,2816]{1,0:T(8,128)(2,1)}) %all-gather.2.cloned.1.call-update) | async-done | bytes 11534352 | tf_op jit(solution)/shard_map/all_gather | solution.py:1764
  222.4 71.1 %feed_front.1 = (bf16[1536,2816]{1,0:T(8,128)(2,1)}, bf16[1408,2048]{1,0:T(8,128)(2,1)}, bf16[384,2048]{1,0:T(8,128)(2,1)}, bf16[2,192,2048]{2,1,0:T(8,128)(2,1)}) custom-call(bf16[1536,2048]{1,0:T(8,128)(2,1)} %bitcast.31, bf16[1152,2048]{1,0:T(8,128)(2,1)} %bitcast.35, bf16[2048,2816]{1,0:T(8,128)(2,1)} %all-gather.2.cloned.1.call-done.wm_hbm, ...), custom_call_target="tpu_custom_call" | custom-call | bytes 239850000 | tf_op jit(solution)/shard_map/feed_front/pallas_call | solution.py:1689
  293.5 0.0 reduce-scatter.5.cloned.1.call-update
  293.5 0.2 reduce-scatter.3.cloned.1.call-start
  293.7 63.6 %feed_back.1 = (f32[384,2048]{1,0:T(8,128)}, bf16[2048,2816]{1,0:T(8,128)(2,1)}) custom-call(bf16[1536,2816]{1,0:T(8,128)(2,1)} %get-tuple-element.64.gh_hbm, bf16[2048,2816]{1,0:T(8,128)(2,1)} %all-gather.2.cloned.1.call-done.wm_hbm, bf16[1536,2048]{1,0:T(8,128)(2,1)} %bitcast.32), custom_call_target="tpu_custom_call" | custom-call | bytes 221400000 | tf_op jit(solution)/shard_map/feed_back/pallas_call | solution.py:1710
  357.4 0.0 reduce-scatter.3.cloned.1.call-update
  357.4 25.9 %branch.1 = (bf16[384,2048]{1,0:T(8,128)(2,1)}, bf16[384,2048]{1,0:T(8,128)(2,1)}, bf16[384,2048]{1,0:T(8,128)(2,1)}, bf16[2048,2048]{1,0:T(8,128)(2,1)}, f32[8,2048]{1,0:T(8,128)}) custom-call(bf16[384,2048]{1,0:T(8,128)(2,1)} %grads.3, f32[384,2048]{1,0:T(8,128)} %get-tuple-element.65.grad_normed, f32[384,2048]{1,0:T(8,128)} %get-tuple-element.66.middle, ...), custom_call_target="tpu_custom_call" | custom-call | bytes 81180000 | tf_op jit(solution)/shard_map/branch/pallas_call | solution.py:1153
  383.3 130.9 %backward.1 = (bf16[384,2048]{1,0:T(8,128)(2,1)}, f32[64,2048]{1,0:T(8,128)}, f32[64,2688]{1,0:T(8,128)}) custom-call(bf16[384,2048]{1,0:T(8,128)(2,1)} %x_hbm.1, bf16[384,2048]{1,0:T(8,128)(2,1)} %get-tuple-element.71.normed_hbm, bf16[384,2560]{1,0:T(8,128)(2,1)} %get-tuple-element.72.qkv, bf16[384,2048]{1,0:T(8,128)(2,1)} %get-tuple-element.73.grad_context, ...), custom_call_target="tpu_custom_call" | custom-call | bytes 387449984 | tf_op jit(solution)/shard_map/backward/pallas_call | solution.py:1292
  514.3 0.0 reduce-scatter.5.cloned.1.call-done.down.refs_3_
  514.3 0.0 reduce-scatter.3.cloned.1.call-done
  514.3 34.2 %norm_parts.1 = (f32[64,11264]{1,0:T(8,128)}, f32[8,128]{1,0:T(8,128)}) custom-call(bf16[4,64,2816]{2,1,0:T(8,128)(2,1)} %bitcast.36, f32[64,2688]{1,0:T(8,128)} %get-tuple-element.80.qkv.gain_block.refs_0_, f32[64,2048]{1,0:T(8,128)} %get-tuple-element.81.out.refs_1_, bf16[176,2048]{1,0:T(8,128)(2,1)} %reduce-scatter.5.cloned.1.call-done.down.refs_3_), custom_call_target="tpu_custom_call" | custom-call | bytes 129150000 | tf_op jit(solution)/shard_map/norm_parts/pallas_call | solution.py:1394
  548.6 1.2 slice.29
  550.5 0.0 copy-start.1
  550.5 17.2 %adam.1 = (f32[64,2560]{1,0:T(8,128)}, f32[64,2560]{1,0:T(8,128)}, f32[64,2560]{1,0:T(8,128)}, f32[64,2048]{1,0:T(8,128)}, f32[64,2048]{1,0:T(8,128)}, /*index=5...) custom-call(f32[8,128]{1,0:T(8,128)} %get-tuple-element.83.total, ...), custom_call_target="tpu_custom_call" | custom-call | bytes 51660000 | tf_op jit(solution)/shard_map/adam/pallas_call | solution.py:1451
  567.7 0.0 copy-done.1
  567.7 0.0 copy-start.2
  567.7 1.1 copy.55
  568.8 0.8 copy-done.2
  569.6 1.1 copy.56
  (5 shorter events, 0.1 us)
Async XLA Ops:
  7.2 3.2 copy-start
  7.2 215.2 %all-gather.2.cloned.1.call-start = ((), (), s32[]{:S(2)}) async-start(), calls=%async_computation.2 | async-start | bytes 12976128 | tf_op jit(solution)/shard_map/all_gather | solution.py:1764
  10.5 103.4 %copy-start.3 = (s32[1,384]{1,0:T(1,128)S(1)}, s32[1,384]{1,0:T(1,128)}, u32[]{:S(2)}) copy-start(s32[1,384]{1,0:T(1,128)} %seg_row.3) | copy-start | bytes 4612
  113.8 400.5 %reduce-scatter.5.cloned.1.call-start = ((), (), s32[]{:S(2)}) async-start(), calls=%async_computation.4 | async-start | bytes 6488064 | tf_op jit(solution)/shard_map/reduce_scatter | solution.py:1801
  293.5 220.8 %reduce-scatter.3.cloned.1.call-start = ((), (), s32[]{:S(2)}) async-start(), calls=%async_computation.3 | async-start | bytes 12976128 | tf_op jit(solution)/shard_map/reduce_scatter | solution.py:1802
  550.5 17.2 %copy-start.1 = (bf16[384,2048]{1,0:T(8,128)(2,1)S(1)}, bf16[384,2048]{1,0:T(8,128)(2,1)}, u32[]{:S(2)}) copy-start(bf16[384,2048]{1,0:T(8,128)(2,1)} %get-tuple-element.123) | copy-start | bytes 4718596
  567.7 2.0 copy-start.2
Sparse Core Ops, SparseCore 0:
  113.9 108.4 all-gather.1
  293.6 63.0 reduce-scatter.4
  359.0 147.1 reduce-scatter.2
